TPU v7x, 32 devices: a whole 2x2x4 slice. The times are simulated.
32 devices in a mesh: dp: 4 (over y, x), fsdp: 8 (over z, core).
Axes of the slice: x: 2, y: 2, z: 4, core: 2. Of those that a mesh axis runs over, the one named last changes fastest.
Arguments:
- tokens: bfloat16 [2, 4096, 768], P(None, ('dp', 'fsdp')), may hold values from -6 to 6
- lengths: int32 [2, 32, 8], P(None, ('dp', 'fsdp')), may hold values from 1 to 96, 128 in all within a row
- ln1_gain: float32 [768], P(('dp', 'fsdp')), may hold values from 0.1 to 1.9
- ln1_shift: float32 [768], P(('dp', 'fsdp')), may hold values from -1.5 to 1.5
- w_qkv: float32 [768, 2304], P(('dp', 'fsdp')), may hold values from -0.21875 to 0.21875
- qv_bias: float32 [1536], P(('dp', 'fsdp')), may hold values from -1.5 to 1.5
- w_out: float32 [768, 768], P(('dp', 'fsdp')), may hold values from -0.875 to 0.875
- out_bias: float32 [768], P(('dp', 'fsdp')), may hold values from -1.5 to 1.5
- ln2_gain: float32 [768], P(('dp', 'fsdp')), may hold values from 0.1 to 1.9
- ln2_shift: float32 [768], P(('dp', 'fsdp')), may hold values from -1.5 to 1.5
- w_fc: float32 [768, 3072], P(('dp', 'fsdp')), may hold values from -0.21875 to 0.21875
- fc_bias: float32 [3072], P(('dp', 'fsdp')), may hold values from -1.5 to 1.5
- w_proj: float32 [3072, 768], P(('dp', 'fsdp')), may hold values from -0.109375 to 0.109375
- proj_bias: float32 [768], P(('dp', 'fsdp')), may hold values from -1.5 to 1.5
- cotangent: bfloat16 [2, 4096, 768], P(None, ('dp', 'fsdp')), may hold values from -6 to 6
Outputs:
- activations: bfloat16 [2, 4096, 768], P(None, ('dp', 'fsdp'))
- token_grad: bfloat16 [2, 4096, 768], P(None, ('dp', 'fsdp'))
- ln1_gain_grad: float32 [768], P(('dp', 'fsdp'))
- ln1_shift_grad: float32 [768], P(('dp', 'fsdp'))
- w_qkv_grad: float32 [768, 2304], P(('dp', 'fsdp'))
- qv_bias_grad: float32 [1536], P(('dp', 'fsdp'))
- w_out_grad: float32 [768, 768], P(('dp', 'fsdp'))
- out_bias_grad: float32 [768], P(('dp', 'fsdp'))
- ln2_gain_grad: float32 [768], P(('dp', 'fsdp'))
- ln2_shift_grad: float32 [768], P(('dp', 'fsdp'))
- w_fc_grad: float32 [768, 3072], P(('dp', 'fsdp'))
- fc_bias_grad: float32 [3072], P(('dp', 'fsdp'))
- w_proj_grad: float32 [3072, 768], P(('dp', 'fsdp'))
- proj_bias_grad: float32 [768], P(('dp', 'fsdp'))
Inputs may be any that keep to these rules, and one draw needn't show every extreme that they name: Each row lengths[m, b, :] sums to 128, and its largest entry is exactly 96.
All inputs are finite; a program needn't handle non-finite values.
Results may differ from a plain program's by a relative error of at most 0.018.
Values may be sent and summed in bfloat16 or wider, within the bound.
No kernel may reach another device: no remote copies, remote signals or barrier semaphores. Data moves between devices by JAX's collectives and lax.ppermute only.
A program may use at most 192 MiB of HBM per device.

v0:
```python
import jax
import jax.numpy as jnp
from jax import lax
from jax.sharding import PartitionSpec as P

HEADS = 12
HD = 64


epsilon = 1e-05
neg_large = -1e30


def norm_rows(hidden, gain_row, shift_row):
    centred = hidden - jnp.mean(hidden, axis=-1, keepdims=True)
    spread = jnp.mean(centred * centred, axis=-1, keepdims=True)
    return centred * lax.rsqrt(spread + epsilon) * gain_row + shift_row


def gelu_tanh(values):
    return jax.nn.gelu(values, approximate=True)


def allowed_pairs(bin_lengths, row_count):
    segment_ends = jnp.cumsum(bin_lengths, axis=-1)
    places = jnp.arange(row_count, dtype=jnp.int32)
    segment = jnp.sum(
        (places[None, :, None] >= segment_ends[:, None, :]).astype(jnp.int32), axis=-1
    )
    same_segment = segment[:, :, None] == segment[:, None, :]
    return jnp.logical_and(same_segment, places[None, None, :] <= places[None, :, None])


def settle(gathered):
    return tuple(
        (member if member.ndim == 2 else member.astype(jnp.float32) for member in gathered)
    )


def split_heads(mixed_rows):
    micro_count, row_count, triple = mixed_rows.shape
    split_rows = mixed_rows.reshape(micro_count, row_count, 3, HEADS, triple // (3 * HEADS))
    return (split_rows[:, :, 0], split_rows[:, :, 1], split_rows[:, :, 2])


def score_block(query_rows, key_rows, allowed):
    scores = jnp.einsum(
        "bqhe,bkhe->bhqk", query_rows, key_rows, preferred_element_type=jnp.float32
    ) * HD ** (-0.5)
    return jnp.where(allowed[:, None], scores, neg_large)


def block_forward(hidden, weights, allowed):
    (
        gain_one,
        shift_one,
        w_mixed,
        mixed_bias,
        w_attn,
        attn_bias,
        gain_two,
        shift_two,
        w_up,
        up_bias,
        w_down,
        down_bias,
    ) = weights
    model_width = hidden.shape[-1]
    normed = norm_rows(hidden, gain_one, shift_one).astype(jnp.bfloat16)
    bias_full = jnp.concatenate(
        [mixed_bias[:model_width], jnp.zeros((model_width,), jnp.float32), mixed_bias[model_width:]]
    )
    mixed_rows = (
        jnp.einsum("btd,de->bte", normed, w_mixed, preferred_element_type=jnp.float32) + bias_full
    ).astype(jnp.bfloat16)
    query_rows, key_rows, value_rows = split_heads(mixed_rows)
    masked = score_block(query_rows, key_rows, allowed)
    row_max = jnp.max(masked, axis=-1, keepdims=True)
    exponent = jnp.exp(masked - row_max)
    denominator = jnp.sum(exponent, axis=-1, keepdims=True)
    probabilities = (exponent / denominator).astype(jnp.bfloat16)
    attended = jnp.einsum(
        "bhqk,bkhe->bqhe", probabilities, value_rows, preferred_element_type=jnp.float32
    )
    attended = attended.reshape(hidden.shape).astype(jnp.bfloat16)
    middle = hidden + (
        jnp.einsum("btd,de->bte", attended, w_attn, preferred_element_type=jnp.float32) + attn_bias
    )
    normed_two = norm_rows(middle, gain_two, shift_two).astype(jnp.bfloat16)
    before = (
        jnp.einsum("btd,df->btf", normed_two, w_up, preferred_element_type=jnp.float32) + up_bias
    )
    active = gelu_tanh(before).astype(jnp.bfloat16)
    output = middle + (
        jnp.einsum("btf,fd->btd", active, w_down, preferred_element_type=jnp.float32) + down_bias
    )
    log_total = row_max + jnp.log(denominator)
    return (output, (hidden, middle, mixed_rows, attended, log_total, before))


def block_backward(grad_output, saved, weights, allowed):
    (
        gain_one,
        shift_one,
        w_mixed,
        mixed_bias,
        w_attn,
        attn_bias,
        gain_two,
        shift_two,
        w_up,
        up_bias,
        w_down,
        down_bias,
    ) = weights
    hidden, middle, mixed_rows, attended, log_total, before = saved
    micro_count, row_count, model_width = hidden.shape
    score_scale = HD ** (-0.5)
    grad_down = grad_output.astype(jnp.bfloat16)
    active, gelu_pull = jax.vjp(gelu_tanh, before)
    grad_w_down = jnp.einsum(
        "btf,btd->fd", active.astype(jnp.bfloat16), grad_down, preferred_element_type=jnp.float32
    )
    grad_down_bias = jnp.sum(grad_down.astype(jnp.float32), axis=(0, 1))
    grad_active = jnp.einsum("btd,fd->btf", grad_down, w_down, preferred_element_type=jnp.float32)
    grad_before = gelu_pull(grad_active)[0].astype(jnp.bfloat16)
    normed_two, norm_two_pull = jax.vjp(norm_rows, middle, gain_two, shift_two)
    grad_w_up = jnp.einsum(
        "btd,btf->df",
        normed_two.astype(jnp.bfloat16),
        grad_before,
        preferred_element_type=jnp.float32,
    )
    grad_up_bias = jnp.sum(grad_before.astype(jnp.float32), axis=(0, 1))
    grad_normed_two = jnp.einsum(
        "btf,df->btd", grad_before, w_up, preferred_element_type=jnp.float32
    )
    grad_middle_norm, grad_gain_two, grad_shift_two = norm_two_pull(grad_normed_two)
    grad_middle = grad_output + grad_middle_norm
    grad_branch = grad_middle.astype(jnp.bfloat16)
    grad_w_attn = jnp.einsum(
        "btd,bte->de", attended, grad_branch, preferred_element_type=jnp.float32
    )
    grad_attn_bias = jnp.sum(grad_branch.astype(jnp.float32), axis=(0, 1))
    grad_attended = jnp.einsum(
        "bte,de->btd", grad_branch, w_attn, preferred_element_type=jnp.float32
    ).astype(jnp.bfloat16)
    grad_heads = grad_attended.reshape(micro_count, row_count, HEADS, model_width // HEADS)
    query_rows, key_rows, value_rows = split_heads(mixed_rows)
    masked = score_block(query_rows, key_rows, allowed)
    probabilities = jnp.exp(masked - log_total)
    grad_probs = jnp.einsum(
        "bqhe,bkhe->bhqk", grad_heads, value_rows, preferred_element_type=jnp.float32
    )
    grad_values = jnp.einsum(
        "bhqk,bqhe->bkhe",
        probabilities.astype(jnp.bfloat16),
        grad_heads,
        preferred_element_type=jnp.float32,
    )
    grad_scores = (
        probabilities * (grad_probs - jnp.sum(probabilities * grad_probs, axis=-1, keepdims=True))
    ).astype(jnp.bfloat16)
    grad_queries = (
        jnp.einsum("bhqk,bkhe->bqhe", grad_scores, key_rows, preferred_element_type=jnp.float32)
        * score_scale
    )
    grad_keys = (
        jnp.einsum("bhqk,bqhe->bkhe", grad_scores, query_rows, preferred_element_type=jnp.float32)
        * score_scale
    )
    grad_mixed = (
        jnp.stack([grad_queries, grad_keys, grad_values], axis=2)
        .reshape(micro_count, row_count, 3 * model_width)
        .astype(jnp.bfloat16)
    )
    column_sums = jnp.sum(grad_mixed.astype(jnp.float32), axis=(0, 1))
    grad_mixed_bias = jnp.concatenate([column_sums[:model_width], column_sums[2 * model_width :]])
    normed, norm_one_pull = jax.vjp(norm_rows, hidden, gain_one, shift_one)
    grad_w_mixed = jnp.einsum(
        "btd,bte->de", normed.astype(jnp.bfloat16), grad_mixed, preferred_element_type=jnp.float32
    )
    grad_normed = jnp.einsum("bte,de->btd", grad_mixed, w_mixed, preferred_element_type=jnp.float32)
    grad_hidden_norm, grad_gain_one, grad_shift_one = norm_one_pull(grad_normed)
    grad_parts = (
        grad_gain_one,
        grad_shift_one,
        grad_w_mixed,
        grad_mixed_bias,
        grad_w_attn,
        grad_attn_bias,
        grad_gain_two,
        grad_shift_two,
        grad_w_up,
        grad_up_bias,
        grad_w_down,
        grad_down_bias,
    )
    return (grad_middle + grad_hidden_norm, grad_parts)


def body(
    tokens,
    lengths,
    ln1_gain,
    ln1_shift,
    w_qkv,
    qv_bias,
    w_out,
    out_bias,
    ln2_gain,
    ln2_shift,
    w_fc,
    fc_bias,
    w_proj,
    proj_bias,
    cotangent,
):
    allowed = allowed_pairs(lengths[:, 0, :], tokens.shape[1])

    def fetch_weights():
        return settle(
            (
                lax.all_gather(ln1_gain.astype(jnp.bfloat16), ("dp", "fsdp"), axis=0, tiled=True),
                lax.all_gather(ln1_shift.astype(jnp.bfloat16), ("dp", "fsdp"), axis=0, tiled=True),
                lax.all_gather(w_qkv.astype(jnp.bfloat16), ("dp", "fsdp"), axis=0, tiled=True),
                lax.all_gather(qv_bias.astype(jnp.bfloat16), ("dp", "fsdp"), axis=0, tiled=True),
                lax.all_gather(w_out.astype(jnp.bfloat16), ("dp", "fsdp"), axis=0, tiled=True),
                lax.all_gather(out_bias.astype(jnp.bfloat16), ("dp", "fsdp"), axis=0, tiled=True),
                lax.all_gather(ln2_gain.astype(jnp.bfloat16), ("dp", "fsdp"), axis=0, tiled=True),
                lax.all_gather(ln2_shift.astype(jnp.bfloat16), ("dp", "fsdp"), axis=0, tiled=True),
                lax.all_gather(w_fc.astype(jnp.bfloat16), ("dp", "fsdp"), axis=0, tiled=True),
                lax.all_gather(fc_bias.astype(jnp.bfloat16), ("dp", "fsdp"), axis=0, tiled=True),
                lax.all_gather(w_proj.astype(jnp.bfloat16), ("dp", "fsdp"), axis=0, tiled=True),
                lax.all_gather(proj_bias.astype(jnp.bfloat16), ("dp", "fsdp"), axis=0, tiled=True),
            )
        )

    hidden = tokens.astype(jnp.float32)
    kept_layers = []
    for repeat in range(2):
        hidden, saved = block_forward(hidden, fetch_weights(), allowed)
        kept_layers.append(saved)
    grad_hidden = cotangent.astype(jnp.float32)
    totals = None
    for repeat in range(2):
        grad_hidden, grad_parts = block_backward(
            grad_hidden, kept_layers[1 - repeat], fetch_weights(), allowed
        )
        if repeat == 0:
            totals = grad_parts
        else:
            totals = jax.tree.map(jnp.add, totals, grad_parts)
    shares = (
        lax.psum_scatter(totals[0], ("dp", "fsdp"), scatter_dimension=0, tiled=True),
        lax.psum_scatter(totals[1], ("dp", "fsdp"), scatter_dimension=0, tiled=True),
        lax.psum_scatter(totals[2], ("dp", "fsdp"), scatter_dimension=0, tiled=True),
        lax.psum_scatter(totals[3], ("dp", "fsdp"), scatter_dimension=0, tiled=True),
        lax.psum_scatter(totals[4], ("dp", "fsdp"), scatter_dimension=0, tiled=True),
        lax.psum_scatter(totals[5], ("dp", "fsdp"), scatter_dimension=0, tiled=True),
        lax.psum_scatter(totals[6], ("dp", "fsdp"), scatter_dimension=0, tiled=True),
        lax.psum_scatter(totals[7], ("dp", "fsdp"), scatter_dimension=0, tiled=True),
        lax.psum_scatter(totals[8], ("dp", "fsdp"), scatter_dimension=0, tiled=True),
        lax.psum_scatter(totals[9], ("dp", "fsdp"), scatter_dimension=0, tiled=True),
        lax.psum_scatter(totals[10], ("dp", "fsdp"), scatter_dimension=0, tiled=True),
        lax.psum_scatter(totals[11], ("dp", "fsdp"), scatter_dimension=0, tiled=True),
    )
    return (hidden.astype(jnp.bfloat16), grad_hidden.astype(jnp.bfloat16)) + tuple(shares)


def solution(mesh):
    return jax.shard_map(
        body,
        mesh=mesh,
        in_specs=(
            P(None, ("dp", "fsdp"), None),
            P(None, ("dp", "fsdp"), None),
            P(("dp", "fsdp")),
            P(("dp", "fsdp")),
            P(("dp", "fsdp"), None),
            P(("dp", "fsdp")),
            P(("dp", "fsdp"), None),
            P(("dp", "fsdp")),
            P(("dp", "fsdp")),
            P(("dp", "fsdp")),
            P(("dp", "fsdp"), None),
            P(("dp", "fsdp")),
            P(("dp", "fsdp"), None),
            P(("dp", "fsdp")),
            P(None, ("dp", "fsdp"), None),
        ),
        out_specs=(
            P(None, ("dp", "fsdp"), None),
            P(None, ("dp", "fsdp"), None),
            P(("dp", "fsdp")),
            P(("dp", "fsdp")),
            P(("dp", "fsdp"), None),
            P(("dp", "fsdp")),
            P(("dp", "fsdp"), None),
            P(("dp", "fsdp")),
            P(("dp", "fsdp")),
            P(("dp", "fsdp")),
            P(("dp", "fsdp"), None),
            P(("dp", "fsdp")),
            P(("dp", "fsdp"), None),
            P(("dp", "fsdp")),
        ),
        check_vma=False,
    )
```

profile of v0, /device:TPU:17, one launch (start us, length us, event | category | flops | bytes accessed | tf_op | source)
XLA Modules:
  0.0 827.0 jit_solution(15931054665243755612)
XLA Ops:
  20.8 41.2 %all-reduce.17 = (bf16[1536]{0:T(1024)(128)(2,1)S(1)}, bf16[768]{0:T(1024)(128)(2,1)S(1)}, bf16[768]{0:T(1024)(128)(2,1)S(1)}, bf16[768]{0:T(1024)(128)(2,1)S(1)...) all-reduce(bf16[1536]{0:T(1024)(128)(2,1)S(1)} %dynamic-update-slic, ...), channel_id=1, replica_groups=mesh['dp'=4,'fsdp'=8] {'dp','fsdp'}, use_global_device_ids=true, to_apply=%add.2 | all-reduce | flops 9216 | bytes 36864
  67.4 5.1 all-gather.5.cloned.1.call-done
  72.5 3.3 fusion.22
  78.9 50.1 %all-gather.7.cloned.1.call-done = bf16[768,768]{1,0:T(8,128)(2,1)} async-done(((bf16[24,768]{1,0:T(8,128)(2,1)}), bf16[768,768]{1,0:T(8,128)(2,1)}) %all-gather.7.cloned.1.call-update) | async-done | bytes 1179664 | tf_op jit(solution)/shard_map/all_gather | solution.py:228
  132.6 63.8 %all-gather.9.cloned.1.call-done = bf16[768,3072]{1,0:T(8,128)(2,1)} async-done(((bf16[24,3072]{1,0:T(8,128)(2,1)}), bf16[768,3072]{1,0:T(8,128)(2,1)}) %all-gather.9.cloned.1.call-update) | async-done | bytes 4718608 | tf_op jit(solution)/shard_map/all_gather | solution.py:232
  196.4 4.0 fusion.16
  200.4 61.9 %all-gather.11.cloned.1.call-done = bf16[3072,768]{1,0:T(8,128)(2,1)} async-done(((bf16[96,768]{1,0:T(8,128)(2,1)}), bf16[3072,768]{1,0:T(8,128)(2,1)}) %all-gather.11.cloned.1.call-update) | async-done | bytes 4718608 | tf_op jit(solution)/shard_map/all_gather | solution.py:234
  262.4 4.7 fusion.120
  270.8 2.4 copy.125
  275.6 2.7 convolution_convert_fusion.2
  281.8 3.9 convert_reduce_fusion.1
  306.3 3.7 convert_reduce_fusion
  317.5 2.6 convolution_convert_fusion
  322.1 2.4 multiply_reduce_fusion
  329.1 4.3 bitcast_add_fusion.2
  333.7 4.3 fusion.108
  338.0 6.0 bitcast_add_fusion
  348.0 5.2 bitcast_add_fusion.1
  359.7 3.7 fusion.109
  365.7 39.7 %all-reduce.16 = (f32[768]{0:T(1024)}, f32[768]{0:T(1024)}, f32[1536]{0:T(1024)}, f32[768]{0:T(1024)}, f32[768]{0:T(1024)}, /*index=5*/f32[768]{0:T(1024)}, f32[3072]{0:T(1024)}, f32[768]{0:T(1024)}) all-reduce(f32[768]{0:T(1024)} %add.298, f32[768]{0:T(1024)} %add.299, ...), channel_id=2, replica_groups=mesh['dp'=4,'fsdp'=8] {'dp','fsdp'}, use_global_device_ids=true, to_apply=%region_26.27.clone | all-reduce | flops 9216 | bytes 73728
  418.1 5.1 fusion.68
  423.2 113.6 %reduce-scatter.5.cloned.1.call-done = f32[24,2304]{1,0:T(8,128)} async-done(((f32[768,2304]{1,0:T(8,128)}), f32[24,2304]{1,0:T(8,128)}) %reduce-scatter.5.cloned.1.call-update) | async-done | bytes 221200 | tf_op jit(solution)/shard_map/reduce_scatter | solution.py:257
  536.7 141.1 %reduce-scatter.11.cloned.1.call-done = f32[96,768]{1,0:T(8,128)} async-done(((f32[3072,768]{1,0:T(8,128)}), f32[96,768]{1,0:T(8,128)}) %reduce-scatter.11.cloned.1.call-update) | async-done | bytes 294928 | tf_op jit(solution)/shard_map/reduce_scatter | solution.py:265
  677.8 142.1 %reduce-scatter.9.cloned.1.call-done = f32[24,3072]{1,0:T(8,128)} async-done(((f32[768,3072]{1,0:T(8,128)}), f32[24,3072]{1,0:T(8,128)}) %reduce-scatter.9.cloned.1.call-update) | async-done | bytes 294928 | tf_op jit(solution)/shard_map/reduce_scatter | solution.py:263
  (375 shorter events, 94.3 us)
Async XLA Ops:
  7.2 65.4 %all-gather.5.cloned.1.call-start = ((), (), s32[]{:S(2)}) async-start(), calls=%async_computation.4 | async-start | bytes 3649536 | tf_op jit(solution)/shard_map/all_gather | solution.py:226
  8.8 120.2 %all-gather.7.cloned.1.call-start = ((), (), s32[]{:S(2)}) async-start(), calls=%async_computation.5 | async-start | bytes 1216512 | tf_op jit(solution)/shard_map/all_gather | solution.py:228
  10.4 186.0 %all-gather.9.cloned.1.call-start = ((), (), s32[]{:S(2)}) async-start(), calls=%async_computation.6 | async-start | bytes 4866048 | tf_op jit(solution)/shard_map/all_gather | solution.py:232
  12.1 250.2 %all-gather.11.cloned.1.call-start = ((), (), s32[]{:S(2)}) async-start(), calls=%async_computation.7 | async-start | bytes 4866048 | tf_op jit(solution)/shard_map/all_gather | solution.py:234
  13.9 409.3 %reduce-scatter.7.cloned.1.call-start = ((), (), s32[]{:S(2)}) async-start(), calls=%async_computation.9 | async-start | bytes 2433024 | tf_op jit(solution)/shard_map/reduce_scatter | solution.py:259
  62.1 67.0 %copy-start.59 = (f32[768]{0:T(1024)}, f32[768]{0:T(1024)S(1)}, u32[]{:S(2)}) copy-start(f32[768]{0:T(1024)S(1)} %convert_element_type.262) | copy-start | bytes 9220
  64.2 11.7 %copy-start.83 = (f32[2304]{0:T(1024)}, f32[2304]{0:T(1024)S(1)}, u32[]{:S(2)}) copy-start(f32[2304]{0:T(1024)S(1)} %pad_maximum_fusion) | copy-start | bytes 27652
  65.4 10.4 %copy-start.68 = (f32[2,128]{1,0:T(2,128)}, f32[2,128]{1,0:T(2,128)S(1)}, u32[]{:S(2)}) copy-start(f32[2,128]{1,0:T(2,128)S(1)} %broadcast_multiply_fusion.3) | copy-start | bytes 3076
  67.3 8.6 %copy-start.80 = (f32[2,128]{1,0:T(2,128)}, f32[2,128]{1,0:T(2,128)S(1)}, u32[]{:S(2)}) copy-start(f32[2,128]{1,0:T(2,128)S(1)} %fusion.102) | copy-start | bytes 3076
  67.4 9.2 %copy-start.64 = (pred[2,128,128]{1,2,0:T(8,128)(4,1)}, pred[2,128,128]{1,2,0:T(8,128)(4,1)S(1)}, u32[]{:S(2)}) copy-start(pred[2,128,128]{1,2,0:T(8,128)(4,1)S(1)} %compare_and_fusion) | copy-start | bytes 98308
  78.3 50.7 %copy-start.16 = (bf16[2,128,768]{2,1,0:T(8,128)(2,1)S(1)}, bf16[2,128,768]{2,1,0:T(8,128)(2,1)}, u32[]{:S(2)}) copy-start(bf16[2,128,768]{2,1,0:T(8,128)(2,1)} %param.15) | copy-start | bytes 1179652
  78.9 53.7 %copy-start.40 = (bf16[2,12,64,128]{3,2,1,0:T(8,128)(2,1)}, bf16[2,12,64,128]{3,2,1,0:T(8,128)(2,1)S(1)}, u32[]{:S(2)}) copy-start(bf16[2,12,64,128]{3,2,1,0:T(8,128)(2,1)S(1)} %convolution_convert_fusion.3) | copy-start | bytes 1179652
  279.1 8.9 %copy-start.11 = (f32[2,128,768]{2,1,0:T(8,128)}, f32[2,128,768]{2,1,0:T(8,128)S(1)}, u32[]{:S(2)}) copy-start(f32[2,128,768]{2,1,0:T(8,128)S(1)} %get-tuple-element.74) | copy-start | bytes 2359300
  279.1 8.9 %copy-start.49 = (f32[2,128]{1,0:T(2,128)}, f32[2,128]{1,0:T(2,128)S(1)}, u32[]{:S(2)}) copy-start(f32[2,128]{1,0:T(2,128)S(1)} %broadcast_multiply_fusion) | copy-start | bytes 3076
  279.4 8.6 %copy-start.56 = (f32[2,128]{1,0:T(2,128)}, f32[2,128]{1,0:T(2,128)S(1)}, u32[]{:S(2)}) copy-start(f32[2,128]{1,0:T(2,128)S(1)} %fusion.105) | copy-start | bytes 3076
  306.3 6.4 copy-start.17
  316.1 220.6 %reduce-scatter.5.cloned.1.call-start = ((), (), s32[]{:S(2)}) async-start(), calls=%async_computation.8 | async-start | bytes 7299072 | tf_op jit(solution)/shard_map/reduce_scatter | solution.py:257
  333.4 344.4 %reduce-scatter.11.cloned.1.call-start = ((), (), s32[]{:S(2)}) async-start(), calls=%async_computation.11 | async-start | bytes 9732096 | tf_op jit(solution)/shard_map/reduce_scatter | solution.py:265
  344.0 475.9 %reduce-scatter.9.cloned.1.call-start = ((), (), s32[]{:S(2)}) async-start(), calls=%async_computation.10 | async-start | bytes 9732096 | tf_op jit(solution)/shard_map/reduce_scatter | solution.py:263
  353.3 6.3 copy-start.70
  359.7 56.6 %copy-start.19 = (f32[2,128,768]{2,1,0:T(8,128)S(1)}, f32[2,128,768]{2,1,0:T(8,128)}, u32[]{:S(2)}) copy-start(f32[2,128,768]{2,1,0:T(8,128)} %copy-done.17) | copy-start | bytes 2359300
  359.7 56.6 %copy-start.21 = (f32[2,128,768]{2,1,0:T(8,128)S(1)}, f32[2,128,768]{2,1,0:T(8,128)}, u32[]{:S(2)}) copy-start(f32[2,128,768]{2,1,0:T(8,128)} %copy-done.20) | copy-start | bytes 2359300
  405.4 12.7 %copy-start.15 = (f32[2,128,3072]{2,1,0:T(8,128)S(1)}, f32[2,128,3072]{2,1,0:T(8,128)}, u32[]{:S(2)}) copy-start(f32[2,128,3072]{2,1,0:T(8,128)} %copy-done.14) | copy-start | bytes 9437188
  405.4 12.7 %copy-start.102 = (f32[768]{0:T(1024)S(1)}, f32[768]{0:T(1024)}, u32[]{:S(2)}) copy-start(f32[768]{0:T(1024)} %convert_element_type.274) | copy-start | bytes 9220
  (97 other events, 264.7 us)
Sparse Core Ops, SparseCore 0:
  11.6 60.8 all-gather.4
  76.1 52.8 all-gather.6
  132.6 63.7 all-gather.8
  199.8 62.4 all-gather.10
  316.3 95.1 reduce-scatter.6
  418.5 118.1 reduce-scatter.4
  543.2 134.6 reduce-scatter.10
  685.3 134.5 reduce-scatter.8
where the time goes:
time: 835 us; the launch traced here: 827 us
  waiting for transfers between devices  578 us (69%)
  matrix products  84.4 us (10%)
  blocking collectives  80.9 us (10%)
  other arithmetic  34.9 us (4%)
  local copies, waits for them, and re-layouts  32.7 us (4%)
  between operations  15.7 us (2%)
    reduce_scatter x1, waiting for transfers between devices, body(): lax.psum_scatter(totals[8], ('dp', 'fsdp'), scatter_dimension=0, tiled=True)  142 us
    reduce_scatter x1, waiting for transfers between devices, body(): lax.psum_scatter(totals[10], ('dp', 'fsdp'), scatter_dimension=0, tiled=T...  141 us
    reduce_scatter x1, waiting for transfers between devices, body(): lax.psum_scatter(totals[2], ('dp', 'fsdp'), scatter_dimension=0, tiled=True)  114 us
    unnamed x2, blocking collectives  80.9 us
    all_gather x1, waiting for transfers between devices, fetch_weights(): lax.all_gather(w_fc.astype(jnp.bfloat16), ('dp', 'fsdp'), axis=0, tiled=T...  63.8 us
    all_gather x1, waiting for transfers between devices, fetch_weights(): lax.all_gather(w_proj.astype(jnp.bfloat16), ('dp', 'fsdp'), axis=0, tiled...  61.9 us
    all_gather x1, waiting for transfers between devices, fetch_weights(): lax.all_gather(w_out.astype(jnp.bfloat16), ('dp', 'fsdp'), axis=0, tiled=...  50.1 us
    unnamed x250, local copies, waits for them, and re-layouts  23 us
  transfers between devices with their start and end apart: 8, of which 7 were waited for; matrix products, arithmetic and copies ran while one was open for 11% of the time, Pallas kernels for 0%

commit v1 on v0

v1 whole, which is shorter than its diff:
```python
import functools

import jax
import jax.numpy as jnp
from jax import lax
from jax.experimental import pallas as pl
from jax.experimental.pallas import tpu as pltpu
from jax.sharding import PartitionSpec as P

HEADS = 12
HD = 64
EPS = 1e-05
NEG = -1e30
AXES = ("dp", "fsdp")
F32 = jnp.float32
BF16 = jnp.bfloat16
GELU_A = 0.7978845608028654
GELU_B = 0.044715

NT = (((1,), (1,)), ((), ()))
TN = (((0,), (0,)), ((), ()))
NN = (((1,), (0,)), ((), ()))

CYCLE = [(0, 0), (0, 1), (0, 2), (0, 3), (1, 3), (1, 2), (1, 1), (1, 0)]
OFFSETS = (4, 3, -3, 2, -2, 1, -1, 0)
BATCHES = ((4,), (3, -3), (2, -2), (1, -1), (0,))


def place(core, u, o, z):
    x, y = (o, u) if core == 0 else (u, o)
    return (y * 2 + x) * 4 + z


def device_of(chip, core):
    return chip * 2 + core


def ring_pairs(step):
    pairs = []
    for core in range(2):
        for o in range(2):
            for i, (u, z) in enumerate(CYCLE):
                u2, z2 = CYCLE[(i + step) % 8]
                pairs.append((device_of(place(core, u, o, z), core), device_of(place(core, u2, o, z2), core)))
    return pairs


def swap_pairs():
    pairs = []
    for core in range(2):
        for o in range(2):
            for u, z in CYCLE:
                pairs.append((device_of(place(core, u, o, z), core), device_of(place(core, u, 1 - o, z), core)))
    return pairs


def core_pairs():
    return [(d, d ^ 1) for d in range(32)]


def relative_chips(sign):
    table = [[[[0, 0] for _ in OFFSETS] for _ in range(2)] for _ in range(16)]
    for core in range(2):
        for o in range(2):
            for i, (u, z) in enumerate(CYCLE):
                me = place(core, u, o, z)
                for slot, off in enumerate(OFFSETS):
                    u2, z2 = CYCLE[(i + sign * off) % 8]
                    for flip in range(2):
                        table[me][core][slot][flip] = place(core, u2, o ^ flip, z2)
    return table


def dot(a, b, dims):
    return lax.dot_general(a, b, dims, preferred_element_type=F32)


SMALL = dict(g1=0, s1=1, qb=2, vb=3, ob=4, g2=5, s2=6, fb=7, pb=11)

def compute(len_ref, tok_ref, cot_ref, sm_ref, act_ref, tg_ref, sg_ref, scr, loaders, ready, emit):
    wide, proj = loaders
    (a_all, att_all, c_all, ga_all, pre_all, mix_all, h_all, mid_all, prob_all,
     gd_all, gb_all, dpre_all, dmix_all, hid, acc, datt, tmp) = scr
    rows, width = tok_ref.shape
    bins = len_ref.shape[0]
    n = rows // bins
    chunk = 32
    chunks = rows // chunk

    def small(name):
        return sm_ref[:, SMALL[name] * width:(SMALL[name] + 1) * width]

    def add_small(name, value):
        ks = slice(SMALL[name] * width, (SMALL[name] + 1) * width)
        sg_ref[:, ks] = sg_ref[:, ks] + value

    def fc_cols(i):
        return pl.ds(pl.multiple_of((SMALL["fb"] + i) * width, 128), width)

    def at(base, r):
        return pl.ds(pl.multiple_of(base + r * chunk, chunk), chunk)

    sg_ref[...] = jnp.zeros_like(sg_ref)
    low_half = lax.broadcasted_iota(jnp.int32, (n, 2 * HD), 1) < HD
    row_i = lax.broadcasted_iota(jnp.int32, (n, n), 0)
    col_i = lax.broadcasted_iota(jnp.int32, (n, n), 1)
    allowed = []
    for m in range(bins):
        seg_r = jnp.zeros((n, n), jnp.int32)
        seg_c = jnp.zeros((n, n), jnp.int32)
        end = jnp.int32(0)
        for i in range(len_ref.shape[1]):
            end = end + len_ref[m, i]
            seg_r += (row_i >= end).astype(jnp.int32)
            seg_c += (col_i >= end).astype(jnp.int32)
        allowed.append(jnp.logical_and(seg_r == seg_c, col_i <= row_i))

    def halves(v):
        zero = jnp.zeros_like(v)
        return jnp.where(low_half, v, zero), jnp.where(low_half, zero, v)

    def join(parts):
        return jnp.where(low_half, parts[0], parts[1])

    def norm_rows(v):
        cen = v - jnp.mean(v, axis=-1, keepdims=True)
        rstd = lax.rsqrt(jnp.mean(cen * cen, axis=-1, keepdims=True) + EPS)
        return cen * rstd, rstd

    def forward_norm(src, base, gain, shift, dst):
        @pl.loop(0, chunks)
        def _(r):
            xhat, _ = norm_rows(src[at(base, r), :])
            dst[at(base, r), :] = (xhat * gain + shift).astype(BF16)

    def backward_norm(src, base, gain, names, dst16, dst_base):
        def step(r, sums):
            xhat, rstd = norm_rows(src[at(base, r), :])
            dy = acc[at(0, r), :]
            dx = dy * gain
            m1 = jnp.mean(dx, axis=-1, keepdims=True)
            m2 = jnp.mean(dx * xhat, axis=-1, keepdims=True)
            total = hid[at(0, r), :] + rstd * (dx - m1 - xhat * m2)
            hid[at(0, r), :] = total
            dst16[at(dst_base, r), :] = total.astype(BF16)
            return sums[0] + jnp.sum(dy * xhat, axis=0, keepdims=True), sums[1] + jnp.sum(dy, axis=0, keepdims=True)
        zero = jnp.zeros((1, width), F32)
        sums = lax.fori_loop(0, chunks, step, (zero, zero))
        add_small(names[0], sums[0])
        add_small(names[1], sums[1])

    def colsum(v16):
        return jnp.sum(v16.astype(F32), axis=0, keepdims=True)

    def forward(b):
        base = b * rows
        rs = slice(base, base + rows)
        forward_norm(h_all, base, small("g1"), small("s1"), a_all)
        ready("qo")
        mix_all[0, rs, :] = (dot(a_all[rs, :], wide(0), NN) + small("qb")).astype(BF16)
        mix_all[1, rs, :] = dot(a_all[rs, :], wide(1), NN).astype(BF16)
        mix_all[2, rs, :] = (dot(a_all[rs, :], wide(2), NN) + small("vb")).astype(BF16)

        @pl.loop(0, HEADS // 2)
        def _(hp):
            ls = pl.ds(pl.multiple_of(hp * 2 * HD, 2 * HD), 2 * HD)
            for m in range(bins):
                rm = slice(base + m * n, base + (m + 1) * n)
                q2, k2, v2 = (mix_all[j, rm, ls] for j in range(3))
                parts = []
                for half, qh in enumerate(halves(q2)):
                    s = jnp.where(allowed[m], dot(qh, k2, NT) * (HD ** -0.5), NEG)
                    e = jnp.exp(s - jnp.max(s, axis=-1, keepdims=True))
                    p = e / jnp.sum(e, axis=-1, keepdims=True)
                    prob_all[(b * bins + m) * HEADS + hp * 2 + half] = p
                    parts.append(dot(p.astype(BF16), v2, NN))
                att_all[rm, ls] = join(parts).astype(BF16)

        mid_all[rs, :] = h_all[rs, :] + (dot(att_all[rs, :], wide(3), NN) + small("ob"))
        forward_norm(mid_all, base, small("g2"), small("s2"), c_all)
        acc[...] = mid_all[rs, :] + small("pb")
        ready("f")
        ready("p")

        @pl.loop(0, 4)
        def _(i):
            pre_all[i, rs, :] = dot(c_all[rs, :], wide(4 + i), NN) + sm_ref[:, fc_cols(i)]

            @pl.loop(0, chunks)
            def _(r):
                v = pre_all[i, at(base, r), :]
                t = jnp.tanh(GELU_A * (v + GELU_B * (v * v * v)))
                ga_all[i, at(base, r), :] = (0.5 * v * (1.0 + t)).astype(BF16)
            acc[...] += dot(ga_all[i, rs, :], proj(i), NN)

    def backward(b):
        base = b * rows
        rs = slice(base, base + rows)
        add_small("pb", colsum(gd_all[rs, :]))
        acc[...] = jnp.zeros_like(acc)

        @pl.loop(0, 4)
        def _(i):
            tmp[...] = dot(gd_all[rs, :], proj(i), NT)

            def step(r, total):
                v = pre_all[i, at(base, r), :]
                v2 = v * v
                t = jnp.tanh(GELU_A * (v + GELU_B * (v * v2)))
                slope = 0.5 * (1.0 + t) + (0.5 * v) * (1.0 - t * t) * (GELU_A * (1.0 + 3.0 * GELU_B * v2))
                d = (tmp[at(0, r), :] * slope).astype(BF16)
                dpre_all[i, at(base, r), :] = d
                return total + colsum(d)
            total = lax.fori_loop(0, chunks, step, jnp.zeros((1, width), F32))
            sg_ref[:, fc_cols(i)] = sg_ref[:, fc_cols(i)] + total
            acc[...] += dot(dpre_all[i, rs, :], wide(4 + i), NT)

        backward_norm(mid_all, base, small("g2"), ("g2", "s2"), gb_all, base)
        add_small("ob", colsum(gb_all[rs, :]))
        datt[...] = dot(gb_all[rs, :], wide(3), NT).astype(BF16)

        @pl.loop(0, HEADS // 2)
        def _(hp):
            ls = pl.ds(pl.multiple_of(hp * 2 * HD, 2 * HD), 2 * HD)
            for m in range(bins):
                rm = slice(base + m * n, base + (m + 1) * n)
                q2, k2, v2 = (mix_all[j, rm, ls] for j in range(3))
                d2 = datt[m * n:(m + 1) * n, ls]
                dq, dk, dv = [], [], []
                for half, dh in enumerate(halves(d2)):
                    p = prob_all[(b * bins + m) * HEADS + hp * 2 + half]
                    dp = dot(dh, v2, NT)
                    dv.append(dot(p.astype(BF16), d2, TN))
                    ds = (p * (dp - jnp.sum(p * dp, axis=-1, keepdims=True))).astype(BF16)
                    dq.append(dot(ds, k2, NN))
                    dk.append(dot(ds, q2, TN))
                dmix_all[0, rm, ls] = (join(dq) * (HD ** -0.5)).astype(BF16)
                dmix_all[1, rm, ls] = (join(dk) * (HD ** -0.5)).astype(BF16)
                dmix_all[2, rm, ls] = join(dv).astype(BF16)

        add_small("qb", colsum(dmix_all[0, rs, :]))
        add_small("vb", colsum(dmix_all[2, rs, :]))
        acc[...] = dot(dmix_all[0, rs, :], wide(0), NT)
        acc[...] += dot(dmix_all[1, rs, :], wide(1), NT)
        acc[...] += dot(dmix_all[2, rs, :], wide(2), NT)
        backward_norm(h_all, base, small("g1"), ("g1", "s1"), gd_all if b == 1 else tg_ref, 0)

    h_all[0:rows, :] = tok_ref[...].astype(F32)
    forward(0)
    h_all[rows:2 * rows, :] = acc[...]
    forward(1)
    act_ref[...] = acc[...].astype(BF16)
    hid[...] = cot_ref[...].astype(F32)
    gd_all[rows:2 * rows, :] = cot_ref[...]
    backward(1)
    backward(0)
    emit(a_all, att_all, c_all, ga_all, dmix_all, gb_all, dpre_all, gd_all)


def compute_scratch(rows, width):
    two = 2 * rows
    return [
        pltpu.VMEM((two, width), BF16),
        pltpu.VMEM((two, width), BF16),
        pltpu.VMEM((two, width), BF16),
        pltpu.VMEM((4, two, width), BF16),
        pltpu.VMEM((4, two, width), F32),
        pltpu.VMEM((3, two, width), BF16),
        pltpu.VMEM((two, width), F32),
        pltpu.VMEM((two, width), F32),
        pltpu.VMEM((4 * HEADS, rows // 2, rows // 2), F32),
        pltpu.VMEM((two, width), BF16),
        pltpu.VMEM((two, width), BF16),
        pltpu.VMEM((4, two, width), BF16),
        pltpu.VMEM((3, two, width), BF16),
        pltpu.VMEM((rows, width), F32),
        pltpu.VMEM((rows, width), F32),
        pltpu.VMEM((rows, width), BF16),
        pltpu.VMEM((rows, width), F32),
    ]


N_SCR = 17
LIMIT = 64 * 1024 * 1024


def kernel(fast, n_in, n_out, *refs):
    tab, len_ref, tok_ref, cot_ref, sm_ref = refs[:5]
    w_in = refs[5:n_in]
    act_ref, tg_ref, sg_ref = refs[n_in:n_in + 3]
    d_out = refs[n_in + 3:n_in + n_out]
    scr = refs[n_in + n_out:n_in + n_out + N_SCR]
    wqf, wp, stage, stage_p, load_sem, store_sem = refs[n_in + n_out + N_SCR:]
    width = tok_ref.shape[1]
    high = wp.shape[1]
    per = width // high
    core = tab[0, 64]

    def chip_of(kind, who, slot, flip):
        return tab[0, ((kind * 2 + who) * 8 + slot) * 2 + flip]

    def rows_of(chip):
        return pl.ds(pl.multiple_of(chip * high, high), high)

    whole = {"qo": (wqf.at[0:4], 0), "f": (wqf.at[4:8], 1), "p": (wp, 2)}

    def pull(src, dst, part):
        pltpu.make_async_copy(src, dst, load_sem.at[whole[part][1]]).start()

    if fast:
        k = 0
        for who in range(2):
            c = core if who == 0 else 1 - core
            for slot in range(8):
                for flip in range(2):
                    chip = chip_of(0, who, slot, flip)
                    cols = pl.ds(2 * c, 2)
                    cols_f = pl.ds(4 + 2 * c, 2)
                    ps = pl.ds(4 * chip + 2 * c, 2)
                    if slot == 0:
                        one, two = w_in[k], w_in[k + 1]
                        k += 2
                        pull(one.at[0:2], wqf.at[cols, rows_of(chip), :], "qo")
                        pull(one.at[2], wqf.at[4 + 2 * c, rows_of(chip), :], "f")
                        pull(two.at[0], wqf.at[5 + 2 * c, rows_of(chip), :], "f")
                        pull(two.at[1:3], wp.at[ps], "p")
                    else:
                        one = w_in[k]
                        k += 1
                        pull(one.at[0:2], wqf.at[cols, rows_of(chip), :], "qo")
                        pull(one.at[2:4], wqf.at[cols_f, rows_of(chip), :], "f")
                        pull(one.at[4:6], wp.at[ps], "p")
    else:
        pull(w_in[0].at[0:4], wqf.at[0:4], "qo")
        pull(w_in[0].at[4:8], wqf.at[4:8], "f")
        pull(w_in[1], wp, "p")

    arrived = set()

    def ready(part):
        if part not in arrived:
            arrived.add(part)
            ref, s = whole[part]
            pltpu.make_async_copy(ref, ref, load_sem.at[s]).wait()

    def load_qf(k):
        return wqf[k]

    def load_p(i):
        return wp[pl.ds(i * per, per)].reshape(width, width)

    def drain(ref, s):
        pltpu.make_async_copy(ref, ref, store_sem.at[s]).wait()

    def push(src, dst, s):
        pltpu.make_async_copy(src, dst, store_sem.at[s]).start()

    part_rows = width // 2

    def product(left, right, out):
        @pl.loop(0, 2)
        def _(r):
            cols = pl.ds(pl.multiple_of(r * part_rows, part_rows), part_rows)
            value = dot(left[:, cols], right[...], TN).astype(BF16)
            out[pl.ds(r * (per // 2), per // 2)] = value.reshape(per // 2, high, width)

    def keep_refs(slot, flip):
        for i, offs in enumerate(BATCHES):
            if OFFSETS[slot] in offs:
                at = offs.index(OFFSETS[slot])
                return d_out[3 * i + flip].at[at], d_out[3 * i + 2].at[flip, at]

    def emit(a_all, att_all, c_all, ga_all, dmix_all, gb_all, dpre_all, gd_all):
        @pl.loop(0, 4)
        def _(i):
            product(ga_all.at[i], gd_all, stage_p.at[pl.ds(i * per, per)])
        if fast:
            for slot in range(8):
                for flip in range(2):
                    kept, sent = keep_refs(slot, flip)
                    for who, dst in ((0, kept), (1, sent)):
                        c = core if who == 0 else 1 - core
                        chip = chip_of(1, who, slot, flip)
                        push(stage_p.at[pl.ds(4 * chip + 2 * c, 2)], dst.at[4:6], 2)
        else:
            push(stage_p, d_out[1], 2)

        for job in range(4):
            s = job % 2
            if job >= 2:
                drain(stage.at[s], s)
            half = job % 2
            if job < 2:
                for h in range(2):
                    product(c_all, dpre_all.at[2 * half + h], stage.at[s, h])
            elif half == 0:
                for h in range(2):
                    product(a_all, dmix_all.at[h], stage.at[s, h])
            else:
                product(a_all, dmix_all.at[2], stage.at[s, 0])
                product(att_all, gb_all, stage.at[s, 1])
            g = 1 if job < 2 else 0
            if not fast:
                push(stage.at[s, 0], d_out[0].at[4 * g + 2 * half], s)
                push(stage.at[s, 1], d_out[0].at[4 * g + 2 * half + 1], s)
                continue
            for slot in range(8):
                for flip in range(2):
                    kept, sent = keep_refs(slot, flip)

                    @pl.when(core == half)
                    def _():
                        push(stage.at[s, :, chip_of(1, 0, slot, flip)], kept.at[2 * g:2 * g + 2], s)

                    @pl.when(core != half)
                    def _():
                        push(stage.at[s, :, chip_of(1, 1, slot, flip)], sent.at[2 * g:2 * g + 2], s)
        drain(stage.at[0], 0)
        drain(stage.at[1], 1)
        drain(stage_p, 2)

    compute(len_ref, tok_ref, cot_ref, sm_ref, act_ref, tg_ref, sg_ref, scr, (load_qf, load_p), ready, emit)


def run_kernel(fast, table, lengths, tokens, cotangent, smalls, w_in, d_shapes):
    rows, width = tokens.shape
    high = 48
    per = width // high
    n_in = 5 + len(w_in)
    smem = pl.BlockSpec(memory_space=pltpu.SMEM)
    vmem = pl.BlockSpec(memory_space=pltpu.VMEM)
    hbm = pl.BlockSpec(memory_space=pl.ANY)
    out_shape = [
        jax.ShapeDtypeStruct((rows, width), BF16),
        jax.ShapeDtypeStruct((rows, width), BF16),
        jax.ShapeDtypeStruct((1, 12 * width), F32),
    ] + [jax.ShapeDtypeStruct(s, BF16) for s in d_shapes]
    return pl.pallas_call(
        functools.partial(kernel, fast, n_in, len(out_shape)),
        out_shape=out_shape,
        in_specs=[smem, smem, vmem, vmem, vmem] + [hbm] * len(w_in),
        out_specs=[vmem, vmem, vmem] + [hbm] * len(d_shapes),
        scratch_shapes=compute_scratch(rows, width) + [
            pltpu.VMEM((8, width, width), BF16),
            pltpu.VMEM((4 * per, high, width), BF16),
            pltpu.VMEM((2, 2, per, high, width), BF16),
            pltpu.VMEM((4 * per, high, width), BF16),
            pltpu.SemaphoreType.DMA((3,)),
            pltpu.SemaphoreType.DMA((3,)),
        ],
        compiler_params=pltpu.CompilerParams(vmem_limit_bytes=LIMIT),
        cost_estimate=pl.CostEstimate(flops=22_000_000_000, bytes_accessed=32_000_000, transcendentals=4_000_000),
        name="blocks",
    )(table, lengths, tokens, cotangent, smalls, *w_in)


VECTORS = ("g1", "s1", "qv", "ob", "g2", "s2", "fb", "pb")


def spread(vectors, count, me):
    parts = []
    for v in vectors:
        mine = v.astype(BF16).astype(F32)
        owner = lax.broadcasted_iota(jnp.int32, (count, v.shape[0]), 0)
        parts.append(jnp.where(owner == me, mine[None, :], 0.0).reshape(-1))
    return jnp.concatenate(parts)


def own_parts(packed, sizes, count, me):
    parts, base = [], 0
    for size in sizes:
        parts.append(lax.dynamic_slice(packed, (base + me * size,), (size,)))
        base += size * count
    return parts


def total_small(packed, steps):
    for axis, pairs in steps:
        packed = packed + lax.ppermute(packed, axis, pairs)
    return packed


def swap_steps(sizes):
    steps = []
    for axis, size in sizes:
        bit = 1
        while bit < size:
            steps.append((axis, [(i, i ^ bit) for i in range(size)]))
            bit *= 2
    return steps


def gather_pieces(piece):
    cw, ccw, swap, pair = ring_pairs(1), ring_pairs(-1), swap_pairs(), core_pairs()

    def go(v, pairs):
        return lax.ppermute(v, AXES, pairs)

    got = {(0, 0): [piece]}
    right = left = piece
    newest = [((0, 0), 0)]
    for step in range(1, 5):
        if step < 4:
            right, left = go(right, cw), go(left, ccw)
            got[(step, 0)], got[(-step, 0)] = [right], [left]
            arrivals = [((step, 0), 0), ((-step, 0), 0)]
        else:
            half = piece.shape[0] // 2
            got[(4, 0)] = [go(right[:half], cw), go(left[half:], ccw)]
            got[(4, 1)] = [None, None]
            arrivals = [((4, 0), 0), ((4, 0), 1)]
        for (off, _), k in newest:
            got[(off, 1)] = [go(got[(off, 0)][k], swap)]
        newest = arrivals
    for (off, _), k in newest:
        got[(off, 1)][k] = go(got[(off, 0)][k], swap)
    own, other = [], []
    for off in OFFSETS:
        for flip in range(2):
            own += got[(off, flip)]
    other = [go(v, pair) for v in own]
    return own + other


def scatter_sums(outs):
    cw, ccw, swap, pair = ring_pairs(1), ring_pairs(-1), swap_pairs(), core_pairs()

    def go(v, pairs):
        return lax.ppermute(v, AXES, pairs)

    def add(a, b):
        return (a.astype(F32) + b.astype(F32)).astype(BF16)

    sums = []
    for i in range(len(BATCHES)):
        kept, flipped, sent = outs[3 * i:3 * i + 3]
        got = go(sent, pair)
        moved = go(add(flipped, got[1]), swap)
        sums.append((kept.astype(F32) + got[0].astype(F32) + moved.astype(F32)))
    half = sums[0].shape[1] // 2
    first = sums[0][0].astype(BF16)
    right, left = go(first[:half], cw), go(first[half:], ccw)
    zero = jnp.zeros_like(right)
    right = (sums[1][0] + jnp.concatenate([right, zero]).astype(F32)).astype(BF16)
    left = (sums[1][1] + jnp.concatenate([zero, left]).astype(F32)).astype(BF16)
    for i in (2, 3):
        right, left = go(right, cw), go(left, ccw)
        right = (sums[i][0] + right.astype(F32)).astype(BF16)
        left = (sums[i][1] + left.astype(F32)).astype(BF16)
    right, left = go(right, cw), go(left, ccw)
    return sums[4][0] + right.astype(F32) + left.astype(F32)


def body(sizes, tokens, lengths, ln1_gain, ln1_shift, w_qkv, qv_bias, w_out, out_bias, ln2_gain, ln2_shift,
         w_fc, fc_bias, w_proj, proj_bias, cotangent):
    dp, fsdp = sizes
    count = dp * fsdp
    me = lax.axis_index("dp") * fsdp + lax.axis_index("fsdp")
    bins, n, width = tokens.shape
    fast = (dp, fsdp) == (4, 8)
    vectors = (ln1_gain, ln1_shift, qv_bias, out_bias, ln2_gain, ln2_shift, fc_bias, proj_bias)
    steps = swap_steps((("fsdp", fsdp), ("dp", dp)))
    smalls = total_small(spread(vectors, count, me), steps).reshape(1, 12 * width)
    part = w_qkv.shape[0]
    wide = jnp.stack([
        w_qkv[:, :width], w_qkv[:, width:2 * width], w_qkv[:, 2 * width:], w_out,
        w_fc[:, :width], w_fc[:, width:2 * width], w_fc[:, 2 * width:3 * width], w_fc[:, 3 * width:],
    ]).astype(BF16)
    proj = w_proj.astype(BF16)
    flat = (lengths.reshape(bins, -1), tokens.reshape(-1, width), cotangent.reshape(-1, width), smalls)
    if fast:
        core = me % 2
        chips = jnp.array(TABLE, jnp.int32)
        table = lax.dynamic_slice(chips, (me, 0), (1, chips.shape[1]))
        halves = wide.reshape(2, 2, 2, part, width)
        mine = jnp.where(core == 0, halves[:, 0], halves[:, 1])
        theirs = jnp.where(core == 0, halves[:, 1], halves[:, 0])
        other = lax.ppermute(theirs, AXES, core_pairs())
        both = jnp.where(core == 0, jnp.concatenate([mine, other], 2), jnp.concatenate([other, mine], 2))
        piece = jnp.concatenate([both.reshape(4, 2 * part, width), proj.reshape(2, 2 * part, width)])
        pieces = gather_pieces(piece)
        shape = piece.shape
        d_shapes = []
        for offs in BATCHES:
            k = len(offs)
            d_shapes += [(k,) + shape, (k,) + shape, (2, k) + shape]
        act, tgrad, small_sums, *outs = run_kernel(True, table, *flat, pieces, d_shapes)
        total = scatter_sums(outs)
        high = total[:4, :part], total[:4, part:]
        own = jnp.where(core == 0, high[0], high[1])
        got = lax.ppermute(jnp.where(core == 0, high[1], high[0]), AXES, core_pairs())
        own, got = own.reshape(2, 2, part, width), got.reshape(2, 2, part, width)
        blocks = jnp.where(core == 0, jnp.concatenate([own, got], 1), jnp.concatenate([got, own], 1))
        blocks = blocks.reshape(8, part, width)
        d_proj = total[4:].reshape(w_proj.shape)
    else:
        table = jnp.zeros((1, 65), jnp.int32)
        w_all = lax.all_gather(wide, AXES, axis=1, tiled=True)
        p_all = lax.all_gather(proj, AXES, axis=0, tiled=True).reshape(-1, 48, width)
        act, tgrad, small_sums, d_wide, d_p = run_kernel(
            False, table, *flat, [w_all, p_all], [(8,) + (p_all.shape[0] // 4,) + p_all.shape[1:], p_all.shape])
        blocks = lax.psum_scatter(d_wide.reshape(w_all.shape), AXES, scatter_dimension=1, tiled=True).astype(F32)
        d_proj = lax.psum_scatter(d_p.reshape(-1, width), AXES, scatter_dimension=0, tiled=True).astype(F32)
    small = own_parts(total_small(small_sums.reshape(-1), steps), [v.shape[0] for v in vectors], count, me)
    g1, s1, qv, ob, g2, s2, fb, pb = small
    d_qkv = jnp.concatenate([blocks[0], blocks[1], blocks[2]], axis=1)
    d_fc = jnp.concatenate([blocks[4], blocks[5], blocks[6], blocks[7]], axis=1)
    return (act.reshape(tokens.shape), tgrad.reshape(tokens.shape), g1, s1, d_qkv, qv, blocks[3], ob, g2, s2,
            d_fc, fb, d_proj, pb)


def make_table():
    gather, scatter = relative_chips(-1), relative_chips(1)
    rows = []
    for chip in range(16):
        for core in range(2):
            row = []
            for table in (gather, scatter):
                for who in range(2):
                    for slot in range(8):
                        row += table[chip][core ^ who][slot]
            rows.append(row + [core])
    return rows


TABLE = make_table()


def solution(mesh):
    both = P(AXES)
    rows = P(None, AXES, None)
    matrix = P(AXES, None)
    weights = (both, both, matrix, both, matrix, both, both, both, matrix, both, matrix, both)
    return jax.shard_map(
        functools.partial(body, (mesh.shape["dp"], mesh.shape["fsdp"])),
        mesh=mesh,
        in_specs=(rows, rows) + weights + (rows,),
        out_specs=(rows, rows) + weights,
        check_vma=False,
    )
```

time: 835 us -> 281 us (0.34)
  waiting for transfers between devices: 578 us -> 81.5 us
  Pallas kernels: 0 us -> 99.9 us
  matrix products: 84.4 us -> 0 us
  blocking collectives: 80.9 us -> 0 us
  starting transfers between devices: 0.5 us -> 77.2 us
  local copies, waits for them, and re-layouts: 32.7 us -> 6.44 us
  other arithmetic: 34.9 us -> 9.36 us
  between operations: 15.7 us -> 1.61 us
    reduce_scatter x4 -> x0, waiting for transfers between devices: 397 us -> none  [the longest x1 142 us: body(): lax.psum_scatter(totals[8], ('dp', 'fsdp'), scatter_dimension=0, tiled=True)]
    all_gather x4 -> x0, waiting for transfers between devices: 181 us -> none  [the longest x1 63.8 us: fetch_weights(): lax.all_gather(w_fc.astype(jnp.bfloat16), ('dp', 'fsdp'), axis=0, tiled=T...]
    pallas_call x0 -> x1, Pallas kernels: none -> 99.9 us  [run_kernel(): pl.pallas_call(functools.partial(kernel, fast, n_in, len(out_shape)), out...]
    dot_general x36 -> x0, matrix products: 84.4 us -> none  [the longest x2 10.3 us: block_backward(): jnp.einsum('btf,btd->fd', active.astype(jnp.bfloat16), grad_down, preferr...]
    ppermute x0 -> x65, waiting for transfers between devices: none -> 81.5 us  [the longest x53 56.2 us: go(): return lax.ppermute(v, AXES, pairs)]
    unnamed x2 -> x0, blocking collectives: 80.9 us -> none
    ppermute x0 -> x65, starting transfers between devices: none -> 77.2 us  [the longest x53 63.5 us: go(): return lax.ppermute(v, AXES, pairs)]
    unnamed x250 -> x111, local copies, waits for them, and re-layouts: 23 us -> 1.35 us
  transfers between devices with their start and end apart: 8 -> 65, of which waited for: 7 -> 26; matrix products, arithmetic and copies ran while one was open for 11% -> 3% of each run, Pallas kernels for 0% -> 0%
where the time goes in v1:
time: 281 us; the launch traced here: 276 us
  Pallas kernels  99.9 us (36%)
  waiting for transfers between devices  81.5 us (29%)
  starting transfers between devices  77.2 us (27%)
  other arithmetic  9.36 us (3%)
  local copies, waits for them, and re-layouts  6.44 us (2%)
    pallas_call x1, Pallas kernels, run_kernel(): pl.pallas_call(functools.partial(kernel, fast, n_in, len(out_shape)), out...  99.9 us
    ppermute x53, starting transfers between devices, go(): return lax.ppermute(v, AXES, pairs)  63.5 us
    ppermute x53, waiting for transfers between devices, go(): return lax.ppermute(v, AXES, pairs)  56.2 us
    ppermute x10, waiting for transfers between devices, total_small(): packed = packed + lax.ppermute(packed, axis, pairs)  25.3 us
    ppermute x10, starting transfers between devices, total_small(): packed = packed + lax.ppermute(packed, axis, pairs)  8.2 us
  transfers between devices with their start and end apart: 65, of which 26 were waited for; matrix products, arithmetic and copies ran while one was open for 3% of the time, Pallas kernels for 0%

profile of v1, /device:TPU:17, one launch (start us, length us, event | category | flops | bytes accessed | tf_op | source)
XLA Modules:
  0.0 276.1 jit_solution(7356144891999168699)
XLA Ops:
  12.6 6.2 %collective-permute-done.1 = f32[9216]{0:T(1024)S(1)} collective-permute-done((f32[9216]{0:T(1024)S(1)}, f32[9216]{0:T(1024)S(1)}, u32[]{:S(2)}, u32[]{:S(2)}) %collective-permute-start.1) | collective-permute-done | bytes 36896 | tf_op jit(solution)/shard_map/ppermute | solution.py:479
  18.9 3.7 %collective-permute-done.2 = f32[9216]{0:T(1024)S(1)} collective-permute-done((f32[9216]{0:T(1024)S(1)}, f32[9216]{0:T(1024)S(1)}, u32[]{:S(2)}, u32[]{:S(2)}) %collective-permute-start.2) | collective-permute-done | bytes 36896 | tf_op jit(solution)/shard_map/ppermute | solution.py:479
  22.6 2.8 %collective-permute-done.3 = f32[9216]{0:T(1024)S(1)} collective-permute-done((f32[9216]{0:T(1024)S(1)}, f32[9216]{0:T(1024)S(1)}, u32[]{:S(2)}, u32[]{:S(2)}) %collective-permute-start.3) | collective-permute-done | bytes 36896 | tf_op jit(solution)/shard_map/ppermute | solution.py:479
  30.1 5.5 %collective-permute-start.35 = (bf16[6,48,768]{2,1,0:T(8,128)(2,1)S(1)}, bf16[6,48,768]{2,1,0:T(8,128)(2,1)S(1)}, u32[]{:S(2)}, u32[]{:S(2)}) collective-permute-start(bf16[6,48,768]{2,1,0:T(8,128)(2,1)S(1)} %collective-permute-done.6.refs_17_), channel_id=1, source_target_pairs={{0,1},{1,0},{2,3},{3,2},{4,5},{5,4},{6,7},{7,6},{8,9},{9,8},{10,11... | collective-permute-start | bytes 1327112 | tf_op jit(solution)/shard_map/ppermute | solution.py:497
  35.7 3.9 %collective-permute-start.37 = (bf16[6,48,768]{2,1,0:T(8,128)(2,1)S(1)}, bf16[6,48,768]{2,1,0:T(8,128)(2,1)S(1)}, u32[]{:S(2)}, u32[]{:S(2)}) collective-permute-start(bf16[6,48,768]{2,1,0:T(8,128)(2,1)S(1)} %collective-permute-done.10.refs_19_), channel_id=1, source_target_pairs={{0,1},{1,0},{2,3},{3,2},{4,5},{5,4},{6,7},{7,6},{8,9},{9,8},{10,11... | collective-permute-start | bytes 1327112 | tf_op jit(solution)/shard_map/ppermute | solution.py:497
  39.6 4.7 %collective-permute-start.8 = (bf16[6,48,768]{2,1,0:T(8,128)(2,1)S(1)}, bf16[6,48,768]{2,1,0:T(8,128)(2,1)S(1)}, u32[]{:S(2)}, u32[]{:S(2)}) collective-permute-start(bf16[6,48,768]{2,1,0:T(8,128)(2,1)S(1)} %collective-permute-done.7.refs_13_), channel_id=1, source_target_pairs={{0,2},{2,4},{4,6},{6,22},{22,20},{20,18},{18,16},{16,0},{8,10},{10... | collective-permute-start | bytes 1327112 | tf_op jit(solution)/shard_map/ppermute | solution.py:497
  48.7 5.3 %collective-permute-done.8.refs_9_ = bf16[6,48,768]{2,1,0:T(8,128)(2,1)S(1)} collective-permute-done((bf16[6,48,768]{2,1,0:T(8,128)(2,1)S(1)}, bf16[6,48,768]{2,1,0:T(8,128)(2,1)S(1)}, u32[]{:S(2)}, u32[]{:S(2)}) %collective-permute-start.8) | collective-permute-done | bytes 442400 | tf_op jit(solution)/shard_map/ppermute | solution.py:497
  57.4 5.7 %collective-permute-start.9 = (bf16[3,48,768]{2,1,0:T(8,128)(2,1)S(1)}, bf16[3,48,768]{2,1,0:T(8,128)(2,1)S(1)}, u32[]{:S(2)}, u32[]{:S(2)}) collective-permute-start(bf16[3,48,768]{2,1,0:T(8,128)(2,1)S(1)} %slice.186), channel_id=1, source_target_pairs={{0,2},{2,4},{4,6},{6,22},{22,20},{20,18},{18,16},{16,0},{8,10},{10... | collective-permute-start | bytes 663560 | tf_op jit(solution)/shard_map/ppermute | solution.py:497
  64.6 2.8 %collective-permute-done.9.refs_5_ = bf16[3,48,768]{2,1,0:T(8,128)(2,1)S(1)} collective-permute-done((bf16[3,48,768]{2,1,0:T(8,128)(2,1)S(1)}, bf16[3,48,768]{2,1,0:T(8,128)(2,1)S(1)}, u32[]{:S(2)}, u32[]{:S(2)}) %collective-permute-start.9) | collective-permute-done | bytes 221216 | tf_op jit(solution)/shard_map/ppermute | solution.py:497
  71.1 6.8 %collective-permute-done.14.refs_7_ = bf16[3,48,768]{2,1,0:T(8,128)(2,1)} collective-permute-done((bf16[3,48,768]{2,1,0:T(8,128)(2,1)S(1)}, bf16[3,48,768]{2,1,0:T(8,128)(2,1)}, u32[]{:S(2)}, u32[]{:S(2)}) %collective-permute-start.14) | collective-permute-done | bytes 221216 | tf_op jit(solution)/shard_map/ppermute | solution.py:497
  87.6 99.9 %blocks.1 = (bf16[256,768]{1,0:T(8,128)(2,1)}, bf16[256,768]{1,0:T(8,128)(2,1)}, f32[1,9216]{1,0:T(1,128)}, bf16[1,6,48,768]{3,2,1,0:T(8,128)(2,1)}, bf16[1,6,48...) custom-call(s32[1,65]{1,0:T(1,128)} %constant_dynamic-slice_fusion.r, ...), custom_call_target="tpu_custom_call" | custom-call | flops 22000001024 | bytes 32000000 | tf_op jit(solution)/shard_map/blocks/pallas_call | solution.py:438
  188.4 4.4 %collective-permute-done.54 = bf16[2,1,6,48,768]{4,3,2,1,0:T(8,128)(2,1)S(1)} collective-permute-done((bf16[2,1,6,48,768]{4,3,2,1,0:T(8,128)(2,1)}, bf16[2,1,6,48,768]{4,3,2,1,0:T(8,128)(2,1)S(1)}, u32[]{:S(2)}, u32[]{:S(2)}) %collective-permute-start.54) | collective-permute-done | bytes 884768 | tf_op jit(solution)/shard_map/ppermute | solution.py:529
  196.7 4.9 %collective-permute-done.55 = bf16[1,6,48,768]{3,2,1,0:T(8,128)(2,1)S(1)} collective-permute-done((bf16[1,6,48,768]{3,2,1,0:T(8,128)(2,1)S(1)}, bf16[1,6,48,768]{3,2,1,0:T(8,128)(2,1)S(1)}, u32[]{:S(2)}, u32[]{:S(2)}) %collective-permute-start.55) | collective-permute-done | bytes 442400 | tf_op jit(solution)/shard_map/ppermute | solution.py:529
  204.5 6.6 %collective-permute-done.53 = bf16[2,6,48,768]{3,2,1,0:T(8,128)(2,1)S(1)} collective-permute-done((bf16[2,6,48,768]{3,2,1,0:T(8,128)(2,1)S(1)}, bf16[2,6,48,768]{3,2,1,0:T(8,128)(2,1)S(1)}, u32[]{:S(2)}, u32[]{:S(2)}) %collective-permute-start.53) | collective-permute-done | bytes 884768 | tf_op jit(solution)/shard_map/ppermute | solution.py:529
  212.7 4.1 %collective-permute-start.57 = (bf16[6,48,768]{2,1,0:T(8,128)(2,1)S(1)}, bf16[6,48,768]{2,1,0:T(8,128)(2,1)S(1)}, u32[]{:S(2)}, u32[]{:S(2)}) collective-permute-start(bf16[6,48,768]{2,1,0:T(8,128)(2,1)S(1)} %get-tuple-element.54), channel_id=1, source_target_pairs={{0,2},{2,4},{4,6},{6,22},{22,20},{20,18},{18,16},{16,0},{8,10},{10... | collective-permute-start | bytes 1327112 | tf_op jit(solution)/shard_map/ppermute | solution.py:529
  218.1 5.1 %collective-permute-done.51 = bf16[2,6,48,768]{3,2,1,0:T(8,128)(2,1)S(1)} collective-permute-done((bf16[2,6,48,768]{3,2,1,0:T(8,128)(2,1)S(1)}, bf16[2,6,48,768]{3,2,1,0:T(8,128)(2,1)S(1)}, u32[]{:S(2)}, u32[]{:S(2)}) %collective-permute-start.51) | collective-permute-done | bytes 884768 | tf_op jit(solution)/shard_map/ppermute | solution.py:529
  227.6 5.8 %collective-permute-start.58 = (bf16[6,48,768]{2,1,0:T(8,128)(2,1)S(1)}, bf16[6,48,768]{2,1,0:T(8,128)(2,1)S(1)}, u32[]{:S(2)}, u32[]{:S(2)}) collective-permute-start(bf16[6,48,768]{2,1,0:T(8,128)(2,1)S(1)} %get-tuple-element.52), channel_id=1, source_target_pairs={{0,2},{2,4},{4,6},{6,22},{22,20},{20,18},{18,16},{16,0},{8,10},{10... | collective-permute-start | bytes 1327112 | tf_op jit(solution)/shard_map/ppermute | solution.py:529
  234.3 7.0 %collective-permute-done.58 = bf16[6,48,768]{2,1,0:T(8,128)(2,1)S(1)} collective-permute-done((bf16[6,48,768]{2,1,0:T(8,128)(2,1)S(1)}, bf16[6,48,768]{2,1,0:T(8,128)(2,1)S(1)}, u32[]{:S(2)}, u32[]{:S(2)}) %collective-permute-start.58) | collective-permute-done | bytes 442400 | tf_op jit(solution)/shard_map/ppermute | solution.py:529
  245.9 3.8 %collective-permute-start.41 = (f32[9216]{0:T(1024)S(1)}, f32[9216]{0:T(1024)S(1)}, u32[]{:S(2)}, u32[]{:S(2)}) collective-permute-start(f32[9216]{0:T(1024)S(1)} %bitcast.179), channel_id=1, source_target_pairs={{0,1},{1,0},{2,3},{3,2},{4,5},{5,4},{6,7},{7,6},{8,9},{9,8},{10,11... | collective-permute-start | bytes 110600 | tf_op jit(solution)/shard_map/ppermute | solution.py:479
  249.7 2.8 %collective-permute-done.59 = bf16[6,48,768]{2,1,0:T(8,128)(2,1)S(1)} collective-permute-done((bf16[6,48,768]{2,1,0:T(8,128)(2,1)S(1)}, bf16[6,48,768]{2,1,0:T(8,128)(2,1)S(1)}, u32[]{:S(2)}, u32[]{:S(2)}) %collective-permute-start.59) | collective-permute-done | bytes 442400 | tf_op jit(solution)/shard_map/ppermute | solution.py:529
  254.2 4.8 %collective-permute-start.64 = (f32[4,24,768]{2,1,0:T(8,128)S(1)}, f32[4,24,768]{2,1,0:T(8,128)S(1)}, u32[]{:S(2)}, u32[]{:S(2)}) collective-permute-start(f32[4,24,768]{2,1,0:T(8,128)S(1)} %get-tuple-element.57), channel_id=1, source_target_pairs={{0,1},{1,0},{2,3},{3,2},{4,5},{5,4},{6,7},{7,6},{8,9},{9,8},{10,11... | collective-permute-start | bytes 884744 | tf_op jit(solution)/shard_map/ppermute | solution.py:591
  259.1 2.8 %collective-permute-done.42 = f32[9216]{0:T(1024)S(1)} collective-permute-done((f32[9216]{0:T(1024)S(1)}, f32[9216]{0:T(1024)S(1)}, u32[]{:S(2)}, u32[]{:S(2)}) %collective-permute-start.42) | collective-permute-done | bytes 36896 | tf_op jit(solution)/shard_map/ppermute | solution.py:479
  262.0 3.5 %collective-permute-done.43 = f32[9216]{0:T(1024)S(1)} collective-permute-done((f32[9216]{0:T(1024)S(1)}, f32[9216]{0:T(1024)S(1)}, u32[]{:S(2)}, u32[]{:S(2)}) %collective-permute-start.43) | collective-permute-done | bytes 36896 | tf_op jit(solution)/shard_map/ppermute | solution.py:479
  265.5 2.8 %collective-permute-done.44 = f32[9216]{0:T(1024)S(1)} collective-permute-done((f32[9216]{0:T(1024)S(1)}, f32[9216]{0:T(1024)S(1)}, u32[]{:S(2)}, u32[]{:S(2)}) %collective-permute-start.44) | collective-permute-done | bytes 36896 | tf_op jit(solution)/shard_map/ppermute | solution.py:479
  (281 shorter events, 69.0 us)
Async XLA Ops:
  5.6 21.3 %collective-permute-start.6 = (bf16[6,48,768]{2,1,0:T(8,128)(2,1)S(1)}, bf16[6,48,768]{2,1,0:T(8,128)(2,1)S(1)}, u32[]{:S(2)}, u32[]{:S(2)}) collective-permute-start(bf16[6,48,768]{2,1,0:T(8,128)(2,1)S(1)} %pad_maximum_fusion.refs_21_), channel_id=1, source_target_pairs={{0,2},{2,4},{4,6},{6,22},{22,20},{20,18},{18,16},{16,0},{8,10},{10... | collective-permute-start | bytes 1327112 | tf_op jit(solution)/shard_map/ppermute | solution.py:497
  7.0 20.0 %collective-permute-start.10 = (bf16[6,48,768]{2,1,0:T(8,128)(2,1)S(1)}, bf16[6,48,768]{2,1,0:T(8,128)(2,1)S(1)}, u32[]{:S(2)}, u32[]{:S(2)}) collective-permute-start(bf16[6,48,768]{2,1,0:T(8,128)(2,1)S(1)} %pad_maximum_fusion.refs_21_), channel_id=1, source_target_pairs={{0,16},{2,0},{4,2},{6,4},{22,6},{20,22},{18,20},{16,18},{8,24},{10... | collective-permute-start | bytes 1327112 | tf_op jit(solution)/shard_map/ppermute | solution.py:497
  7.1 22.6 %collective-permute-start.22 = (bf16[6,48,768]{2,1,0:T(8,128)(2,1)S(1)}, bf16[6,48,768]{2,1,0:T(8,128)(2,1)S(1)}, u32[]{:S(2)}, u32[]{:S(2)}) collective-permute-start(bf16[6,48,768]{2,1,0:T(8,128)(2,1)S(1)} %pad_maximum_fusion.refs_21_), channel_id=1, source_target_pairs={{0,8},{2,10},{4,12},{6,14},{22,30},{20,28},{18,26},{16,24},{8,0},{... | collective-permute-start | bytes 1327112 | tf_op jit(solution)/shard_map/ppermute | solution.py:497
  8.6 21.5 %collective-permute-start.39 = (bf16[6,48,768]{2,1,0:T(8,128)(2,1)S(1)}, bf16[6,48,768]{2,1,0:T(8,128)(2,1)S(1)}, u32[]{:S(2)}, u32[]{:S(2)}) collective-permute-start(bf16[6,48,768]{2,1,0:T(8,128)(2,1)S(1)} %pad_maximum_fusion.refs_21_), channel_id=1, source_target_pairs={{0,1},{1,0},{2,3},{3,2},{4,5},{5,4},{6,7},{7,6},{8,9},{9,8},{10,11... | collective-permute-start | bytes 1327112 | tf_op jit(solution)/shard_map/ppermute | solution.py:497
  27.0 12.6 %collective-permute-start.11 = (bf16[6,48,768]{2,1,0:T(8,128)(2,1)S(1)}, bf16[6,48,768]{2,1,0:T(8,128)(2,1)S(1)}, u32[]{:S(2)}, u32[]{:S(2)}) collective-permute-start(bf16[6,48,768]{2,1,0:T(8,128)(2,1)S(1)} %collective-permute-done.10.refs_19_), channel_id=1, source_target_pairs={{0,16},{2,0},{4,2},{6,4},{22,6},{20,22},{18,20},{16,18},{8,24},{10... | collective-permute-start | bytes 1327112 | tf_op jit(solution)/shard_map/ppermute | solution.py:497
  29.8 14.6 %collective-permute-start.21 = (bf16[6,48,768]{2,1,0:T(8,128)(2,1)S(1)}, bf16[6,48,768]{2,1,0:T(8,128)(2,1)S(1)}, u32[]{:S(2)}, u32[]{:S(2)}) collective-permute-start(bf16[6,48,768]{2,1,0:T(8,128)(2,1)S(1)} %collective-permute-done.10.refs_19_), channel_id=1, source_target_pairs={{0,8},{2,10},{4,12},{6,14},{22,30},{20,28},{18,26},{16,24},{8,0},{... | collective-permute-start | bytes 1327112 | tf_op jit(solution)/shard_map/ppermute | solution.py:497
  30.1 14.3 %collective-permute-start.35 = (bf16[6,48,768]{2,1,0:T(8,128)(2,1)S(1)}, bf16[6,48,768]{2,1,0:T(8,128)(2,1)S(1)}, u32[]{:S(2)}, u32[]{:S(2)}) collective-permute-start(bf16[6,48,768]{2,1,0:T(8,128)(2,1)S(1)} %collective-permute-done.6.refs_17_), channel_id=1, source_target_pairs={{0,1},{1,0},{2,3},{3,2},{4,5},{5,4},{6,7},{7,6},{8,9},{9,8},{10,11... | collective-permute-start | bytes 1327112 | tf_op jit(solution)/shard_map/ppermute | solution.py:497
  39.6 14.3 %collective-permute-start.8 = (bf16[6,48,768]{2,1,0:T(8,128)(2,1)S(1)}, bf16[6,48,768]{2,1,0:T(8,128)(2,1)S(1)}, u32[]{:S(2)}, u32[]{:S(2)}) collective-permute-start(bf16[6,48,768]{2,1,0:T(8,128)(2,1)S(1)} %collective-permute-done.7.refs_13_), channel_id=1, source_target_pairs={{0,2},{2,4},{4,6},{6,22},{22,20},{20,18},{18,16},{16,0},{8,10},{10... | collective-permute-start | bytes 1327112 | tf_op jit(solution)/shard_map/ppermute | solution.py:497
  44.4 12.8 %collective-permute-start.18 = (bf16[6,48,768]{2,1,0:T(8,128)(2,1)S(1)}, bf16[6,48,768]{2,1,0:T(8,128)(2,1)S(1)}, u32[]{:S(2)}, u32[]{:S(2)}) collective-permute-start(bf16[6,48,768]{2,1,0:T(8,128)(2,1)S(1)} %collective-permute-done.7.refs_13_), channel_id=1, source_target_pairs={{0,8},{2,10},{4,12},{6,14},{22,30},{20,28},{18,26},{16,24},{8,0},{... | collective-permute-start | bytes 1327112 | tf_op jit(solution)/shard_map/ppermute | solution.py:497
  44.5 12.9 %collective-permute-start.19 = (bf16[6,48,768]{2,1,0:T(8,128)(2,1)S(1)}, bf16[6,48,768]{2,1,0:T(8,128)(2,1)S(1)}, u32[]{:S(2)}, u32[]{:S(2)}) collective-permute-start(bf16[6,48,768]{2,1,0:T(8,128)(2,1)S(1)} %collective-permute-done.11.refs_15_), channel_id=1, source_target_pairs={{0,8},{2,10},{4,12},{6,14},{22,30},{20,28},{18,26},{16,24},{8,0},{... | collective-permute-start | bytes 1327112 | tf_op jit(solution)/shard_map/ppermute | solution.py:497
  46.0 17.1 %collective-permute-start.31 = (bf16[6,48,768]{2,1,0:T(8,128)(2,1)S(1)}, bf16[6,48,768]{2,1,0:T(8,128)(2,1)S(1)}, u32[]{:S(2)}, u32[]{:S(2)}) collective-permute-start(bf16[6,48,768]{2,1,0:T(8,128)(2,1)S(1)} %collective-permute-done.7.refs_13_), channel_id=1, source_target_pairs={{0,1},{1,0},{2,3},{3,2},{4,5},{5,4},{6,7},{7,6},{8,9},{9,8},{10,11... | collective-permute-start | bytes 1327112 | tf_op jit(solution)/shard_map/ppermute | solution.py:497
  63.1 18.6 %collective-permute-start.16 = (bf16[6,48,768]{2,1,0:T(8,128)(2,1)S(1)}, bf16[6,48,768]{2,1,0:T(8,128)(2,1)S(1)}, u32[]{:S(2)}, u32[]{:S(2)}) collective-permute-start(bf16[6,48,768]{2,1,0:T(8,128)(2,1)S(1)} %collective-permute-done.8.refs_9_), channel_id=1, source_target_pairs={{0,8},{2,10},{4,12},{6,14},{22,30},{20,28},{18,26},{16,24},{8,0},{... | collective-permute-start | bytes 1327112 | tf_op jit(solution)/shard_map/ppermute | solution.py:497
  63.2 18.6 %collective-permute-start.17 = (bf16[6,48,768]{2,1,0:T(8,128)(2,1)S(1)}, bf16[6,48,768]{2,1,0:T(8,128)(2,1)S(1)}, u32[]{:S(2)}, u32[]{:S(2)}) collective-permute-start(bf16[6,48,768]{2,1,0:T(8,128)(2,1)S(1)} %collective-permute-done.12.refs_11_), channel_id=1, source_target_pairs={{0,8},{2,10},{4,12},{6,14},{22,30},{20,28},{18,26},{16,24},{8,0},{... | collective-permute-start | bytes 1327112 | tf_op jit(solution)/shard_map/ppermute | solution.py:497
  69.4 14.1 %collective-permute-start.27 = (bf16[6,48,768]{2,1,0:T(8,128)(2,1)S(1)}, bf16[6,48,768]{2,1,0:T(8,128)(2,1)S(1)}, u32[]{:S(2)}, u32[]{:S(2)}) collective-permute-start(bf16[6,48,768]{2,1,0:T(8,128)(2,1)S(1)} %collective-permute-done.8.refs_9_), channel_id=1, source_target_pairs={{0,1},{1,0},{2,3},{3,2},{4,5},{5,4},{6,7},{7,6},{8,9},{9,8},{10,11... | collective-permute-start | bytes 1327112 | tf_op jit(solution)/shard_map/ppermute | solution.py:497
  188.2 16.1 %collective-permute-start.50 = (bf16[2,2,6,48,768]{4,3,2,1,0:T(8,128)(2,1)}, bf16[2,2,6,48,768]{4,3,2,1,0:T(8,128)(2,1)S(1)}, u32[]{:S(2)}, u32[]{:S(2)}) collective-permute-start(bf16[2,2,6,48,768]{4,3,2,1,0:T(8,128)(2,1)} %get-tuple-element.42), channel_id=1, source_target_pairs={{0,1},{1,0},{2,3},{3,2},{4,5},{5,4},{6,7},{7,6},{8,9},{9,8},{10,11... | collective-permute-start | bytes 5308424 | tf_op jit(solution)/shard_map/ppermute | solution.py:529
  195.3 21.5 %collective-permute-start.48 = (bf16[2,2,6,48,768]{4,3,2,1,0:T(8,128)(2,1)}, bf16[2,2,6,48,768]{4,3,2,1,0:T(8,128)(2,1)S(1)}, u32[]{:S(2)}, u32[]{:S(2)}) collective-permute-start(bf16[2,2,6,48,768]{4,3,2,1,0:T(8,128)(2,1)} %get-tuple-element.39), channel_id=1, source_target_pairs={{0,1},{1,0},{2,3},{3,2},{4,5},{5,4},{6,7},{7,6},{8,9},{9,8},{10,11... | collective-permute-start | bytes 5308424 | tf_op jit(solution)/shard_map/ppermute | solution.py:529
  195.6 15.5 %collective-permute-start.53 = (bf16[2,6,48,768]{3,2,1,0:T(8,128)(2,1)S(1)}, bf16[2,6,48,768]{3,2,1,0:T(8,128)(2,1)S(1)}, u32[]{:S(2)}, u32[]{:S(2)}) collective-permute-start(bf16[2,6,48,768]{3,2,1,0:T(8,128)(2,1)S(1)} %fusion), channel_id=1, source_target_pairs={{0,8},{2,10},{4,12},{6,14},{22,30},{20,28},{18,26},{16,24},{8,0},{... | collective-permute-start | bytes 2654216 | tf_op jit(solution)/shard_map/ppermute | solution.py:529
  196.1 37.3 %collective-permute-start.46 = (bf16[2,1,6,48,768]{4,3,2,1,0:T(8,128)(2,1)S(1)}, bf16[2,1,6,48,768]{4,3,2,1,0:T(8,128)(2,1)S(1)}, u32[]{:S(2)}, u32[]{:S(2)}) collective-permute-start(bf16[2,1,6,48,768]{4,3,2,1,0:T(8,128)(2,1)S(1)} %copy-done.20), channel_id=1, source_target_pairs={{0,1},{1,0},{2,3},{3,2},{4,5},{5,4},{6,7},{7,6},{8,9},{9,8},{10,11... | collective-permute-start | bytes 2654216 | tf_op jit(solution)/shard_map/ppermute | solution.py:529
  212.7 12.7 %collective-permute-start.57 = (bf16[6,48,768]{2,1,0:T(8,128)(2,1)S(1)}, bf16[6,48,768]{2,1,0:T(8,128)(2,1)S(1)}, u32[]{:S(2)}, u32[]{:S(2)}) collective-permute-start(bf16[6,48,768]{2,1,0:T(8,128)(2,1)S(1)} %get-tuple-element.54), channel_id=1, source_target_pairs={{0,2},{2,4},{4,6},{6,22},{22,20},{20,18},{18,16},{16,0},{8,10},{10... | collective-permute-start | bytes 1327112 | tf_op jit(solution)/shard_map/ppermute | solution.py:529
  217.1 16.9 %collective-permute-start.49 = (bf16[2,6,48,768]{3,2,1,0:T(8,128)(2,1)S(1)}, bf16[2,6,48,768]{3,2,1,0:T(8,128)(2,1)S(1)}, u32[]{:S(2)}, u32[]{:S(2)}) collective-permute-start(bf16[2,6,48,768]{3,2,1,0:T(8,128)(2,1)S(1)} %fusion.4), channel_id=1, source_target_pairs={{0,8},{2,10},{4,12},{6,14},{22,30},{20,28},{18,26},{16,24},{8,0},{... | collective-permute-start | bytes 2654216 | tf_op jit(solution)/shard_map/ppermute | solution.py:529
  227.6 13.7 %collective-permute-start.58 = (bf16[6,48,768]{2,1,0:T(8,128)(2,1)S(1)}, bf16[6,48,768]{2,1,0:T(8,128)(2,1)S(1)}, u32[]{:S(2)}, u32[]{:S(2)}) collective-permute-start(bf16[6,48,768]{2,1,0:T(8,128)(2,1)S(1)} %get-tuple-element.52), channel_id=1, source_target_pairs={{0,2},{2,4},{4,6},{6,22},{22,20},{20,18},{18,16},{16,0},{8,10},{10... | collective-permute-start | bytes 1327112 | tf_op jit(solution)/shard_map/ppermute | solution.py:529
  233.5 16.2 %collective-permute-start.47 = (bf16[1,6,48,768]{3,2,1,0:T(8,128)(2,1)S(1)}, bf16[1,6,48,768]{3,2,1,0:T(8,128)(2,1)S(1)}, u32[]{:S(2)}, u32[]{:S(2)}) collective-permute-start(bf16[1,6,48,768]{3,2,1,0:T(8,128)(2,1)S(1)} %fusion.21), channel_id=1, source_target_pairs={{0,8},{2,10},{4,12},{6,14},{22,30},{20,28},{18,26},{16,24},{8,0},{... | collective-permute-start | bytes 1327112 | tf_op jit(solution)/shard_map/ppermute | solution.py:529
  245.9 13.0 %collective-permute-start.41 = (f32[9216]{0:T(1024)S(1)}, f32[9216]{0:T(1024)S(1)}, u32[]{:S(2)}, u32[]{:S(2)}) collective-permute-start(f32[9216]{0:T(1024)S(1)} %bitcast.179), channel_id=1, source_target_pairs={{0,1},{1,0},{2,3},{3,2},{4,5},{5,4},{6,7},{7,6},{8,9},{9,8},{10,11... | collective-permute-start | bytes 110600 | tf_op jit(solution)/shard_map/ppermute | solution.py:479
  254.2 19.8 %collective-permute-start.64 = (f32[4,24,768]{2,1,0:T(8,128)S(1)}, f32[4,24,768]{2,1,0:T(8,128)S(1)}, u32[]{:S(2)}, u32[]{:S(2)}) collective-permute-start(f32[4,24,768]{2,1,0:T(8,128)S(1)} %get-tuple-element.57), channel_id=1, source_target_pairs={{0,1},{1,0},{2,3},{3,2},{4,5},{5,4},{6,7},{7,6},{8,9},{9,8},{10,11... | collective-permute-start | bytes 884744 | tf_op jit(solution)/shard_map/ppermute | solution.py:591
  (90 other events, 1073.7 us)

commit v2 on v1

v2 whole, which is shorter than its diff:
```python
import functools

import jax
import jax.numpy as jnp
from jax import lax
from jax.experimental import pallas as pl
from jax.experimental.pallas import tpu as pltpu
from jax.sharding import PartitionSpec as P

HEADS = 12
HD = 64
EPS = 1e-05
NEG = -1e30
AXES = ("dp", "fsdp")
F32 = jnp.float32
BF16 = jnp.bfloat16
GELU_A = 0.7978845608028654
GELU_B = 0.044715

NT = (((1,), (1,)), ((), ()))
TN = (((0,), (0,)), ((), ()))
NN = (((1,), (0,)), ((), ()))

CYCLE = [(0, 0), (0, 1), (0, 2), (0, 3), (1, 3), (1, 2), (1, 1), (1, 0)]
OFFSETS = (4, 3, -3, 2, -2, 1, -1, 0)
BATCHES = ((4,), (3, -3), (2, -2), (1, -1), (0,))


def place(core, u, o, z):
    x, y = (o, u) if core == 0 else (u, o)
    return (y * 2 + x) * 4 + z


def device_of(chip, core):
    return chip * 2 + core


def ring_pairs(step):
    pairs = []
    for core in range(2):
        for o in range(2):
            for i, (u, z) in enumerate(CYCLE):
                u2, z2 = CYCLE[(i + step) % 8]
                pairs.append((device_of(place(core, u, o, z), core), device_of(place(core, u2, o, z2), core)))
    return pairs


def swap_pairs():
    pairs = []
    for core in range(2):
        for o in range(2):
            for u, z in CYCLE:
                pairs.append((device_of(place(core, u, o, z), core), device_of(place(core, u, 1 - o, z), core)))
    return pairs


def core_pairs():
    return [(d, d ^ 1) for d in range(32)]


def relative_chips(sign):
    table = [[[[0, 0] for _ in OFFSETS] for _ in range(2)] for _ in range(16)]
    for core in range(2):
        for o in range(2):
            for i, (u, z) in enumerate(CYCLE):
                me = place(core, u, o, z)
                for slot, off in enumerate(OFFSETS):
                    u2, z2 = CYCLE[(i + sign * off) % 8]
                    for flip in range(2):
                        table[me][core][slot][flip] = place(core, u2, o ^ flip, z2)
    return table


def dot(a, b, dims):
    return lax.dot_general(a, b, dims, preferred_element_type=F32)


SMALL = dict(g1=0, s1=1, qb=2, vb=3, ob=4, g2=5, s2=6, fb=7, pb=11)

def compute(len_ref, tok_ref, cot_ref, sm_ref, act_ref, tg_ref, sg_ref, scr, loaders, ready, emit):
    wide, proj = loaders
    (a_all, att_all, c_all, ga_all, slope_all, mix_all, xh1_all, xh2_all, rs1_all, rs2_all, prob_all,
     gd_all, gb_all, dpre_all, dmix_all, hid, acc, datt) = scr
    rows, width = tok_ref.shape
    bins = len_ref.shape[0]
    n = rows // bins

    def small(name):
        return sm_ref[:, SMALL[name] * width:(SMALL[name] + 1) * width]

    def add_small(name, value):
        ks = slice(SMALL[name] * width, (SMALL[name] + 1) * width)
        sg_ref[:, ks] = sg_ref[:, ks] + value

    def fc_cols(i):
        return slice((SMALL["fb"] + i) * width, (SMALL["fb"] + i + 1) * width)

    sg_ref[...] = jnp.zeros_like(sg_ref)
    low_half = lax.broadcasted_iota(jnp.int32, (n, 2 * HD), 1) < HD
    key_i = lax.broadcasted_iota(jnp.int32, (n, n), 0)
    query_i = lax.broadcasted_iota(jnp.int32, (n, n), 1)
    allowed = []
    for m in range(bins):
        seg_k = jnp.zeros((n, n), jnp.int32)
        seg_q = jnp.zeros((n, n), jnp.int32)
        end = jnp.int32(0)
        for i in range(len_ref.shape[1]):
            end = end + len_ref[m, i]
            seg_k += (key_i >= end).astype(jnp.int32)
            seg_q += (query_i >= end).astype(jnp.int32)
        allowed.append(jnp.logical_and(seg_k == seg_q, key_i <= query_i))

    def halves(v):
        zero = jnp.zeros_like(v)
        return jnp.where(low_half, v, zero), jnp.where(low_half, zero, v)

    def fold(v):
        return jnp.sum(v.reshape(v.shape[0] // 8, 8, v.shape[1]), axis=0)

    def forward_norm(v, rs, gain, shift, dst, xh_all, rs_all):
        cen = v - jnp.mean(v, axis=-1, keepdims=True)
        rstd = lax.rsqrt(jnp.mean(cen * cen, axis=-1, keepdims=True) + EPS)
        xhat = cen * rstd
        xh_all[rs, :] = xhat
        rs_all[rs, :] = jnp.broadcast_to(rstd, (rows, 128))
        dst[rs, :] = (xhat * gain + shift).astype(BF16)

    def backward_norm(xh_all, rs_all, rs, gain, names):
        xhat = xh_all[rs, :]
        dy = acc[...]
        dx = dy * gain
        m1 = jnp.mean(dx, axis=-1, keepdims=True)
        m2 = jnp.mean(dx * xhat, axis=-1, keepdims=True)
        add_small(names[0], jnp.sum(fold(dy * xhat), axis=0, keepdims=True))
        add_small(names[1], jnp.sum(fold(dy), axis=0, keepdims=True))
        return hid[...] + rs_all[rs, 0:1] * (dx - m1 - xhat * m2)

    def colsum(v16):
        return jnp.sum(fold(v16.astype(F32)), axis=0, keepdims=True)

    def stack(v):
        return jnp.concatenate(halves(v), axis=0)

    def unstack(v):
        return jnp.where(low_half, v[:n], v[n:])

    def pairs(base, body):
        for hp in range(HEADS // 2):
            body(slice(hp * 2 * HD, (hp + 1) * 2 * HD), [slice(base + m * n, base + (m + 1) * n) for m in range(bins)], hp)

    def forward(b):
        base = b * rows
        rs = slice(base, base + rows)
        forward_norm(acc[...], rs, small("g1"), small("s1"), a_all, xh1_all, rs1_all)
        ready("qo")
        mix_all[0, rs, :] = (dot(a_all[rs, :], wide(0), NN) + small("qb")).astype(BF16)
        mix_all[1, rs, :] = dot(a_all[rs, :], wide(1), NN).astype(BF16)
        mix_all[2, rs, :] = (dot(a_all[rs, :], wide(2), NN) + small("vb")).astype(BF16)

        def head_pair(ls, rms, hp):
            scores = [dot(stack(mix_all[1, rm, ls] * (HD ** -0.5)), mix_all[0, rm, ls], NT) for rm in rms]
            probs = []
            for m, v in enumerate(scores):
                v = jnp.where(allowed[m], v.reshape(2, n, n), NEG)
                e = jnp.exp(v - jnp.max(v, axis=1, keepdims=True))
                probs.append(e * (1.0 / jnp.sum(e, axis=1, keepdims=True)))
            for m, rm in enumerate(rms):
                prob_all[(b * bins + m) * (HEADS // 2) + hp] = probs[m]
                p16 = probs[m].reshape(2 * n, n).astype(BF16)
                att_all[rm, ls] = dot(p16, stack(mix_all[2, rm, ls]), TN).astype(BF16)
        pairs(base, head_pair)

        mid = acc[...] + (dot(att_all[rs, :], wide(3), NN) + small("ob"))
        acc[...] = mid + small("pb")
        forward_norm(mid, rs, small("g2"), small("s2"), c_all, xh2_all, rs2_all)
        ready("f")
        ready("p")

        for i in range(4):
            v = dot(c_all[rs, :], wide(4 + i), NN) + sm_ref[:, fc_cols(i)]
            v2 = v * v
            t = jnp.tanh(v * (GELU_A + (GELU_A * GELU_B) * v2))
            half = 0.5 + 0.5 * t
            ga_all[i, rs, :] = (v * half).astype(BF16)
            slope_all[i, rs, :] = half * (1.0 + v * (1.0 - t) * (GELU_A + (3.0 * GELU_A * GELU_B) * v2))
            acc[...] += dot(ga_all[i, rs, :], proj(i), NN)

    def backward(b):
        base = b * rows
        rs = slice(base, base + rows)
        add_small("pb", colsum(gd_all[rs, :]))
        acc[...] = jnp.zeros_like(acc)
        for i in range(4):
            d = (dot(gd_all[rs, :], proj(i), NT) * slope_all[i, rs, :]).astype(BF16)
            dpre_all[i, rs, :] = d
            sg_ref[:, fc_cols(i)] = sg_ref[:, fc_cols(i)] + colsum(d)
            acc[...] += dot(dpre_all[i, rs, :], wide(4 + i), NT)

        dmid = backward_norm(xh2_all, rs2_all, rs, small("g2"), ("g2", "s2"))
        hid[...] = dmid
        gb_all[rs, :] = dmid.astype(BF16)
        add_small("ob", colsum(gb_all[rs, :]))
        datt[...] = dot(gb_all[rs, :], wide(3), NT).astype(BF16)

        def head_pair(ls, rms, hp):
            outs = [datt[m * n:(m + 1) * n, ls] for m in range(bins)]
            dprobs = [dot(stack(mix_all[2, rm, ls]), outs[m], NT) for m, rm in enumerate(rms)]
            for m, rm in enumerate(rms):
                p = prob_all[(b * bins + m) * (HEADS // 2) + hp]
                dmix_all[2, rm, ls] = unstack(dot(p.reshape(2 * n, n).astype(BF16), outs[m], NN)).astype(BF16)
            dscores = []
            for m in range(bins):
                p = prob_all[(b * bins + m) * (HEADS // 2) + hp]
                dp = dprobs[m].reshape(2, n, n)
                ds = p * (dp - jnp.sum(p * dp, axis=1, keepdims=True))
                dscores.append(ds.reshape(2 * n, n).astype(BF16))
            for m, rm in enumerate(rms):
                ds = dscores[m]
                dmix_all[1, rm, ls] = (unstack(dot(ds, mix_all[0, rm, ls], NN)) * (HD ** -0.5)).astype(BF16)
                dmix_all[0, rm, ls] = (dot(ds, stack(mix_all[1, rm, ls]), TN) * (HD ** -0.5)).astype(BF16)
        pairs(base, head_pair)

        add_small("qb", colsum(dmix_all[0, rs, :]))
        add_small("vb", colsum(dmix_all[2, rs, :]))
        acc[...] = dot(dmix_all[0, rs, :], wide(0), NT)
        acc[...] += dot(dmix_all[1, rs, :], wide(1), NT)
        acc[...] += dot(dmix_all[2, rs, :], wide(2), NT)
        dh = backward_norm(xh1_all, rs1_all, rs, small("g1"), ("g1", "s1"))
        hid[...] = dh
        (gd_all if b == 1 else tg_ref)[0:rows, :] = dh.astype(BF16)

    acc[...] = tok_ref[...].astype(F32)
    forward(0)
    forward(1)
    act_ref[...] = acc[...].astype(BF16)
    hid[...] = cot_ref[...].astype(F32)
    gd_all[rows:2 * rows, :] = cot_ref[...]
    backward(1)
    backward(0)
    emit(a_all, att_all, c_all, ga_all, dmix_all, gb_all, dpre_all, gd_all)


def compute_scratch(rows, width):
    two = 2 * rows
    return [
        pltpu.VMEM((two, width), BF16),
        pltpu.VMEM((two, width), BF16),
        pltpu.VMEM((two, width), BF16),
        pltpu.VMEM((4, two, width), BF16),
        pltpu.VMEM((4, two, width), F32),
        pltpu.VMEM((3, two, width), BF16),
        pltpu.VMEM((two, width), F32),
        pltpu.VMEM((two, width), F32),
        pltpu.VMEM((two, 128), F32),
        pltpu.VMEM((two, 128), F32),
        pltpu.VMEM((2 * HEADS, 2, rows // 2, rows // 2), F32),
        pltpu.VMEM((two, width), BF16),
        pltpu.VMEM((two, width), BF16),
        pltpu.VMEM((4, two, width), BF16),
        pltpu.VMEM((3, two, width), BF16),
        pltpu.VMEM((rows, width), F32),
        pltpu.VMEM((rows, width), F32),
        pltpu.VMEM((rows, width), BF16),
    ]


N_SCR = 18
LIMIT = 64 * 1024 * 1024


def kernel(fast, n_in, n_out, *refs):
    tab, len_ref, tok_ref, cot_ref, sm_ref = refs[:5]
    w_in = refs[5:n_in]
    act_ref, tg_ref, sg_ref = refs[n_in:n_in + 3]
    d_out = refs[n_in + 3:n_in + n_out]
    scr = refs[n_in + n_out:n_in + n_out + N_SCR]
    wqf, wp, load_sem, store_sem = refs[n_in + n_out + N_SCR:]
    width = tok_ref.shape[1]
    high = wp.shape[1]
    per = width // high
    core = tab[0, 64]

    def chip_of(kind, who, slot, flip):
        return tab[0, ((kind * 2 + who) * 8 + slot) * 2 + flip]

    whole = {"qo": (wqf.at[0:4], 0), "f": (wqf.at[4:8], 1), "p": (wp, 2)}

    def pull(src, dst, part):
        pltpu.make_async_copy(src, dst, load_sem.at[whole[part][1]]).start()

    if fast:
        for who in range(2):
            c = core if who == 0 else 1 - core
            for flip in range(2):
                for i, offs in enumerate(BATCHES):
                    src = w_in[(who * 2 + flip) * len(BATCHES) + i]
                    for j, off in enumerate(offs):
                        chip = chip_of(0, who, OFFSETS.index(off), flip)
                        pull(src.at[6 * j:6 * j + 2], wqf.at[pl.ds(2 * c, 2), chip], "qo")
                        pull(src.at[6 * j + 2:6 * j + 4], wqf.at[pl.ds(4 + 2 * c, 2), chip], "f")
                        pull(src.at[6 * j + 4:6 * j + 6], wp.at[pl.ds(4 * chip + 2 * c, 2)], "p")
    else:
        pull(w_in[0].at[0:4], wqf.at[0:4], "qo")
        pull(w_in[0].at[4:8], wqf.at[4:8], "f")
        pull(w_in[1], wp, "p")

    arrived = set()

    def ready(part):
        if part not in arrived:
            arrived.add(part)
            ref, s = whole[part]
            pltpu.make_async_copy(ref, ref, load_sem.at[s]).wait()

    def load_qf(k):
        return wqf[k].reshape(width, width)

    def load_p(i):
        return wp[pl.ds(i * per, per)].reshape(width, width)

    def drain(ref, s):
        pltpu.make_async_copy(ref, ref, store_sem.at[s]).wait()

    def push(src, dst, s):
        pltpu.make_async_copy(src, dst, store_sem.at[s]).start()

    def product(left, right, out):
        half = width // 2
        for r in range(2):
            value = dot(left[:, r * half:(r + 1) * half], right[...], TN).astype(BF16)
            out[r * (per // 2):(r + 1) * (per // 2)] = value.reshape(per // 2, high, width)

    def keep_refs(slot, flip):
        for i, offs in enumerate(BATCHES):
            if OFFSETS[slot] in offs:
                at = offs.index(OFFSETS[slot])
                return d_out[3 * i + flip].at[at], d_out[3 * i + 2].at[flip, at]

    def emit(a_all, att_all, c_all, ga_all, dmix_all, gb_all, dpre_all, gd_all):
        for i in range(4):
            product(ga_all.at[i], gd_all, wp.at[i * per:(i + 1) * per])
        if fast:
            for slot in range(8):
                for flip in range(2):
                    kept, sent = keep_refs(slot, flip)
                    for who, dst in ((0, kept), (1, sent)):
                        c = core if who == 0 else 1 - core
                        push(wp.at[pl.ds(4 * chip_of(1, who, slot, flip) + 2 * c, 2)], dst.at[4:6], 1)
        else:
            push(wp, d_out[1], 1)

        for part, first in ((1, 4), (0, 0)):
            for half in range(2):
                k = first + 2 * half
                for h in range(2):
                    if part == 1:
                        product(c_all, dpre_all.at[2 * half + h], wqf.at[k + h])
                    elif k + h < 3:
                        product(a_all, dmix_all.at[k + h], wqf.at[k + h])
                    else:
                        product(att_all, gb_all, wqf.at[k + h])
                if not fast:
                    push(wqf.at[k:k + 2], d_out[0].at[k:k + 2], 0)
                    continue
                for slot in range(8):
                    for flip in range(2):
                        kept, sent = keep_refs(slot, flip)

                        @pl.when(core == half)
                        def _():
                            push(wqf.at[k:k + 2, chip_of(1, 0, slot, flip)], kept.at[2 * part:2 * part + 2], 0)

                        @pl.when(core != half)
                        def _():
                            push(wqf.at[k:k + 2, chip_of(1, 1, slot, flip)], sent.at[2 * part:2 * part + 2], 0)
        drain(wqf, 0)
        drain(wp, 1)

    compute(len_ref, tok_ref, cot_ref, sm_ref, act_ref, tg_ref, sg_ref, scr, (load_qf, load_p), ready, emit)


def run_kernel(fast, table, lengths, tokens, cotangent, smalls, w_in, d_shapes):
    rows, width = tokens.shape
    high = 48
    per = width // high
    n_in = 5 + len(w_in)
    smem = pl.BlockSpec(memory_space=pltpu.SMEM)
    vmem = pl.BlockSpec(memory_space=pltpu.VMEM)
    hbm = pl.BlockSpec(memory_space=pl.ANY)
    out_shape = [
        jax.ShapeDtypeStruct((rows, width), BF16),
        jax.ShapeDtypeStruct((rows, width), BF16),
        jax.ShapeDtypeStruct((1, 12 * width), F32),
    ] + [jax.ShapeDtypeStruct(s, BF16) for s in d_shapes]
    return pl.pallas_call(
        functools.partial(kernel, fast, n_in, len(out_shape)),
        out_shape=out_shape,
        in_specs=[smem, smem, vmem, vmem, vmem] + [hbm] * len(w_in),
        out_specs=[vmem, vmem, vmem] + [hbm] * len(d_shapes),
        scratch_shapes=compute_scratch(rows, width) + [
            pltpu.VMEM((8, per, high, width), BF16),
            pltpu.VMEM((4 * per, high, width), BF16),
            pltpu.SemaphoreType.DMA((3,)),
            pltpu.SemaphoreType.DMA((2,)),
        ],
        compiler_params=pltpu.CompilerParams(vmem_limit_bytes=LIMIT),
        cost_estimate=pl.CostEstimate(flops=22_000_000_000, bytes_accessed=32_000_000, transcendentals=4_000_000),
        name="blocks",
    )(table, lengths, tokens, cotangent, smalls, *w_in)


VECTORS = ("g1", "s1", "qv", "ob", "g2", "s2", "fb", "pb")


def spread(vectors, count, me):
    parts = []
    for v in vectors:
        mine = v.astype(BF16).astype(F32)
        owner = lax.broadcasted_iota(jnp.int32, (count, v.shape[0]), 0)
        parts.append(jnp.where(owner == me, mine[None, :], 0.0).reshape(-1))
    return jnp.concatenate(parts)


def own_parts(packed, sizes, count, me):
    parts, base = [], 0
    for size in sizes:
        parts.append(lax.dynamic_slice(packed, (base + me * size,), (size,)))
        base += size * count
    return parts


def total_small(packed, steps):
    for step in steps:
        packed = add_swapped(packed, step)
    return packed


def add_swapped(packed, step):
    return packed + lax.ppermute(packed, *step)


def swap_steps(sizes):
    steps = []
    for axis, size in sizes:
        bit = 1
        while bit < size:
            steps.append((axis, [(i, i ^ bit) for i in range(size)]))
            bit *= 2
    return steps


def both_ways():
    cw, ccw, swap, pair = ring_pairs(1), ring_pairs(-1), swap_pairs(), core_pairs()
    return tuple(functools.partial(lax.ppermute, axis_name=AXES, perm=p) for p in (cw, ccw, swap, pair))


def gather_pieces(piece, packed, steps):
    cw, ccw, swap, pair = both_ways()
    stage = lax.optimization_barrier
    half = piece.shape[0] // 2

    right, left = cw(piece), ccw(piece)
    s0 = swap(piece)
    c0 = pair(piece)
    packed = add_swapped(packed, steps[0])
    right, left, c0, packed = stage((right, left, c0, packed))

    p1 = jnp.concatenate([right, left])
    right, left = cw(right), ccw(left)
    s1 = swap(p1)
    c1 = pair(p1)
    c1, packed = stage((c1, packed))
    packed = add_swapped(packed, steps[1])
    right, left, s0, c1, packed = stage((right, left, s0, c1, packed))

    p2 = jnp.concatenate([right, left])
    right, left = cw(right), ccw(left)
    s2 = swap(p2)
    cs0 = pair(s0)
    cs0, packed = stage((cs0, packed))
    packed = add_swapped(packed, steps[2])
    packed, p2 = stage((packed, p2))
    c2 = pair(p2)
    right, left, s1, c2, cs0, packed = stage((right, left, s1, c2, cs0, packed))

    p3 = jnp.concatenate([right, left])
    right, left = cw(right[:half]), ccw(left[half:])
    s3 = swap(p3)
    cs1 = pair(s1)
    cs1, packed = stage((cs1, packed))
    packed = add_swapped(packed, steps[3])
    packed, p3 = stage((packed, p3))
    c3 = pair(p3)
    right, left, s2, c3, cs1, packed = stage((right, left, s2, c3, cs1, packed))

    p4 = jnp.concatenate([right, left])
    s4 = swap(p4)
    cs2 = pair(s2)
    c4 = pair(p4)
    cs2, c4, packed = stage((cs2, c4, packed))
    packed = add_swapped(packed, steps[4])
    s3, packed, cs2, c4 = stage((s3, packed, cs2, c4))
    cs3 = pair(s3)
    cs4 = pair(s4)
    return [p4, p3, p2, p1, piece, s4, s3, s2, s1, s0, c4, c3, c2, c1, c0, cs4, cs3, cs2, cs1, cs0], packed


def scatter_sums(outs, packed, steps):
    cw, ccw, swap, pair = both_ways()
    stage = lax.optimization_barrier

    def add(a, b):
        return (a.astype(F32) + b.astype(F32)).astype(BF16)

    kept, flipped, sent = outs[0::3], outs[1::3], list(outs[2::3])
    got = [pair(sent[0]), pair(sent[1]), pair(sent[2]), None, None]
    moved = [None] * 5

    def total(i):
        return kept[i].astype(F32) + got[i][0].astype(F32) + moved[i].astype(F32)

    moved[0] = swap(add(flipped[0], got[0][1]))
    sent[3], got[0] = stage((sent[3], got[0]))
    got[3] = pair(sent[3])
    moved[1] = swap(add(flipped[1], got[1][1]))
    sent[4], got[1] = stage((sent[4], got[1]))
    got[4] = pair(sent[4])
    moved[0], got[2], got[3] = stage((moved[0], got[2], got[3]))
    first = total(0)[0].astype(BF16)
    half = first.shape[0] // 2
    right, left = cw(first[:half]), ccw(first[half:])
    moved[2] = swap(add(flipped[2], got[2][1]))
    got[4], packed = stage((got[4], packed))
    packed = add_swapped(packed, steps[0])
    zero = jnp.zeros_like(right)
    moved[1], right, left, packed = stage((moved[1], right, left, packed))
    second = total(1)
    right = cw((second[0] + jnp.concatenate([right, zero]).astype(F32)).astype(BF16))
    left = ccw((second[1] + jnp.concatenate([zero, left]).astype(F32)).astype(BF16))
    moved[3] = swap(add(flipped[3], got[3][1]))
    packed = add_swapped(packed, steps[1])
    moved[2], right, left, packed = stage((moved[2], right, left, packed))
    third = total(2)
    right = cw((third[0] + right.astype(F32)).astype(BF16))
    left = ccw((third[1] + left.astype(F32)).astype(BF16))
    moved[4] = swap(add(flipped[4], got[4][1]))
    packed = add_swapped(packed, steps[2])
    moved[3], right, left, packed = stage((moved[3], right, left, packed))
    fourth = total(3)
    right = cw((fourth[0] + right.astype(F32)).astype(BF16))
    left = ccw((fourth[1] + left.astype(F32)).astype(BF16))
    packed = add_swapped(packed, steps[3])
    moved[4], packed = stage((moved[4], packed))
    packed = add_swapped(packed, steps[4])
    return total(4)[0] + right.astype(F32) + left.astype(F32), packed


def body(sizes, tokens, lengths, ln1_gain, ln1_shift, w_qkv, qv_bias, w_out, out_bias, ln2_gain, ln2_shift,
         w_fc, fc_bias, w_proj, proj_bias, cotangent):
    dp, fsdp = sizes
    count = dp * fsdp
    me = lax.axis_index("dp") * fsdp + lax.axis_index("fsdp")
    bins, n, width = tokens.shape
    fast = (dp, fsdp) == (4, 8)
    vectors = (ln1_gain, ln1_shift, qv_bias, out_bias, ln2_gain, ln2_shift, fc_bias, proj_bias)
    steps = swap_steps((("fsdp", fsdp), ("dp", dp)))
    packed = spread(vectors, count, me)
    part = w_qkv.shape[0]
    wide = jnp.stack([
        w_qkv[:, :width], w_qkv[:, width:2 * width], w_qkv[:, 2 * width:], w_out,
        w_fc[:, :width], w_fc[:, width:2 * width], w_fc[:, 2 * width:3 * width], w_fc[:, 3 * width:],
    ]).astype(BF16)
    proj = w_proj.astype(BF16)
    flat = (lengths.reshape(bins, -1), tokens.reshape(-1, width), cotangent.reshape(-1, width))
    if fast:
        core = me % 2
        chips = jnp.array(TABLE, jnp.int32)
        table = lax.dynamic_slice(chips, (me, 0), (1, chips.shape[1]))
        halves = wide.reshape(2, 2, 2, part, width)
        mine = jnp.where(core == 0, halves[:, 0], halves[:, 1])
        theirs = jnp.where(core == 0, halves[:, 1], halves[:, 0])
        other = lax.ppermute(theirs, AXES, core_pairs())
        both = jnp.where(core == 0, jnp.concatenate([mine, other], 2), jnp.concatenate([other, mine], 2))
        piece = jnp.concatenate([both.reshape(4, 2 * part, width), proj.reshape(2, 2 * part, width)])
        pieces, packed = gather_pieces(piece, packed, steps)
        shape = piece.shape
        d_shapes = []
        for offs in BATCHES:
            k = len(offs)
            d_shapes += [(k,) + shape, (k,) + shape, (2, k) + shape]
        act, tgrad, small_sums, *outs = run_kernel(True, table, *flat, packed.reshape(1, -1), pieces, d_shapes)
        total, small_sums = scatter_sums(outs, small_sums.reshape(-1), steps)
        high = total[:4, :part], total[:4, part:]
        own = jnp.where(core == 0, high[0], high[1])
        got = lax.ppermute(jnp.where(core == 0, high[1], high[0]), AXES, core_pairs())
        own, got = own.reshape(2, 2, part, width), got.reshape(2, 2, part, width)
        blocks = jnp.where(core == 0, jnp.concatenate([own, got], 1), jnp.concatenate([got, own], 1))
        blocks = blocks.reshape(8, part, width)
        d_proj = total[4:].reshape(w_proj.shape)
    else:
        table = jnp.zeros((1, 65), jnp.int32)
        w_all = lax.all_gather(wide, AXES, axis=1, tiled=True)
        p_all = lax.all_gather(proj, AXES, axis=0, tiled=True).reshape(-1, 48, width)
        blocks_all = w_all.reshape((8, -1) + p_all.shape[1:])
        act, tgrad, small_sums, d_wide, d_p = run_kernel(
            False, table, *flat, total_small(packed, steps).reshape(1, -1), [blocks_all, p_all],
            [blocks_all.shape, p_all.shape])
        blocks = lax.psum_scatter(d_wide.reshape(w_all.shape), AXES, scatter_dimension=1, tiled=True).astype(F32)
        d_proj = lax.psum_scatter(d_p.reshape(-1, width), AXES, scatter_dimension=0, tiled=True).astype(F32)
        small_sums = total_small(small_sums.reshape(-1), steps)
    small = own_parts(small_sums, [v.shape[0] for v in vectors], count, me)
    g1, s1, qv, ob, g2, s2, fb, pb = small
    d_qkv = jnp.concatenate([blocks[0], blocks[1], blocks[2]], axis=1)
    d_fc = jnp.concatenate([blocks[4], blocks[5], blocks[6], blocks[7]], axis=1)
    return (act.reshape(tokens.shape), tgrad.reshape(tokens.shape), g1, s1, d_qkv, qv, blocks[3], ob, g2, s2,
            d_fc, fb, d_proj, pb)


def make_table():
    gather, scatter = relative_chips(-1), relative_chips(1)
    rows = []
    for chip in range(16):
        for core in range(2):
            row = []
            for table in (gather, scatter):
                for who in range(2):
                    for slot in range(8):
                        row += table[chip][core ^ who][slot]
            rows.append(row + [core])
    return rows


TABLE = make_table()


def solution(mesh):
    both = P(AXES)
    rows = P(None, AXES, None)
    matrix = P(AXES, None)
    weights = (both, both, matrix, both, matrix, both, both, both, matrix, both, matrix, both)
    return jax.shard_map(
        functools.partial(body, (mesh.shape["dp"], mesh.shape["fsdp"])),
        mesh=mesh,
        in_specs=(rows, rows) + weights + (rows,),
        out_specs=(rows, rows) + weights,
        check_vma=False,
    )
```

time: 281 us -> 223 us (0.79)
  the two profiles are of different devices: /device:TPU:17 before, /device:TPU:0 now
where the time goes in v2:
time: 223 us; the launch traced here: 220 us
  waiting for transfers between devices  128 us (57%)
  Pallas kernels  42.5 us (19%)
  starting transfers between devices  31.1 us (14%)
  other arithmetic  9.3 us (4%)
  local copies, waits for them, and re-layouts  7.45 us (3%)
    ppermute x10, waiting for transfers between devices, add_swapped(): return packed + lax.ppermute(packed, *step)  56.8 us
    pallas_call x1, Pallas kernels, run_kernel(): pl.pallas_call(functools.partial(kernel, fast, n_in, len(out_shape)), out...  42.5 us
    ppermute x2, waiting for transfers between devices, gather_pieces(): right, left = (cw(piece), ccw(piece))  10.2 us
    ppermute x1, waiting for transfers between devices, scatter_sums(): moved[1] = swap(add(flipped[1], got[1][1]))  9.21 us
    ppermute x2, waiting for transfers between devices, gather_pieces(): right, left = (cw(right[:half]), ccw(left[half:]))  7.26 us
    ppermute x1, waiting for transfers between devices, gather_pieces(): s1 = swap(p1)  6.73 us
    ppermute x10, starting transfers between devices, add_swapped(): return packed + lax.ppermute(packed, *step)  6.47 us
    ppermute x1, waiting for transfers between devices, gather_pieces(): s3 = swap(p3)  4.95 us
  transfers between devices with their start and end apart: 53, of which 32 were waited for; matrix products, arithmetic and copies ran while one was open for 4% of the time, Pallas kernels for 0%

profile of v2, /device:TPU:0, one launch (start us, length us, event | category | flops | bytes accessed | tf_op | source)
XLA Modules:
  0.0 220.2 jit_solution(7270424667330319637)
XLA Ops:
  5.5 2.9 %collective-permute-start.1 = (bf16[6,48,768]{2,1,0:T(8,128)(2,1)S(1)}, bf16[6,48,768]{2,1,0:T(8,128)(2,1)S(1)}, u32[]{:S(2)}, u32[]{:S(2)}) collective-permute-start(bf16[6,48,768]{2,1,0:T(8,128)(2,1)S(1)} %pad_maximum_fusion.refs_9_), channel_id=1, source_target_pairs={{0,2},{2,4},{4,6},{6,22},{22,20},{20,18},{18,16},{16,0},{8,10},{10... | collective-permute-start | bytes 1327112 | tf_op jit(solution)/shard_map/ppermute | solution.py:462
  10.3 8.0 %collective-permute-done.1 = bf16[6,48,768]{2,1,0:T(8,128)(2,1)S(1)} collective-permute-done((bf16[6,48,768]{2,1,0:T(8,128)(2,1)S(1)}, bf16[6,48,768]{2,1,0:T(8,128)(2,1)S(1)}, u32[]{:S(2)}, u32[]{:S(2)}) %collective-permute-start.1) | collective-permute-done | bytes 442400 | tf_op jit(solution)/shard_map/ppermute | solution.py:462
  24.7 10.7 %collective-permute-done.9 = f32[9216]{0:T(1024)S(1)} collective-permute-done((f32[9216]{0:T(1024)S(1)}, f32[9216]{0:T(1024)S(1)}, u32[]{:S(2)}, u32[]{:S(2)}) %collective-permute-start.9) | collective-permute-done | bytes 36896 | tf_op jit(solution)/shard_map/ppermute | solution.py:439
  37.3 2.4 %collective-permute-start.14 = (f32[9216]{0:T(1024)S(1)}, f32[9216]{0:T(1024)S(1)}, u32[]{:S(2)}, u32[]{:S(2)}) collective-permute-start(f32[9216]{0:T(1024)S(1)} %add.155), channel_id=1, source_target_pairs={{0,4},{1,5},{2,6},{3,7},{4,0},{5,1},{6,2},{7,3},{8,12},{9,13},{10,... | collective-permute-start | bytes 110600 | tf_op jit(solution)/shard_map/ppermute | solution.py:439
  39.8 2.8 %collective-permute-done.14 = f32[9216]{0:T(1024)S(1)} collective-permute-done((f32[9216]{0:T(1024)S(1)}, f32[9216]{0:T(1024)S(1)}, u32[]{:S(2)}, u32[]{:S(2)}) %collective-permute-start.14) | collective-permute-done | bytes 36896 | tf_op jit(solution)/shard_map/ppermute | solution.py:439
  44.7 6.7 %collective-permute-done.12.refs_13_ = bf16[12,48,768]{2,1,0:T(8,128)(2,1)S(1)} collective-permute-done((bf16[12,48,768]{2,1,0:T(8,128)(2,1)S(1)}, bf16[12,48,768]{2,1,0:T(8,128)(2,1)S(1)}, u32[]{:S(2)}, u32[]{:S(2)}) %collective-permute-start.12) | collective-permute-done | bytes 884768 | tf_op jit(solution)/shard_map/ppermute | solution.py:470
  53.0 2.7 %collective-permute-done.11 = bf16[6,48,768]{2,1,0:T(8,128)(2,1)S(1)} collective-permute-done((bf16[6,48,768]{2,1,0:T(8,128)(2,1)S(1)}, bf16[6,48,768]{2,1,0:T(8,128)(2,1)S(1)}, u32[]{:S(2)}, u32[]{:S(2)}) %collective-permute-start.11) | collective-permute-done | bytes 442400 | tf_op jit(solution)/shard_map/ppermute | solution.py:477
  58.9 11.6 %collective-permute-done.21 = f32[9216]{0:T(1024)S(1)} collective-permute-done((f32[9216]{0:T(1024)S(1)}, f32[9216]{0:T(1024)S(1)}, u32[]{:S(2)}, u32[]{:S(2)}) %collective-permute-start.21) | collective-permute-done | bytes 36896 | tf_op jit(solution)/shard_map/ppermute | solution.py:439
  72.8 4.9 %collective-permute-done.17 = bf16[3,48,768]{2,1,0:T(8,128)(2,1)S(1)} collective-permute-done((bf16[3,48,768]{2,1,0:T(8,128)(2,1)S(1)}, bf16[3,48,768]{2,1,0:T(8,128)(2,1)S(1)}, u32[]{:S(2)}, u32[]{:S(2)}) %collective-permute-start.17) | collective-permute-done | bytes 221216 | tf_op jit(solution)/shard_map/ppermute | solution.py:487
  77.7 2.4 %collective-permute-done.18 = bf16[3,48,768]{2,1,0:T(8,128)(2,1)S(1)} collective-permute-done((bf16[3,48,768]{2,1,0:T(8,128)(2,1)S(1)}, bf16[3,48,768]{2,1,0:T(8,128)(2,1)S(1)}, u32[]{:S(2)}, u32[]{:S(2)}) %collective-permute-start.18) | collective-permute-done | bytes 221216 | tf_op jit(solution)/shard_map/ppermute | solution.py:487
  80.8 2.4 %collective-permute-done.24.refs_15_ = bf16[6,48,768]{2,1,0:T(8,128)(2,1)S(1)} collective-permute-done((bf16[6,48,768]{2,1,0:T(8,128)(2,1)S(1)}, bf16[6,48,768]{2,1,0:T(8,128)(2,1)S(1)}, u32[]{:S(2)}, u32[]{:S(2)}) %collective-permute-start.24) | collective-permute-done | bytes 442400 | tf_op jit(solution)/shard_map/ppermute | solution.py:499
  84.3 3.4 %collective-permute-done.25 = f32[9216]{0:T(1024)S(1)} collective-permute-done((f32[9216]{0:T(1024)S(1)}, f32[9216]{0:T(1024)S(1)}, u32[]{:S(2)}, u32[]{:S(2)}) %collective-permute-start.25) | collective-permute-done | bytes 36896 | tf_op jit(solution)/shard_map/ppermute | solution.py:439
  88.3 4.9 %collective-permute-done.16.refs_11_ = bf16[12,48,768]{2,1,0:T(8,128)(2,1)S(1)} collective-permute-done((bf16[12,48,768]{2,1,0:T(8,128)(2,1)S(1)}, bf16[12,48,768]{2,1,0:T(8,128)(2,1)S(1)}, u32[]{:S(2)}, u32[]{:S(2)}) %collective-permute-start.16) | collective-permute-done | bytes 884768 | tf_op jit(solution)/shard_map/ppermute | solution.py:488
  94.3 3.7 %collective-permute-done.26.refs_10_ = bf16[6,48,768]{2,1,0:T(8,128)(2,1)S(1)} collective-permute-done((bf16[6,48,768]{2,1,0:T(8,128)(2,1)S(1)}, bf16[6,48,768]{2,1,0:T(8,128)(2,1)S(1)}, u32[]{:S(2)}, u32[]{:S(2)}) %collective-permute-start.26) | collective-permute-done | bytes 442400 | tf_op jit(solution)/shard_map/ppermute | solution.py:497
  101.0 42.5 %blocks.1 = (bf16[256,768]{1,0:T(8,128)(2,1)}, bf16[256,768]{1,0:T(8,128)(2,1)}, f32[1,9216]{1,0:T(1,128)}, bf16[1,6,48,768]{3,2,1,0:T(8,128)(2,1)}, bf16[1,6,48...) custom-call(s32[1,65]{1,0:T(1,128)} %constant_dynamic-slice_fusion.r, ...), custom_call_target="tpu_custom_call" | custom-call | flops 22000001024 | bytes 32000000 | tf_op jit(solution)/shard_map/blocks/pallas_call | solution.py:395
  144.2 4.6 %collective-permute-done.32 = bf16[2,1,6,48,768]{4,3,2,1,0:T(8,128)(2,1)S(1)} collective-permute-done((bf16[2,1,6,48,768]{4,3,2,1,0:T(8,128)(2,1)}, bf16[2,1,6,48,768]{4,3,2,1,0:T(8,128)(2,1)S(1)}, u32[]{:S(2)}, u32[]{:S(2)}) %collective-permute-start.32) | collective-permute-done | bytes 884768 | tf_op jit(solution)/shard_map/ppermute | solution.py:516
  155.2 3.6 %collective-permute-done.33 = bf16[1,6,48,768]{3,2,1,0:T(8,128)(2,1)S(1)} collective-permute-done((bf16[1,6,48,768]{3,2,1,0:T(8,128)(2,1)S(1)}, bf16[1,6,48,768]{3,2,1,0:T(8,128)(2,1)S(1)}, u32[]{:S(2)}, u32[]{:S(2)}) %collective-permute-start.33) | collective-permute-done | bytes 442400 | tf_op jit(solution)/shard_map/ppermute | solution.py:522
  161.5 9.2 %collective-permute-done.38 = bf16[2,6,48,768]{3,2,1,0:T(8,128)(2,1)S(1)} collective-permute-done((bf16[2,6,48,768]{3,2,1,0:T(8,128)(2,1)S(1)}, bf16[2,6,48,768]{3,2,1,0:T(8,128)(2,1)S(1)}, u32[]{:S(2)}, u32[]{:S(2)}) %collective-permute-start.38) | collective-permute-done | bytes 884768 | tf_op jit(solution)/shard_map/ppermute | solution.py:525
  173.6 9.8 %collective-permute-done.44 = f32[9216]{0:T(1024)S(1)} collective-permute-done((f32[9216]{0:T(1024)S(1)}, f32[9216]{0:T(1024)S(1)}, u32[]{:S(2)}, u32[]{:S(2)}) %collective-permute-start.44) | collective-permute-done | bytes 36896 | tf_op jit(solution)/shard_map/ppermute | solution.py:439
  187.9 8.1 %collective-permute-done.47 = f32[9216]{0:T(1024)S(1)} collective-permute-done((f32[9216]{0:T(1024)S(1)}, f32[9216]{0:T(1024)S(1)}, u32[]{:S(2)}, u32[]{:S(2)}) %collective-permute-start.47) | collective-permute-done | bytes 36896 | tf_op jit(solution)/shard_map/ppermute | solution.py:439
  196.1 3.0 %collective-permute-done.36 = bf16[2,6,48,768]{3,2,1,0:T(8,128)(2,1)S(1)} collective-permute-done((bf16[2,6,48,768]{3,2,1,0:T(8,128)(2,1)S(1)}, bf16[2,6,48,768]{3,2,1,0:T(8,128)(2,1)S(1)}, u32[]{:S(2)}, u32[]{:S(2)}) %collective-permute-start.36) | collective-permute-done | bytes 884768 | tf_op jit(solution)/shard_map/ppermute | solution.py:540
  201.8 5.4 %collective-permute-done.48 = f32[9216]{0:T(1024)S(1)} collective-permute-done((f32[9216]{0:T(1024)S(1)}, f32[9216]{0:T(1024)S(1)}, u32[]{:S(2)}, u32[]{:S(2)}) %collective-permute-start.48) | collective-permute-done | bytes 36896 | tf_op jit(solution)/shard_map/ppermute | solution.py:439
  208.6 2.3 %collective-permute-done.51 = bf16[6,48,768]{2,1,0:T(8,128)(2,1)S(1)} collective-permute-done((bf16[6,48,768]{2,1,0:T(8,128)(2,1)S(1)}, bf16[6,48,768]{2,1,0:T(8,128)(2,1)S(1)}, u32[]{:S(2)}, u32[]{:S(2)}) %collective-permute-start.51) | collective-permute-done | bytes 442400 | tf_op jit(solution)/shard_map/ppermute | solution.py:551
  211.6 3.7 %collective-permute-done.49 = f32[9216]{0:T(1024)S(1)} collective-permute-done((f32[9216]{0:T(1024)S(1)}, f32[9216]{0:T(1024)S(1)}, u32[]{:S(2)}, u32[]{:S(2)}) %collective-permute-start.49) | collective-permute-done | bytes 36896 | tf_op jit(solution)/shard_map/ppermute | solution.py:439
  (245 shorter events, 56.6 us)
Async XLA Ops:
  5.5 12.7 %collective-permute-start.1 = (bf16[6,48,768]{2,1,0:T(8,128)(2,1)S(1)}, bf16[6,48,768]{2,1,0:T(8,128)(2,1)S(1)}, u32[]{:S(2)}, u32[]{:S(2)}) collective-permute-start(bf16[6,48,768]{2,1,0:T(8,128)(2,1)S(1)} %pad_maximum_fusion.refs_9_), channel_id=1, source_target_pairs={{0,2},{2,4},{4,6},{6,22},{22,20},{20,18},{18,16},{16,0},{8,10},{10... | collective-permute-start | bytes 1327112 | tf_op jit(solution)/shard_map/ppermute | solution.py:462
  8.4 12.1 %collective-permute-start.2 = (bf16[6,48,768]{2,1,0:T(8,128)(2,1)S(1)}, bf16[6,48,768]{2,1,0:T(8,128)(2,1)S(1)}, u32[]{:S(2)}, u32[]{:S(2)}) collective-permute-start(bf16[6,48,768]{2,1,0:T(8,128)(2,1)S(1)} %pad_maximum_fusion.refs_9_), channel_id=1, source_target_pairs={{0,16},{2,0},{4,2},{6,4},{22,6},{20,22},{18,20},{16,18},{8,24},{10... | collective-permute-start | bytes 1327112 | tf_op jit(solution)/shard_map/ppermute | solution.py:462
  8.4 12.0 %collective-permute-start.3 = (bf16[6,48,768]{2,1,0:T(8,128)(2,1)S(1)}, bf16[6,48,768]{2,1,0:T(8,128)(2,1)S(1)}, u32[]{:S(2)}, u32[]{:S(2)}) collective-permute-start(bf16[6,48,768]{2,1,0:T(8,128)(2,1)S(1)} %pad_maximum_fusion.refs_9_), channel_id=1, source_target_pairs={{0,1},{1,0},{2,3},{3,2},{4,5},{5,4},{6,7},{7,6},{8,9},{9,8},{10,11... | collective-permute-start | bytes 1327112 | tf_op jit(solution)/shard_map/ppermute | solution.py:464
  20.6 14.8 %collective-permute-start.7 = (bf16[6,48,768]{2,1,0:T(8,128)(2,1)S(1)}, bf16[6,48,768]{2,1,0:T(8,128)(2,1)S(1)}, u32[]{:S(2)}, u32[]{:S(2)}) collective-permute-start(bf16[6,48,768]{2,1,0:T(8,128)(2,1)S(1)} %pad_maximum_fusion.refs_9_), channel_id=1, source_target_pairs={{0,8},{2,10},{4,12},{6,14},{22,30},{20,28},{18,26},{16,24},{8,0},{... | collective-permute-start | bytes 1327112 | tf_op jit(solution)/shard_map/ppermute | solution.py:463
  20.9 14.6 %collective-permute-start.5 = (bf16[6,48,768]{2,1,0:T(8,128)(2,1)S(1)}, bf16[6,48,768]{2,1,0:T(8,128)(2,1)S(1)}, u32[]{:S(2)}, u32[]{:S(2)}) collective-permute-start(bf16[6,48,768]{2,1,0:T(8,128)(2,1)S(1)} %collective-permute-done.1), channel_id=1, source_target_pairs={{0,2},{2,4},{4,6},{6,22},{22,20},{20,18},{18,16},{16,0},{8,10},{10... | collective-permute-start | bytes 1327112 | tf_op jit(solution)/shard_map/ppermute | solution.py:469
  22.6 12.8 %collective-permute-start.6 = (bf16[6,48,768]{2,1,0:T(8,128)(2,1)S(1)}, bf16[6,48,768]{2,1,0:T(8,128)(2,1)S(1)}, u32[]{:S(2)}, u32[]{:S(2)}) collective-permute-start(bf16[6,48,768]{2,1,0:T(8,128)(2,1)S(1)} %collective-permute-done.2), channel_id=1, source_target_pairs={{0,16},{2,0},{4,2},{6,4},{22,6},{20,22},{18,20},{16,18},{8,24},{10... | collective-permute-start | bytes 1327112 | tf_op jit(solution)/shard_map/ppermute | solution.py:469
  23.0 12.4 %collective-permute-start.9 = (f32[9216]{0:T(1024)S(1)}, f32[9216]{0:T(1024)S(1)}, u32[]{:S(2)}, u32[]{:S(2)}) collective-permute-start(f32[9216]{0:T(1024)S(1)} %add.154), channel_id=1, source_target_pairs={{0,2},{1,3},{2,0},{3,1},{4,6},{5,7},{6,4},{7,5},{8,10},{9,11},{10,... | collective-permute-start | bytes 110600 | tf_op jit(solution)/shard_map/ppermute | solution.py:439
  35.5 15.9 %collective-permute-start.12 = (bf16[12,48,768]{2,1,0:T(8,128)(2,1)S(1)}, bf16[12,48,768]{2,1,0:T(8,128)(2,1)S(1)}, u32[]{:S(2)}, u32[]{:S(2)}) collective-permute-start(bf16[12,48,768]{2,1,0:T(8,128)(2,1)S(1)} %constant_dynamic-update-slice_fusion.2.refs_8_), channel_id=1, source_target_pairs={{0,8},{2,10},{4,12},{6,14},{22,30},{20,28},{18,26},{16,24},{8,0},{... | collective-permute-start | bytes 2654216 | tf_op jit(solution)/shard_map/ppermute | solution.py:470
  42.6 13.2 %collective-permute-start.15 = (bf16[12,48,768]{2,1,0:T(8,128)(2,1)S(1)}, bf16[12,48,768]{2,1,0:T(8,128)(2,1)S(1)}, u32[]{:S(2)}, u32[]{:S(2)}) collective-permute-start(bf16[12,48,768]{2,1,0:T(8,128)(2,1)S(1)} %constant_dynamic-update-slice_fusion.4.refs_7_), channel_id=1, source_target_pairs={{0,1},{1,0},{2,3},{3,2},{4,5},{5,4},{6,7},{7,6},{8,9},{9,8},{10,11... | collective-permute-start | bytes 2654216 | tf_op jit(solution)/shard_map/ppermute | solution.py:483
  43.0 12.8 %collective-permute-start.11 = (bf16[6,48,768]{2,1,0:T(8,128)(2,1)S(1)}, bf16[6,48,768]{2,1,0:T(8,128)(2,1)S(1)}, u32[]{:S(2)}, u32[]{:S(2)}) collective-permute-start(bf16[6,48,768]{2,1,0:T(8,128)(2,1)S(1)} %collective-permute-done.6), channel_id=1, source_target_pairs={{0,16},{2,0},{4,2},{6,4},{22,6},{20,22},{18,20},{16,18},{8,24},{10... | collective-permute-start | bytes 1327112 | tf_op jit(solution)/shard_map/ppermute | solution.py:477
  56.7 16.1 %collective-permute-start.19 = (bf16[12,48,768]{2,1,0:T(8,128)(2,1)S(1)}, bf16[12,48,768]{2,1,0:T(8,128)(2,1)S(1)}, u32[]{:S(2)}, u32[]{:S(2)}) collective-permute-start(bf16[12,48,768]{2,1,0:T(8,128)(2,1)S(1)} %constant_dynamic-update-slice_fusion.4.refs_7_), channel_id=1, source_target_pairs={{0,8},{2,10},{4,12},{6,14},{22,30},{20,28},{18,26},{16,24},{8,0},{... | collective-permute-start | bytes 2654216 | tf_op jit(solution)/shard_map/ppermute | solution.py:478
  58.3 12.3 %collective-permute-start.21 = (f32[9216]{0:T(1024)S(1)}, f32[9216]{0:T(1024)S(1)}, u32[]{:S(2)}, u32[]{:S(2)}) collective-permute-start(f32[9216]{0:T(1024)S(1)} %add.156), channel_id=1, source_target_pairs={{0,8},{8,0},{16,24},{24,16},{1,9},{9,1},{17,25},{25,17},{2,10},{10... | collective-permute-start | bytes 110600 | tf_op jit(solution)/shard_map/ppermute | solution.py:439
  80.1 13.1 %collective-permute-start.16 = (bf16[12,48,768]{2,1,0:T(8,128)(2,1)S(1)}, bf16[12,48,768]{2,1,0:T(8,128)(2,1)S(1)}, u32[]{:S(2)}, u32[]{:S(2)}) collective-permute-start(bf16[12,48,768]{2,1,0:T(8,128)(2,1)S(1)} %constant_dynamic-update-slice_fusion.6.refs_6_), channel_id=1, source_target_pairs={{0,8},{2,10},{4,12},{6,14},{22,30},{20,28},{18,26},{16,24},{8,0},{... | collective-permute-start | bytes 2654216 | tf_op jit(solution)/shard_map/ppermute | solution.py:488
  83.9 14.0 %collective-permute-start.26 = (bf16[6,48,768]{2,1,0:T(8,128)(2,1)S(1)}, bf16[6,48,768]{2,1,0:T(8,128)(2,1)S(1)}, u32[]{:S(2)}, u32[]{:S(2)}) collective-permute-start(bf16[6,48,768]{2,1,0:T(8,128)(2,1)S(1)} %constant_dynamic-update-slice_fusion.8.refs_5_), channel_id=1, source_target_pairs={{0,8},{2,10},{4,12},{6,14},{22,30},{20,28},{18,26},{16,24},{8,0},{... | collective-permute-start | bytes 1327112 | tf_op jit(solution)/shard_map/ppermute | solution.py:497
  144.1 14.7 %collective-permute-start.34 = (bf16[2,2,6,48,768]{4,3,2,1,0:T(8,128)(2,1)}, bf16[2,2,6,48,768]{4,3,2,1,0:T(8,128)(2,1)S(1)}, u32[]{:S(2)}, u32[]{:S(2)}) collective-permute-start(bf16[2,2,6,48,768]{4,3,2,1,0:T(8,128)(2,1)} %get-tuple-element.142), channel_id=1, source_target_pairs={{0,1},{1,0},{2,3},{3,2},{4,5},{5,4},{6,7},{7,6},{8,9},{9,8},{10,11... | collective-permute-start | bytes 5308424 | tf_op jit(solution)/shard_map/ppermute | solution.py:516
  150.8 19.9 %collective-permute-start.38 = (bf16[2,6,48,768]{3,2,1,0:T(8,128)(2,1)S(1)}, bf16[2,6,48,768]{3,2,1,0:T(8,128)(2,1)S(1)}, u32[]{:S(2)}, u32[]{:S(2)}) collective-permute-start(bf16[2,6,48,768]{3,2,1,0:T(8,128)(2,1)S(1)} %fusion.1), channel_id=1, source_target_pairs={{0,8},{2,10},{4,12},{6,14},{22,30},{20,28},{18,26},{16,24},{8,0},{... | collective-permute-start | bytes 2654216 | tf_op jit(solution)/shard_map/ppermute | solution.py:525
  159.1 11.6 %collective-permute-start.39 = (bf16[3,48,768]{2,1,0:T(8,128)(2,1)S(1)}, bf16[3,48,768]{2,1,0:T(8,128)(2,1)S(1)}, u32[]{:S(2)}, u32[]{:S(2)}) collective-permute-start(bf16[3,48,768]{2,1,0:T(8,128)(2,1)S(1)} %get-tuple-element.189), channel_id=1, source_target_pairs={{0,2},{2,4},{4,6},{6,22},{22,20},{20,18},{18,16},{16,0},{8,10},{10... | collective-permute-start | bytes 663560 | tf_op jit(solution)/shard_map/ppermute | solution.py:531
  161.4 23.5 %collective-permute-start.37 = (bf16[2,6,48,768]{3,2,1,0:T(8,128)(2,1)S(1)}, bf16[2,6,48,768]{3,2,1,0:T(8,128)(2,1)S(1)}, u32[]{:S(2)}, u32[]{:S(2)}) collective-permute-start(bf16[2,6,48,768]{3,2,1,0:T(8,128)(2,1)S(1)} %fusion.3), channel_id=1, source_target_pairs={{0,8},{2,10},{4,12},{6,14},{22,30},{20,28},{18,26},{16,24},{8,0},{... | collective-permute-start | bytes 2654216 | tf_op jit(solution)/shard_map/ppermute | solution.py:532
  171.1 13.2 %collective-permute-start.42 = (bf16[6,48,768]{2,1,0:T(8,128)(2,1)S(1)}, bf16[6,48,768]{2,1,0:T(8,128)(2,1)S(1)}, u32[]{:S(2)}, u32[]{:S(2)}) collective-permute-start(bf16[6,48,768]{2,1,0:T(8,128)(2,1)S(1)} %get-tuple-element.177), channel_id=1, source_target_pairs={{0,2},{2,4},{4,6},{6,22},{22,20},{20,18},{18,16},{16,0},{8,10},{10... | collective-permute-start | bytes 1327112 | tf_op jit(solution)/shard_map/ppermute | solution.py:538
  171.2 13.1 %collective-permute-start.43 = (bf16[6,48,768]{2,1,0:T(8,128)(2,1)S(1)}, bf16[6,48,768]{2,1,0:T(8,128)(2,1)S(1)}, u32[]{:S(2)}, u32[]{:S(2)}) collective-permute-start(bf16[6,48,768]{2,1,0:T(8,128)(2,1)S(1)} %get-tuple-element.176), channel_id=1, source_target_pairs={{0,16},{2,0},{4,2},{6,4},{22,6},{20,22},{18,20},{16,18},{8,24},{10... | collective-permute-start | bytes 1327112 | tf_op jit(solution)/shard_map/ppermute | solution.py:539
  173.5 25.6 %collective-permute-start.36 = (bf16[2,6,48,768]{3,2,1,0:T(8,128)(2,1)S(1)}, bf16[2,6,48,768]{3,2,1,0:T(8,128)(2,1)S(1)}, u32[]{:S(2)}, u32[]{:S(2)}) collective-permute-start(bf16[2,6,48,768]{3,2,1,0:T(8,128)(2,1)S(1)} %fusion.5), channel_id=1, source_target_pairs={{0,8},{2,10},{4,12},{6,14},{22,30},{20,28},{18,26},{16,24},{8,0},{... | collective-permute-start | bytes 2654216 | tf_op jit(solution)/shard_map/ppermute | solution.py:540
  185.4 13.7 %collective-permute-start.45 = (bf16[6,48,768]{2,1,0:T(8,128)(2,1)S(1)}, bf16[6,48,768]{2,1,0:T(8,128)(2,1)S(1)}, u32[]{:S(2)}, u32[]{:S(2)}) collective-permute-start(bf16[6,48,768]{2,1,0:T(8,128)(2,1)S(1)} %get-tuple-element.175), channel_id=1, source_target_pairs={{0,2},{2,4},{4,6},{6,22},{22,20},{20,18},{18,16},{16,0},{8,10},{10... | collective-permute-start | bytes 1327112 | tf_op jit(solution)/shard_map/ppermute | solution.py:544
  185.5 13.6 %collective-permute-start.46 = (bf16[6,48,768]{2,1,0:T(8,128)(2,1)S(1)}, bf16[6,48,768]{2,1,0:T(8,128)(2,1)S(1)}, u32[]{:S(2)}, u32[]{:S(2)}) collective-permute-start(bf16[6,48,768]{2,1,0:T(8,128)(2,1)S(1)} %get-tuple-element.174), channel_id=1, source_target_pairs={{0,16},{2,0},{4,2},{6,4},{22,6},{20,22},{18,20},{16,18},{8,24},{10... | collective-permute-start | bytes 1327112 | tf_op jit(solution)/shard_map/ppermute | solution.py:545
  187.6 19.5 %collective-permute-start.31 = (bf16[1,6,48,768]{3,2,1,0:T(8,128)(2,1)S(1)}, bf16[1,6,48,768]{3,2,1,0:T(8,128)(2,1)S(1)}, u32[]{:S(2)}, u32[]{:S(2)}) collective-permute-start(bf16[1,6,48,768]{3,2,1,0:T(8,128)(2,1)S(1)} %fusion.25), channel_id=1, source_target_pairs={{0,8},{2,10},{4,12},{6,14},{22,30},{20,28},{18,26},{16,24},{8,0},{... | collective-permute-start | bytes 1327112 | tf_op jit(solution)/shard_map/ppermute | solution.py:546
  (68 other events, 645.4 us)

commit v3 on v2

--- a/solution.py
+++ b/solution.py
@@ -23,6 +23,7 @@
 
 CYCLE = [(0, 0), (0, 1), (0, 2), (0, 3), (1, 3), (1, 2), (1, 1), (1, 0)]
 OFFSETS = (4, 3, -3, 2, -2, 1, -1, 0)
+PIECE = 19
 BATCHES = ((4,), (3, -3), (2, -2), (1, -1), (0,))
 
 
@@ -75,6 +76,8 @@
     return lax.dot_general(a, b, dims, preferred_element_type=F32)
 
 
+SMALL_ROWS = (1, 1, 2, 1, 1, 1, 4, 1)
+PART = 24
 SMALL = dict(g1=0, s1=1, qb=2, vb=3, ob=4, g2=5, s2=6, fb=7, pb=11)
 
 def compute(len_ref, tok_ref, cot_ref, sm_ref, act_ref, tg_ref, sg_ref, scr, loaders, ready, emit):
@@ -151,8 +154,8 @@
     def forward(b):
         base = b * rows
         rs = slice(base, base + rows)
+        ready("qo")
         forward_norm(acc[...], rs, small("g1"), small("s1"), a_all, xh1_all, rs1_all)
-        ready("qo")
         mix_all[0, rs, :] = (dot(a_all[rs, :], wide(0), NN) + small("qb")).astype(BF16)
         mix_all[1, rs, :] = dot(a_all[rs, :], wide(1), NN).astype(BF16)
         mix_all[2, rs, :] = (dot(a_all[rs, :], wide(2), NN) + small("vb")).astype(BF16)
@@ -269,12 +272,12 @@
 
 
 def kernel(fast, n_in, n_out, *refs):
-    tab, len_ref, tok_ref, cot_ref, sm_ref = refs[:5]
+    tab, len_ref, tok_ref, cot_ref, sm_in = refs[:5]
     w_in = refs[5:n_in]
     act_ref, tg_ref, sg_ref = refs[n_in:n_in + 3]
     d_out = refs[n_in + 3:n_in + n_out]
     scr = refs[n_in + n_out:n_in + n_out + N_SCR]
-    wqf, wp, load_sem, store_sem = refs[n_in + n_out + N_SCR:]
+    wqo, wf, wp, sm_ref, load_sem, store_sem = refs[n_in + n_out + N_SCR:]
     width = tok_ref.shape[1]
     high = wp.shape[1]
     per = width // high
@@ -283,26 +286,36 @@
     def chip_of(kind, who, slot, flip):
         return tab[0, ((kind * 2 + who) * 8 + slot) * 2 + flip]
 
-    whole = {"qo": (wqf.at[0:4], 0), "f": (wqf.at[4:8], 1), "p": (wp, 2)}
+    whole = {"qo": (wqo, 0), "f": (wf, 1), "p": (wp, 2)}
 
     def pull(src, dst, part):
         pltpu.make_async_copy(src, dst, load_sem.at[whole[part][1]]).start()
 
-    if fast:
+    def pieces():
         for who in range(2):
             c = core if who == 0 else 1 - core
             for flip in range(2):
                 for i, offs in enumerate(BATCHES):
                     src = w_in[(who * 2 + flip) * len(BATCHES) + i]
                     for j, off in enumerate(offs):
-                        chip = chip_of(0, who, OFFSETS.index(off), flip)
-                        pull(src.at[6 * j:6 * j + 2], wqf.at[pl.ds(2 * c, 2), chip], "qo")
-                        pull(src.at[6 * j + 2:6 * j + 4], wqf.at[pl.ds(4 + 2 * c, 2), chip], "f")
-                        pull(src.at[6 * j + 4:6 * j + 6], wp.at[pl.ds(4 * chip + 2 * c, 2)], "p")
+                        yield c, chip_of(0, who, OFFSETS.index(off), flip), src, PIECE * j
+
+    if fast:
+        for c, chip, src, k in pieces():
+            pull(src.at[k:k + 7], wqo.at[c, chip], "qo")
+        for c, chip, src, k in pieces():
+            pull(src.at[k + 7:k + 13], wf.at[c, chip], "f")
+        for c, chip, src, k in pieces():
+            pull(src.at[k + 13:k + 19], wp.at[pl.ds(12 * chip + 6 * c, 6)], "p")
     else:
-        pull(w_in[0].at[0:4], wqf.at[0:4], "qo")
-        pull(w_in[0].at[4:8], wqf.at[4:8], "f")
+        for c in range(2):
+            for h in range(2):
+                src = w_in[0].at[2 * c + h].reshape(16, 3, high, width)
+                pull(src, wqo.at[c, :, 1 + 3 * h:4 + 3 * h], "qo")
+                src = w_in[0].at[4 + 2 * c + h].reshape(16, 3, high, width)
+                pull(src, wf.at[c, :, 3 * h:3 * h + 3], "f")
         pull(w_in[1], wp, "p")
+        sm_ref[...] = sm_in[...]
 
     arrived = set()
 
@@ -310,10 +323,57 @@
         if part not in arrived:
             arrived.add(part)
             ref, s = whole[part]
-            pltpu.make_async_copy(ref, ref, load_sem.at[s]).wait()
+            if part == "qo" and not fast:
+                for c in range(2):
+                    pltpu.make_async_copy(wqo.at[c, :, 1:7], wqo.at[c, :, 1:7], load_sem.at[s]).wait()
+            else:
+                pltpu.make_async_copy(ref, ref, load_sem.at[s]).wait()
+            if part == "qo" and fast:
+                unpack_small()
+
+    def one_hot(v, size):
+        return (lax.broadcasted_iota(jnp.int32, (size, width), 0) == sm_in[v:v + 1, :]).astype(BF16)
+
+    def owned(v):
+        return lax.broadcasted_iota(jnp.int32, (32, width), 0) == sm_in[12 + v:13 + v, :]
+
+    def first_rows():
+        line = lax.broadcasted_iota(jnp.int32, (32, 32 * high), 0)
+        return (lax.broadcasted_iota(jnp.int32, (32, 32 * high), 1) == high * line).astype(BF16)
+
+    lanes = 384
+
+    def small_parts():
+        base, v = 0, 0
+        for rows in SMALL_ROWS:
+            for _ in range(rows):
+                yield v, base, rows * PART
+                v += 1
+            base += rows * PART
+
+    def unpack_small():
+        tiles = wqo[:, :, 0].reshape(32 * high, width)
+        packed = dot(first_rows(), tiles[:, :lanes], NN).astype(BF16)
+        for v, base, size in small_parts():
+            full = jnp.where(owned(v), dot(packed[:, base:base + size], one_hot(v, size), NN), 0.0)
+            sm_ref[:, v * width:(v + 1) * width] = jnp.sum(full, axis=0, keepdims=True)
+
+    def pack_small():
+        packed = jnp.zeros((32, lanes), F32)
+        for v, base, size in small_parts():
+            mine = jnp.where(owned(v), sg_ref[:, v * width:(v + 1) * width], 0.0).astype(BF16)
+            part = dot(mine, one_hot(v, size), NT).astype(BF16)
+            shift = lax.broadcasted_iota(jnp.int32, (size, lanes), 1) - lax.broadcasted_iota(jnp.int32, (size, lanes), 0)
+            packed += dot(part, (shift == base).astype(BF16), NN)
+        tiles = dot(first_rows(), packed.astype(BF16), TN).astype(BF16)
+        wqo[:, :, 0, :, :lanes] = tiles.reshape(2, 16, high, lanes)
+
+    def view(k):
+        c, h = k % 4 // 2, k % 2
+        return wqo.at[c, :, 1 + 3 * h:4 + 3 * h] if k < 4 else wf.at[c, :, 3 * h:3 * h + 3]
 
     def load_qf(k):
-        return wqf[k].reshape(width, width)
+        return view(k)[...].reshape(width, width)
 
     def load_p(i):
         return wp[pl.ds(i * per, per)].reshape(width, width)
@@ -328,7 +388,8 @@
         half = width // 2
         for r in range(2):
             value = dot(left[:, r * half:(r + 1) * half], right[...], TN).astype(BF16)
-            out[r * (per // 2):(r + 1) * (per // 2)] = value.reshape(per // 2, high, width)
+            tiles = out.shape[0] // 2
+            out[r * tiles:(r + 1) * tiles] = value.reshape((tiles,) + out.shape[1:])
 
     def keep_refs(slot, flip):
         for i, offs in enumerate(BATCHES):
@@ -336,52 +397,55 @@
                 at = offs.index(OFFSETS[slot])
                 return d_out[3 * i + flip].at[at], d_out[3 * i + 2].at[flip, at]
 
+    def half_stored(c, who, slot, flip, dst):
+        @pl.when(core == (c if who == 0 else 1 - c))
+        def _():
+            push(wqo.at[c, chip_of(1, who, slot, flip)], dst.at[0:7], 2)
+
+    def targets():
+        for slot in range(8):
+            for flip in range(2):
+                for who, dst in enumerate(keep_refs(slot, flip)):
+                    yield core if who == 0 else 1 - core, chip_of(1, who, slot, flip), dst
+
     def emit(a_all, att_all, c_all, ga_all, dmix_all, gb_all, dpre_all, gd_all):
         for i in range(4):
             product(ga_all.at[i], gd_all, wp.at[i * per:(i + 1) * per])
         if fast:
-            for slot in range(8):
-                for flip in range(2):
-                    kept, sent = keep_refs(slot, flip)
-                    for who, dst in ((0, kept), (1, sent)):
-                        c = core if who == 0 else 1 - core
-                        push(wp.at[pl.ds(4 * chip_of(1, who, slot, flip) + 2 * c, 2)], dst.at[4:6], 1)
+            for c, chip, dst in targets():
+                push(wp.at[pl.ds(12 * chip + 6 * c, 6)], dst.at[13:19], 0)
         else:
-            push(wp, d_out[1], 1)
-
-        for part, first in ((1, 4), (0, 0)):
-            for half in range(2):
-                k = first + 2 * half
-                for h in range(2):
-                    if part == 1:
-                        product(c_all, dpre_all.at[2 * half + h], wqf.at[k + h])
-                    elif k + h < 3:
-                        product(a_all, dmix_all.at[k + h], wqf.at[k + h])
-                    else:
-                        product(att_all, gb_all, wqf.at[k + h])
-                if not fast:
-                    push(wqf.at[k:k + 2], d_out[0].at[k:k + 2], 0)
-                    continue
+            push(wp, d_out[1], 0)
+        for i in range(4):
+            product(c_all, dpre_all.at[i], view(4 + i))
+        if fast:
+            for c, chip, dst in targets():
+                push(wf.at[c, chip], dst.at[7:13], 1)
+            pack_small()
+        product(att_all, gb_all, view(3))
+        for i in (2, 0, 1):
+            product(a_all, dmix_all.at[i], view(i))
+            if fast and i != 0:
                 for slot in range(8):
                     for flip in range(2):
-                        kept, sent = keep_refs(slot, flip)
-
-                        @pl.when(core == half)
-                        def _():
-                            push(wqf.at[k:k + 2, chip_of(1, 0, slot, flip)], kept.at[2 * part:2 * part + 2], 0)
-
-                        @pl.when(core != half)
-                        def _():
-                            push(wqf.at[k:k + 2, chip_of(1, 1, slot, flip)], sent.at[2 * part:2 * part + 2], 0)
-        drain(wqf, 0)
-        drain(wp, 1)
+                        for who, dst in enumerate(keep_refs(slot, flip)):
+                            half_stored(1 if i == 2 else 0, who, slot, flip, dst)
+        if fast:
+            drain(wqo, 2)
+        else:
+            for k in range(8):
+                push(view(k), d_out[0].at[k].reshape(16, 3, high, width), 1 if k >= 4 else 2)
+            for c in range(2):
+                drain(wqo.at[c, :, 1:7], 2)
+        drain(wf, 1)
+        drain(wp, 0)
 
     compute(len_ref, tok_ref, cot_ref, sm_ref, act_ref, tg_ref, sg_ref, scr, (load_qf, load_p), ready, emit)
 
 
 def run_kernel(fast, table, lengths, tokens, cotangent, smalls, w_in, d_shapes):
     rows, width = tokens.shape
-    high = 48
+    high = 16
     per = width // high
     n_in = 5 + len(w_in)
     smem = pl.BlockSpec(memory_space=pltpu.SMEM)
@@ -398,10 +462,12 @@
         in_specs=[smem, smem, vmem, vmem, vmem] + [hbm] * len(w_in),
         out_specs=[vmem, vmem, vmem] + [hbm] * len(d_shapes),
         scratch_shapes=compute_scratch(rows, width) + [
-            pltpu.VMEM((8, per, high, width), BF16),
+            pltpu.VMEM((2, 16, 7, high, width), BF16),
+            pltpu.VMEM((2, 16, 6, high, width), BF16),
             pltpu.VMEM((4 * per, high, width), BF16),
+            pltpu.VMEM((1, 12 * width), F32),
             pltpu.SemaphoreType.DMA((3,)),
-            pltpu.SemaphoreType.DMA((2,)),
+            pltpu.SemaphoreType.DMA((3,)),
         ],
         compiler_params=pltpu.CompilerParams(vmem_limit_bytes=LIMIT),
         cost_estimate=pl.CostEstimate(flops=22_000_000_000, bytes_accessed=32_000_000, transcendentals=4_000_000),
@@ -454,58 +520,29 @@
     return tuple(functools.partial(lax.ppermute, axis_name=AXES, perm=p) for p in (cw, ccw, swap, pair))
 
 
-def gather_pieces(piece, packed, steps):
+def gather_pieces(piece):
     cw, ccw, swap, pair = both_ways()
     stage = lax.optimization_barrier
     half = piece.shape[0] // 2
 
-    right, left = cw(piece), ccw(piece)
-    s0 = swap(piece)
-    c0 = pair(piece)
-    packed = add_swapped(packed, steps[0])
-    right, left, c0, packed = stage((right, left, c0, packed))
-
+    right, left, s0, c0 = stage((cw(piece), ccw(piece), swap(piece), pair(piece)))
     p1 = jnp.concatenate([right, left])
-    right, left = cw(right), ccw(left)
-    s1 = swap(p1)
-    c1 = pair(p1)
-    c1, packed = stage((c1, packed))
-    packed = add_swapped(packed, steps[1])
-    right, left, s0, c1, packed = stage((right, left, s0, c1, packed))
-
+    s1, c1, cs0 = swap(p1), pair(p1), pair(s0)
+    right, left, c1, cs0 = stage((cw(right), ccw(left), c1, cs0))
     p2 = jnp.concatenate([right, left])
-    right, left = cw(right), ccw(left)
-    s2 = swap(p2)
-    cs0 = pair(s0)
-    cs0, packed = stage((cs0, packed))
-    packed = add_swapped(packed, steps[2])
-    packed, p2 = stage((packed, p2))
-    c2 = pair(p2)
-    right, left, s1, c2, cs0, packed = stage((right, left, s1, c2, cs0, packed))
-
+    s2, c2 = swap(p2), pair(p2)
+    right, left, c2, s1 = stage((cw(right), ccw(left), c2, s1))
     p3 = jnp.concatenate([right, left])
-    right, left = cw(right[:half]), ccw(left[half:])
-    s3 = swap(p3)
-    cs1 = pair(s1)
-    cs1, packed = stage((cs1, packed))
-    packed = add_swapped(packed, steps[3])
-    packed, p3 = stage((packed, p3))
-    c3 = pair(p3)
-    right, left, s2, c3, cs1, packed = stage((right, left, s2, c3, cs1, packed))
-
+    s3, c3, cs1 = swap(p3), pair(p3), pair(s1)
+    right, left, c3, cs1, s2 = stage((cw(right[:half]), ccw(left[half:]), c3, cs1, s2))
     p4 = jnp.concatenate([right, left])
-    s4 = swap(p4)
-    cs2 = pair(s2)
-    c4 = pair(p4)
-    cs2, c4, packed = stage((cs2, c4, packed))
-    packed = add_swapped(packed, steps[4])
-    s3, packed, cs2, c4 = stage((s3, packed, cs2, c4))
-    cs3 = pair(s3)
-    cs4 = pair(s4)
-    return [p4, p3, p2, p1, piece, s4, s3, s2, s1, s0, c4, c3, c2, c1, c0, cs4, cs3, cs2, cs1, cs0], packed
-
-
-def scatter_sums(outs, packed, steps):
+    s4, c4, cs2 = swap(p4), pair(p4), pair(s2)
+    s3, s4, c4, cs2 = stage((s3, s4, c4, cs2))
+    cs3, cs4 = pair(s3), pair(s4)
+    return [p4, p3, p2, p1, piece, s4, s3, s2, s1, s0, c4, c3, c2, c1, c0, cs4, cs3, cs2, cs1, cs0]
+
+
+def scatter_sums(outs):
     cw, ccw, swap, pair = both_ways()
     stage = lax.optimization_barrier
 
@@ -530,29 +567,22 @@
     half = first.shape[0] // 2
     right, left = cw(first[:half]), ccw(first[half:])
     moved[2] = swap(add(flipped[2], got[2][1]))
-    got[4], packed = stage((got[4], packed))
-    packed = add_swapped(packed, steps[0])
-    zero = jnp.zeros_like(right)
-    moved[1], right, left, packed = stage((moved[1], right, left, packed))
+    moved[1], right, left = stage((moved[1], right, left))
     second = total(1)
-    right = cw((second[0] + jnp.concatenate([right, zero]).astype(F32)).astype(BF16))
-    left = ccw((second[1] + jnp.concatenate([zero, left]).astype(F32)).astype(BF16))
+    right, left = jnp.concatenate([right, jnp.zeros_like(left)]), jnp.concatenate([jnp.zeros_like(right), left])
+    right = cw((second[0] + right.astype(F32)).astype(BF16))
+    left = ccw((second[1] + left.astype(F32)).astype(BF16))
     moved[3] = swap(add(flipped[3], got[3][1]))
-    packed = add_swapped(packed, steps[1])
-    moved[2], right, left, packed = stage((moved[2], right, left, packed))
+    moved[2], right, left = stage((moved[2], right, left))
     third = total(2)
     right = cw((third[0] + right.astype(F32)).astype(BF16))
     left = ccw((third[1] + left.astype(F32)).astype(BF16))
     moved[4] = swap(add(flipped[4], got[4][1]))
-    packed = add_swapped(packed, steps[2])
-    moved[3], right, left, packed = stage((moved[3], right, left, packed))
+    moved[3], right, left = stage((moved[3], right, left))
     fourth = total(3)
     right = cw((fourth[0] + right.astype(F32)).astype(BF16))
     left = ccw((fourth[1] + left.astype(F32)).astype(BF16))
-    packed = add_swapped(packed, steps[3])
-    moved[4], packed = stage((moved[4], packed))
-    packed = add_swapped(packed, steps[4])
-    return total(4)[0] + right.astype(F32) + left.astype(F32), packed
+    return total(4)[0] + right.astype(F32) + left.astype(F32)
 
 
 def body(sizes, tokens, lengths, ln1_gain, ln1_shift, w_qkv, qv_bias, w_out, out_bias, ln2_gain, ln2_shift,
@@ -564,7 +594,6 @@
     fast = (dp, fsdp) == (4, 8)
     vectors = (ln1_gain, ln1_shift, qv_bias, out_bias, ln2_gain, ln2_shift, fc_bias, proj_bias)
     steps = swap_steps((("fsdp", fsdp), ("dp", dp)))
-    packed = spread(vectors, count, me)
     part = w_qkv.shape[0]
     wide = jnp.stack([
         w_qkv[:, :width], w_qkv[:, width:2 * width], w_qkv[:, 2 * width:], w_out,
@@ -581,34 +610,41 @@
         theirs = jnp.where(core == 0, halves[:, 1], halves[:, 0])
         other = lax.ppermute(theirs, AXES, core_pairs())
         both = jnp.where(core == 0, jnp.concatenate([mine, other], 2), jnp.concatenate([other, mine], 2))
-        piece = jnp.concatenate([both.reshape(4, 2 * part, width), proj.reshape(2, 2 * part, width)])
-        pieces, packed = gather_pieces(piece, packed, steps)
+        row = jnp.concatenate(vectors).astype(BF16)
+        row = jnp.pad(row[None, None, :], ((0, 0), (0, 15), (0, width - row.shape[0])))
+        piece = jnp.concatenate([row, both.reshape(12, 16, width), proj.reshape(6, 16, width)])
+        pieces = gather_pieces(piece)
         shape = piece.shape
         d_shapes = []
         for offs in BATCHES:
             k = len(offs)
             d_shapes += [(k,) + shape, (k,) + shape, (2, k) + shape]
-        act, tgrad, small_sums, *outs = run_kernel(True, table, *flat, packed.reshape(1, -1), pieces, d_shapes)
-        total, small_sums = scatter_sums(outs, small_sums.reshape(-1), steps)
-        high = total[:4, :part], total[:4, part:]
+        act, tgrad, _, *outs = run_kernel(True, table, *flat, small_spots(), pieces, d_shapes)
+        total = scatter_sums(outs)
+        square = total[1:13].reshape(4, 2 * part, width)
+        high = square[:, :part], square[:, part:]
         own = jnp.where(core == 0, high[0], high[1])
         got = lax.ppermute(jnp.where(core == 0, high[1], high[0]), AXES, core_pairs())
         own, got = own.reshape(2, 2, part, width), got.reshape(2, 2, part, width)
         blocks = jnp.where(core == 0, jnp.concatenate([own, got], 1), jnp.concatenate([got, own], 1))
         blocks = blocks.reshape(8, part, width)
-        d_proj = total[4:].reshape(w_proj.shape)
+        d_proj = total[13:].reshape(w_proj.shape)
+        small, base = [], 0
+        for v in vectors:
+            small.append(total[0, 0, base:base + v.shape[0]])
+            base += v.shape[0]
     else:
         table = jnp.zeros((1, 65), jnp.int32)
         w_all = lax.all_gather(wide, AXES, axis=1, tiled=True)
-        p_all = lax.all_gather(proj, AXES, axis=0, tiled=True).reshape(-1, 48, width)
+        p_all = lax.all_gather(proj, AXES, axis=0, tiled=True).reshape(-1, 16, width)
+        packed = spread(vectors, count, me)
         blocks_all = w_all.reshape((8, -1) + p_all.shape[1:])
         act, tgrad, small_sums, d_wide, d_p = run_kernel(
             False, table, *flat, total_small(packed, steps).reshape(1, -1), [blocks_all, p_all],
             [blocks_all.shape, p_all.shape])
         blocks = lax.psum_scatter(d_wide.reshape(w_all.shape), AXES, scatter_dimension=1, tiled=True).astype(F32)
         d_proj = lax.psum_scatter(d_p.reshape(-1, width), AXES, scatter_dimension=0, tiled=True).astype(F32)
-        small_sums = total_small(small_sums.reshape(-1), steps)
-    small = own_parts(small_sums, [v.shape[0] for v in vectors], count, me)
+        small = own_parts(total_small(small_sums.reshape(-1), steps), [v.shape[0] for v in vectors], count, me)
     g1, s1, qv, ob, g2, s2, fb, pb = small
     d_qkv = jnp.concatenate([blocks[0], blocks[1], blocks[2]], axis=1)
     d_fc = jnp.concatenate([blocks[4], blocks[5], blocks[6], blocks[7]], axis=1)
@@ -633,6 +669,16 @@
 TABLE = make_table()
 
 
+def small_spots():
+    spots, owners = [], []
+    for rows in SMALL_ROWS:
+        size = rows * PART
+        for r in range(rows):
+            spots.append([(r * 768 + col) % size for col in range(768)])
+            owners.append([(r * 768 + col) // size % 2 * 16 + (r * 768 + col) // size // 2 for col in range(768)])
+    return jnp.array(spots + owners, jnp.int32)
+
+
 def solution(mesh):
     both = P(AXES)
     rows = P(None, AXES, None)

time: 223 us -> 200 us (0.90)
  the two profiles are of different devices: /device:TPU:0 before, /device:TPU:17 now
where the time goes in v3:
time: 200 us; the launch traced here: 197 us
  waiting for transfers between devices  88.7 us (44%)
  starting transfers between devices  49 us (24%)
  Pallas kernels  43 us (22%)
  other arithmetic  8.77 us (4%)
  local copies, waits for them, and re-layouts  6.05 us (3%)
    pallas_call x1, Pallas kernels, run_kernel(): pl.pallas_call(functools.partial(kernel, fast, n_in, len(out_shape)), out...  43 us
    ppermute x2, waiting for transfers between devices, gather_pieces(): right, left, c1, cs0 = stage((cw(right), ccw(left), c1, cs0))  10.9 us
    ppermute x2, waiting for transfers between devices, gather_pieces(): right, left, c2, s1 = stage((cw(right), ccw(left), c2, s1))  10.2 us
    ppermute x1, waiting for transfers between devices, scatter_sums(): left = ccw((third[1] + left.astype(F32)).astype(BF16))  9.41 us
    ppermute x1, waiting for transfers between devices, scatter_sums(): right = cw((fourth[0] + right.astype(F32)).astype(BF16))  8.91 us
    ppermute x1, waiting for transfers between devices, scatter_sums(): left = ccw((second[1] + left.astype(F32)).astype(BF16))  7.06 us
    ppermute x1, starting transfers between devices, scatter_sums(): right = cw((second[0] + right.astype(F32)).astype(BF16))  5.98 us
    ppermute x1, waiting for transfers between devices, scatter_sums(): moved[0] = swap(add(flipped[0], got[0][1]))  5.92 us
  transfers between devices with their start and end apart: 43, of which 19 were waited for; matrix products, arithmetic and copies ran while one was open for 4% of the time, Pallas kernels for 0%

profile of v3, /device:TPU:17, one launch (start us, length us, event | category | flops | bytes accessed | tf_op | source)
XLA Modules:
  0.0 197.1 jit_solution(12697531670831165001)
XLA Ops:
  8.8 5.0 %collective-permute-done.3.refs_14_ = bf16[19,16,768]{2,1,0:T(8,128)(2,1)S(1)} collective-permute-done((bf16[19,16,768]{2,1,0:T(8,128)(2,1)S(1)}, bf16[19,16,768]{2,1,0:T(8,128)(2,1)S(1)}, u32[]{:S(2)}, u32[]{:S(2)}) %collective-permute-start.3) | collective-permute-done | bytes 466976 | tf_op jit(solution)/shard_map/ppermute | solution.py:528
  13.8 5.4 %collective-permute-done.2 = bf16[19,16,768]{2,1,0:T(8,128)(2,1)S(1)} collective-permute-done((bf16[19,16,768]{2,1,0:T(8,128)(2,1)S(1)}, bf16[19,16,768]{2,1,0:T(8,128)(2,1)S(1)}, u32[]{:S(2)}, u32[]{:S(2)}) %collective-permute-start.2) | collective-permute-done | bytes 466976 | tf_op jit(solution)/shard_map/ppermute | solution.py:528
  23.1 9.9 %collective-permute-done.5 = bf16[19,16,768]{2,1,0:T(8,128)(2,1)S(1)} collective-permute-done((bf16[19,16,768]{2,1,0:T(8,128)(2,1)S(1)}, bf16[19,16,768]{2,1,0:T(8,128)(2,1)S(1)}, u32[]{:S(2)}, u32[]{:S(2)}) %collective-permute-start.5) | collective-permute-done | bytes 466976 | tf_op jit(solution)/shard_map/ppermute | solution.py:531
  36.8 10.2 %collective-permute-done.9 = bf16[19,16,768]{2,1,0:T(8,128)(2,1)S(1)} collective-permute-done((bf16[19,16,768]{2,1,0:T(8,128)(2,1)S(1)}, bf16[19,16,768]{2,1,0:T(8,128)(2,1)S(1)}, u32[]{:S(2)}, u32[]{:S(2)}) %collective-permute-start.9) | collective-permute-done | bytes 466976 | tf_op jit(solution)/shard_map/ppermute | solution.py:534
  47.1 1.7 collective-permute-start.15
  51.5 5.3 %collective-permute-done.13 = bf16[9,16,768]{2,1,0:T(8,128)(2,1)S(1)} collective-permute-done((bf16[9,16,768]{2,1,0:T(8,128)(2,1)S(1)}, bf16[9,16,768]{2,1,0:T(8,128)(2,1)S(1)}, u32[]{:S(2)}, u32[]{:S(2)}) %collective-permute-start.13) | collective-permute-done | bytes 221216 | tf_op jit(solution)/shard_map/ppermute | solution.py:537
  56.8 1.7 collective-permute-start.21
  58.7 4.8 %collective-permute-done.18.refs_11_ = bf16[38,16,768]{2,1,0:T(8,128)(2,1)S(1)} collective-permute-done((bf16[38,16,768]{2,1,0:T(8,128)(2,1)S(1)}, bf16[38,16,768]{2,1,0:T(8,128)(2,1)S(1)}, u32[]{:S(2)}, u32[]{:S(2)}) %collective-permute-start.18) | collective-permute-done | bytes 933920 | tf_op jit(solution)/shard_map/ppermute | solution.py:536
  63.5 5.0 %collective-permute-done.19.refs_10_ = bf16[19,16,768]{2,1,0:T(8,128)(2,1)S(1)} collective-permute-done((bf16[19,16,768]{2,1,0:T(8,128)(2,1)S(1)}, bf16[19,16,768]{2,1,0:T(8,128)(2,1)S(1)}, u32[]{:S(2)}, u32[]{:S(2)}) %collective-permute-start.19) | collective-permute-done | bytes 466976 | tf_op jit(solution)/shard_map/ppermute | solution.py:539
  68.5 2.3 %collective-permute-start.23 = (bf16[38,16,768]{2,1,0:T(8,128)(2,1)S(1)}, bf16[38,16,768]{2,1,0:T(8,128)(2,1)S(1)}, u32[]{:S(2)}, u32[]{:S(2)}) collective-permute-start(bf16[38,16,768]{2,1,0:T(8,128)(2,1)S(1)} %collective-permute-done.18.refs_11_), channel_id=1, source_target_pairs={{0,1},{1,0},{2,3},{3,2},{4,5},{5,4},{6,7},{7,6},{8,9},{9,8},{10,11... | collective-permute-start | bytes 2801672 | tf_op jit(solution)/shard_map/ppermute | solution.py:541
  74.7 43.0 %blocks.1 = (bf16[256,768]{1,0:T(8,128)(2,1)}, bf16[256,768]{1,0:T(8,128)(2,1)}, f32[1,9216]{1,0:T(1,128)}, bf16[1,19,16,768]{3,2,1,0:T(8,128)(2,1)}, bf16[1,19,...) custom-call(s32[1,65]{1,0:T(1,128)} %constant_dynamic-slice_fusion.r, ...), custom_call_target="tpu_custom_call" | custom-call | flops 22000001024 | bytes 32000000 | tf_op jit(solution)/shard_map/blocks/pallas_call | solution.py:459
  118.6 1.9 collective-permute-done.27
  123.8 5.9 %collective-permute-done.28 = bf16[1,19,16,768]{3,2,1,0:T(8,128)(2,1)S(1)} collective-permute-done((bf16[1,19,16,768]{3,2,1,0:T(8,128)(2,1)S(1)}, bf16[1,19,16,768]{3,2,1,0:T(8,128)(2,1)S(1)}, u32[]{:S(2)}, u32[]{:S(2)}) %collective-permute-start.28) | collective-permute-done | bytes 466976 | tf_op jit(solution)/shard_map/ppermute | solution.py:559
  130.0 5.7 %collective-permute-start.34 = (bf16[9,16,768]{2,1,0:T(8,128)(2,1)S(1)}, bf16[9,16,768]{2,1,0:T(8,128)(2,1)S(1)}, u32[]{:S(2)}, u32[]{:S(2)}) collective-permute-start(bf16[9,16,768]{2,1,0:T(8,128)(2,1)S(1)} %slice_bitcast_fusion.11), channel_id=1, source_target_pairs={{0,2},{2,4},{4,6},{6,22},{22,20},{20,18},{18,16},{16,0},{8,10},{10... | collective-permute-start | bytes 663560 | tf_op jit(solution)/shard_map/ppermute | solution.py:568
  137.3 2.4 %collective-permute-done.33 = bf16[2,19,16,768]{3,2,1,0:T(8,128)(2,1)S(1)} collective-permute-done((bf16[2,19,16,768]{3,2,1,0:T(8,128)(2,1)S(1)}, bf16[2,19,16,768]{3,2,1,0:T(8,128)(2,1)S(1)}, u32[]{:S(2)}, u32[]{:S(2)}) %collective-permute-start.33) | collective-permute-done | bytes 933920 | tf_op jit(solution)/shard_map/ppermute | solution.py:562
  139.8 2.1 %collective-permute-done.35 = bf16[10,16,768]{2,1,0:T(8,128)(2,1)S(1)} collective-permute-done((bf16[10,16,768]{2,1,0:T(8,128)(2,1)S(1)}, bf16[10,16,768]{2,1,0:T(8,128)(2,1)S(1)}, u32[]{:S(2)}, u32[]{:S(2)}) %collective-permute-start.35) | collective-permute-done | bytes 245792 | tf_op jit(solution)/shard_map/ppermute | solution.py:568
  142.8 6.0 %collective-permute-start.36 = (bf16[19,16,768]{2,1,0:T(8,128)(2,1)S(1)}, bf16[19,16,768]{2,1,0:T(8,128)(2,1)S(1)}, u32[]{:S(2)}, u32[]{:S(2)}) collective-permute-start(bf16[19,16,768]{2,1,0:T(8,128)(2,1)S(1)} %get-tuple-element.127), channel_id=1, source_target_pairs={{0,2},{2,4},{4,6},{6,22},{22,20},{20,18},{18,16},{16,0},{8,10},{10... | collective-permute-start | bytes 1400840 | tf_op jit(solution)/shard_map/ppermute | solution.py:573
  151.6 7.1 %collective-permute-done.37 = bf16[19,16,768]{2,1,0:T(8,128)(2,1)S(1)} collective-permute-done((bf16[19,16,768]{2,1,0:T(8,128)(2,1)S(1)}, bf16[19,16,768]{2,1,0:T(8,128)(2,1)S(1)}, u32[]{:S(2)}, u32[]{:S(2)}) %collective-permute-start.37) | collective-permute-done | bytes 466976 | tf_op jit(solution)/shard_map/ppermute | solution.py:574
  159.3 4.4 %collective-permute-start.38 = (bf16[19,16,768]{2,1,0:T(8,128)(2,1)S(1)}, bf16[19,16,768]{2,1,0:T(8,128)(2,1)S(1)}, u32[]{:S(2)}, u32[]{:S(2)}) collective-permute-start(bf16[19,16,768]{2,1,0:T(8,128)(2,1)S(1)} %get-tuple-element.125), channel_id=1, source_target_pairs={{0,2},{2,4},{4,6},{6,22},{22,20},{20,18},{18,16},{16,0},{8,10},{10... | collective-permute-start | bytes 1400840 | tf_op jit(solution)/shard_map/ppermute | solution.py:578
  164.3 9.4 %collective-permute-done.39 = bf16[19,16,768]{2,1,0:T(8,128)(2,1)S(1)} collective-permute-done((bf16[19,16,768]{2,1,0:T(8,128)(2,1)S(1)}, bf16[19,16,768]{2,1,0:T(8,128)(2,1)S(1)}, u32[]{:S(2)}, u32[]{:S(2)}) %collective-permute-start.39) | collective-permute-done | bytes 466976 | tf_op jit(solution)/shard_map/ppermute | solution.py:579
  174.3 4.4 %collective-permute-start.40 = (bf16[19,16,768]{2,1,0:T(8,128)(2,1)S(1)}, bf16[19,16,768]{2,1,0:T(8,128)(2,1)S(1)}, u32[]{:S(2)}, u32[]{:S(2)}) collective-permute-start(bf16[19,16,768]{2,1,0:T(8,128)(2,1)S(1)} %get-tuple-element.122), channel_id=1, source_target_pairs={{0,2},{2,4},{4,6},{6,22},{22,20},{20,18},{18,16},{16,0},{8,10},{10... | collective-permute-start | bytes 1400840 | tf_op jit(solution)/shard_map/ppermute | solution.py:583
  178.7 8.9 %collective-permute-done.40 = bf16[19,16,768]{2,1,0:T(8,128)(2,1)S(1)} collective-permute-done((bf16[19,16,768]{2,1,0:T(8,128)(2,1)S(1)}, bf16[19,16,768]{2,1,0:T(8,128)(2,1)S(1)}, u32[]{:S(2)}, u32[]{:S(2)}) %collective-permute-start.40) | collective-permute-done | bytes 466976 | tf_op jit(solution)/shard_map/ppermute | solution.py:583
  187.7 1.9 collective-permute-done.41
  190.5 2.3 %collective-permute-start.42 = (f32[4,24,768]{2,1,0:T(8,128)S(1)}, f32[4,24,768]{2,1,0:T(8,128)S(1)}, u32[]{:S(2)}, u32[]{:S(2)}) collective-permute-start(f32[4,24,768]{2,1,0:T(8,128)S(1)} %get-tuple-element.143), channel_id=1, source_target_pairs={{0,1},{1,0},{2,3},{3,2},{4,5},{5,4},{6,7},{7,6},{8,9},{9,8},{10,11... | collective-permute-start | bytes 884744 | tf_op jit(solution)/shard_map/ppermute | solution.py:627
  (193 shorter events, 38.9 us)
Async XLA Ops:
  7.3 11.9 %collective-permute-start.2 = (bf16[19,16,768]{2,1,0:T(8,128)(2,1)S(1)}, bf16[19,16,768]{2,1,0:T(8,128)(2,1)S(1)}, u32[]{:S(2)}, u32[]{:S(2)}) collective-permute-start(bf16[19,16,768]{2,1,0:T(8,128)(2,1)S(1)} %fusion.28.refs_9_), channel_id=1, source_target_pairs={{0,16},{2,0},{4,2},{6,4},{22,6},{20,22},{18,20},{16,18},{8,24},{10... | collective-permute-start | bytes 1400840 | tf_op jit(solution)/shard_map/ppermute | solution.py:528
  7.5 11.7 %collective-permute-start.1 = (bf16[19,16,768]{2,1,0:T(8,128)(2,1)S(1)}, bf16[19,16,768]{2,1,0:T(8,128)(2,1)S(1)}, u32[]{:S(2)}, u32[]{:S(2)}) collective-permute-start(bf16[19,16,768]{2,1,0:T(8,128)(2,1)S(1)} %fusion.28.refs_9_), channel_id=1, source_target_pairs={{0,2},{2,4},{4,6},{6,22},{22,20},{20,18},{18,16},{16,0},{8,10},{10... | collective-permute-start | bytes 1400840 | tf_op jit(solution)/shard_map/ppermute | solution.py:528
  19.3 14.7 %collective-permute-start.7 = (bf16[38,16,768]{2,1,0:T(8,128)(2,1)S(1)}, bf16[38,16,768]{2,1,0:T(8,128)(2,1)}, u32[]{:S(2)}, u32[]{:S(2)}) collective-permute-start(bf16[38,16,768]{2,1,0:T(8,128)(2,1)S(1)} %constant_dynamic-update-slice_fusion.refs_8_), channel_id=1, source_target_pairs={{0,1},{1,0},{2,3},{3,2},{4,5},{5,4},{6,7},{7,6},{8,9},{9,8},{10,11... | collective-permute-start | bytes 2801672 | tf_op jit(solution)/shard_map/ppermute | solution.py:530
  20.8 12.2 %collective-permute-start.5 = (bf16[19,16,768]{2,1,0:T(8,128)(2,1)S(1)}, bf16[19,16,768]{2,1,0:T(8,128)(2,1)S(1)}, u32[]{:S(2)}, u32[]{:S(2)}) collective-permute-start(bf16[19,16,768]{2,1,0:T(8,128)(2,1)S(1)} %collective-permute-done.1), channel_id=1, source_target_pairs={{0,2},{2,4},{4,6},{6,22},{22,20},{20,18},{18,16},{16,0},{8,10},{10... | collective-permute-start | bytes 1400840 | tf_op jit(solution)/shard_map/ppermute | solution.py:531
  22.1 11.9 %collective-permute-start.6 = (bf16[19,16,768]{2,1,0:T(8,128)(2,1)S(1)}, bf16[19,16,768]{2,1,0:T(8,128)(2,1)S(1)}, u32[]{:S(2)}, u32[]{:S(2)}) collective-permute-start(bf16[19,16,768]{2,1,0:T(8,128)(2,1)S(1)} %collective-permute-done.2), channel_id=1, source_target_pairs={{0,16},{2,0},{4,2},{6,4},{22,6},{20,22},{18,20},{16,18},{8,24},{10... | collective-permute-start | bytes 1400840 | tf_op jit(solution)/shard_map/ppermute | solution.py:531
  22.2 11.8 %collective-permute-start.8 = (bf16[19,16,768]{2,1,0:T(8,128)(2,1)S(1)}, bf16[19,16,768]{2,1,0:T(8,128)(2,1)S(1)}, u32[]{:S(2)}, u32[]{:S(2)}) collective-permute-start(bf16[19,16,768]{2,1,0:T(8,128)(2,1)S(1)} %collective-permute-done.3.refs_14_), channel_id=1, source_target_pairs={{0,1},{1,0},{2,3},{3,2},{4,5},{5,4},{6,7},{7,6},{8,9},{9,8},{10,11... | collective-permute-start | bytes 1400840 | tf_op jit(solution)/shard_map/ppermute | solution.py:530
  22.9 14.0 %collective-permute-start.12 = (bf16[38,16,768]{2,1,0:T(8,128)(2,1)S(1)}, bf16[38,16,768]{2,1,0:T(8,128)(2,1)S(1)}, u32[]{:S(2)}, u32[]{:S(2)}) collective-permute-start(bf16[38,16,768]{2,1,0:T(8,128)(2,1)S(1)} %constant_dynamic-update-slice_fusion.refs_8_), channel_id=1, source_target_pairs={{0,8},{2,10},{4,12},{6,14},{22,30},{20,28},{18,26},{16,24},{8,0},{... | collective-permute-start | bytes 2801672 | tf_op jit(solution)/shard_map/ppermute | solution.py:530
  34.1 12.9 %collective-permute-start.11 = (bf16[38,16,768]{2,1,0:T(8,128)(2,1)S(1)}, bf16[38,16,768]{2,1,0:T(8,128)(2,1)}, u32[]{:S(2)}, u32[]{:S(2)}) collective-permute-start(bf16[38,16,768]{2,1,0:T(8,128)(2,1)S(1)} %constant_dynamic-update-slice_fusion.2.refs_7_), channel_id=1, source_target_pairs={{0,1},{1,0},{2,3},{3,2},{4,5},{5,4},{6,7},{7,6},{8,9},{9,8},{10,11... | collective-permute-start | bytes 2801672 | tf_op jit(solution)/shard_map/ppermute | solution.py:533
  35.4 11.7 %collective-permute-start.9 = (bf16[19,16,768]{2,1,0:T(8,128)(2,1)S(1)}, bf16[19,16,768]{2,1,0:T(8,128)(2,1)S(1)}, u32[]{:S(2)}, u32[]{:S(2)}) collective-permute-start(bf16[19,16,768]{2,1,0:T(8,128)(2,1)S(1)} %collective-permute-done.5), channel_id=1, source_target_pairs={{0,2},{2,4},{4,6},{6,22},{22,20},{20,18},{18,16},{16,0},{8,10},{10... | collective-permute-start | bytes 1400840 | tf_op jit(solution)/shard_map/ppermute | solution.py:534
  35.4 11.6 %collective-permute-start.10 = (bf16[19,16,768]{2,1,0:T(8,128)(2,1)S(1)}, bf16[19,16,768]{2,1,0:T(8,128)(2,1)S(1)}, u32[]{:S(2)}, u32[]{:S(2)}) collective-permute-start(bf16[19,16,768]{2,1,0:T(8,128)(2,1)S(1)} %collective-permute-done.6), channel_id=1, source_target_pairs={{0,16},{2,0},{4,2},{6,4},{22,6},{20,22},{18,20},{16,18},{8,24},{10... | collective-permute-start | bytes 1400840 | tf_op jit(solution)/shard_map/ppermute | solution.py:534
  36.8 13.9 %collective-permute-start.17 = (bf16[38,16,768]{2,1,0:T(8,128)(2,1)S(1)}, bf16[38,16,768]{2,1,0:T(8,128)(2,1)S(1)}, u32[]{:S(2)}, u32[]{:S(2)}) collective-permute-start(bf16[38,16,768]{2,1,0:T(8,128)(2,1)S(1)} %constant_dynamic-update-slice_fusion.2.refs_7_), channel_id=1, source_target_pairs={{0,8},{2,10},{4,12},{6,14},{22,30},{20,28},{18,26},{16,24},{8,0},{... | collective-permute-start | bytes 2801672 | tf_op jit(solution)/shard_map/ppermute | solution.py:533
  50.8 12.7 %collective-permute-start.18 = (bf16[38,16,768]{2,1,0:T(8,128)(2,1)S(1)}, bf16[38,16,768]{2,1,0:T(8,128)(2,1)S(1)}, u32[]{:S(2)}, u32[]{:S(2)}) collective-permute-start(bf16[38,16,768]{2,1,0:T(8,128)(2,1)S(1)} %constant_dynamic-update-slice_fusion.4.refs_6_), channel_id=1, source_target_pairs={{0,8},{2,10},{4,12},{6,14},{22,30},{20,28},{18,26},{16,24},{8,0},{... | collective-permute-start | bytes 2801672 | tf_op jit(solution)/shard_map/ppermute | solution.py:536
  56.8 11.7 %collective-permute-start.21 = (bf16[38,16,768]{2,1,0:T(8,128)(2,1)S(1)}, bf16[38,16,768]{2,1,0:T(8,128)(2,1)S(1)}, u32[]{:S(2)}, u32[]{:S(2)}) collective-permute-start(bf16[38,16,768]{2,1,0:T(8,128)(2,1)S(1)} %collective-permute-done.17.refs_12_), channel_id=1, source_target_pairs={{0,1},{1,0},{2,3},{3,2},{4,5},{5,4},{6,7},{7,6},{8,9},{9,8},{10,11... | collective-permute-start | bytes 2801672 | tf_op jit(solution)/shard_map/ppermute | solution.py:539
  118.3 11.5 %collective-permute-start.29 = (bf16[2,2,19,16,768]{4,3,2,1,0:T(8,128)(2,1)}, bf16[2,2,19,16,768]{4,3,2,1,0:T(8,128)(2,1)S(1)}, u32[]{:S(2)}, u32[]{:S(2)}) collective-permute-start(bf16[2,2,19,16,768]{4,3,2,1,0:T(8,128)(2,1)} %get-tuple-element.99), channel_id=1, source_target_pairs={{0,1},{1,0},{2,3},{3,2},{4,5},{5,4},{6,7},{7,6},{8,9},{9,8},{10,11... | collective-permute-start | bytes 5603336 | tf_op jit(solution)/shard_map/ppermute | solution.py:553
  123.4 16.4 %collective-permute-start.33 = (bf16[2,19,16,768]{3,2,1,0:T(8,128)(2,1)S(1)}, bf16[2,19,16,768]{3,2,1,0:T(8,128)(2,1)S(1)}, u32[]{:S(2)}, u32[]{:S(2)}) collective-permute-start(bf16[2,19,16,768]{3,2,1,0:T(8,128)(2,1)S(1)} %fusion), channel_id=1, source_target_pairs={{0,8},{2,10},{4,12},{6,14},{22,30},{20,28},{18,26},{16,24},{8,0},{... | collective-permute-start | bytes 2801672 | tf_op jit(solution)/shard_map/ppermute | solution.py:562
  136.0 22.6 %collective-permute-start.32 = (bf16[2,19,16,768]{3,2,1,0:T(8,128)(2,1)S(1)}, bf16[2,19,16,768]{3,2,1,0:T(8,128)(2,1)S(1)}, u32[]{:S(2)}, u32[]{:S(2)}) collective-permute-start(bf16[2,19,16,768]{3,2,1,0:T(8,128)(2,1)S(1)} %fusion.2), channel_id=1, source_target_pairs={{0,8},{2,10},{4,12},{6,14},{22,30},{20,28},{18,26},{16,24},{8,0},{... | collective-permute-start | bytes 2801672 | tf_op jit(solution)/shard_map/ppermute | solution.py:569
  142.4 16.2 %collective-permute-start.37 = (bf16[19,16,768]{2,1,0:T(8,128)(2,1)S(1)}, bf16[19,16,768]{2,1,0:T(8,128)(2,1)S(1)}, u32[]{:S(2)}, u32[]{:S(2)}) collective-permute-start(bf16[19,16,768]{2,1,0:T(8,128)(2,1)S(1)} %get-tuple-element.126), channel_id=1, source_target_pairs={{0,16},{2,0},{4,2},{6,4},{22,6},{20,22},{18,20},{16,18},{8,24},{10... | collective-permute-start | bytes 1400840 | tf_op jit(solution)/shard_map/ppermute | solution.py:574
  142.8 15.9 %collective-permute-start.36 = (bf16[19,16,768]{2,1,0:T(8,128)(2,1)S(1)}, bf16[19,16,768]{2,1,0:T(8,128)(2,1)S(1)}, u32[]{:S(2)}, u32[]{:S(2)}) collective-permute-start(bf16[19,16,768]{2,1,0:T(8,128)(2,1)S(1)} %get-tuple-element.127), channel_id=1, source_target_pairs={{0,2},{2,4},{4,6},{6,22},{22,20},{20,18},{18,16},{16,0},{8,10},{10... | collective-permute-start | bytes 1400840 | tf_op jit(solution)/shard_map/ppermute | solution.py:573
  148.7 15.1 %collective-permute-start.25 = (bf16[2,1,19,16,768]{4,3,2,1,0:T(8,128)(2,1)S(1)}, bf16[2,1,19,16,768]{4,3,2,1,0:T(8,128)(2,1)S(1)}, u32[]{:S(2)}, u32[]{:S(2)}) collective-permute-start(bf16[2,1,19,16,768]{4,3,2,1,0:T(8,128)(2,1)S(1)} %copy-done.21), channel_id=1, source_target_pairs={{0,1},{1,0},{2,3},{3,2},{4,5},{5,4},{6,7},{7,6},{8,9},{9,8},{10,11... | collective-permute-start | bytes 2801672 | tf_op jit(solution)/shard_map/ppermute | solution.py:564
  150.3 14.0 %collective-permute-start.31 = (bf16[2,19,16,768]{3,2,1,0:T(8,128)(2,1)S(1)}, bf16[2,19,16,768]{3,2,1,0:T(8,128)(2,1)S(1)}, u32[]{:S(2)}, u32[]{:S(2)}) collective-permute-start(bf16[2,19,16,768]{3,2,1,0:T(8,128)(2,1)S(1)} %fusion.4), channel_id=1, source_target_pairs={{0,8},{2,10},{4,12},{6,14},{22,30},{20,28},{18,26},{16,24},{8,0},{... | collective-permute-start | bytes 2801672 | tf_op jit(solution)/shard_map/ppermute | solution.py:575
  159.3 14.4 %collective-permute-start.39 = (bf16[19,16,768]{2,1,0:T(8,128)(2,1)S(1)}, bf16[19,16,768]{2,1,0:T(8,128)(2,1)S(1)}, u32[]{:S(2)}, u32[]{:S(2)}) collective-permute-start(bf16[19,16,768]{2,1,0:T(8,128)(2,1)S(1)} %get-tuple-element.124), channel_id=1, source_target_pairs={{0,16},{2,0},{4,2},{6,4},{22,6},{20,22},{18,20},{16,18},{8,24},{10... | collective-permute-start | bytes 1400840 | tf_op jit(solution)/shard_map/ppermute | solution.py:579
  159.3 14.4 %collective-permute-start.38 = (bf16[19,16,768]{2,1,0:T(8,128)(2,1)S(1)}, bf16[19,16,768]{2,1,0:T(8,128)(2,1)S(1)}, u32[]{:S(2)}, u32[]{:S(2)}) collective-permute-start(bf16[19,16,768]{2,1,0:T(8,128)(2,1)S(1)} %get-tuple-element.125), channel_id=1, source_target_pairs={{0,2},{2,4},{4,6},{6,22},{22,20},{20,18},{18,16},{16,0},{8,10},{10... | collective-permute-start | bytes 1400840 | tf_op jit(solution)/shard_map/ppermute | solution.py:578
  163.9 14.8 %collective-permute-start.26 = (bf16[1,19,16,768]{3,2,1,0:T(8,128)(2,1)S(1)}, bf16[1,19,16,768]{3,2,1,0:T(8,128)(2,1)S(1)}, u32[]{:S(2)}, u32[]{:S(2)}) collective-permute-start(bf16[1,19,16,768]{3,2,1,0:T(8,128)(2,1)S(1)} %fusion.21), channel_id=1, source_target_pairs={{0,8},{2,10},{4,12},{6,14},{22,30},{20,28},{18,26},{16,24},{8,0},{... | collective-permute-start | bytes 1400840 | tf_op jit(solution)/shard_map/ppermute | solution.py:580
  174.3 13.3 %collective-permute-start.40 = (bf16[19,16,768]{2,1,0:T(8,128)(2,1)S(1)}, bf16[19,16,768]{2,1,0:T(8,128)(2,1)S(1)}, u32[]{:S(2)}, u32[]{:S(2)}) collective-permute-start(bf16[19,16,768]{2,1,0:T(8,128)(2,1)S(1)} %get-tuple-element.122), channel_id=1, source_target_pairs={{0,2},{2,4},{4,6},{6,22},{22,20},{20,18},{18,16},{16,0},{8,10},{10... | collective-permute-start | bytes 1400840 | tf_op jit(solution)/shard_map/ppermute | solution.py:583
  (56 other events, 483.6 us)

commit v4 on v3

--- a/solution.py
+++ b/solution.py
@@ -120,13 +120,14 @@
     def fold(v):
         return jnp.sum(v.reshape(v.shape[0] // 8, 8, v.shape[1]), axis=0)
 
-    def forward_norm(v, rs, gain, shift, dst, xh_all, rs_all):
+    def forward_norm(v, rs, names, dst, xh_all, rs_all):
         cen = v - jnp.mean(v, axis=-1, keepdims=True)
         rstd = lax.rsqrt(jnp.mean(cen * cen, axis=-1, keepdims=True) + EPS)
         xhat = cen * rstd
         xh_all[rs, :] = xhat
         rs_all[rs, :] = jnp.broadcast_to(rstd, (rows, 128))
-        dst[rs, :] = (xhat * gain + shift).astype(BF16)
+        ready("qo")
+        dst[rs, :] = (xh_all[rs, :] * small(names[0]) + small(names[1])).astype(BF16)
 
     def backward_norm(xh_all, rs_all, rs, gain, names):
         xhat = xh_all[rs, :]
@@ -154,8 +155,7 @@
     def forward(b):
         base = b * rows
         rs = slice(base, base + rows)
-        ready("qo")
-        forward_norm(acc[...], rs, small("g1"), small("s1"), a_all, xh1_all, rs1_all)
+        forward_norm(acc[...], rs, ("g1", "s1"), a_all, xh1_all, rs1_all)
         mix_all[0, rs, :] = (dot(a_all[rs, :], wide(0), NN) + small("qb")).astype(BF16)
         mix_all[1, rs, :] = dot(a_all[rs, :], wide(1), NN).astype(BF16)
         mix_all[2, rs, :] = (dot(a_all[rs, :], wide(2), NN) + small("vb")).astype(BF16)
@@ -175,7 +175,7 @@
 
         mid = acc[...] + (dot(att_all[rs, :], wide(3), NN) + small("ob"))
         acc[...] = mid + small("pb")
-        forward_norm(mid, rs, small("g2"), small("s2"), c_all, xh2_all, rs2_all)
+        forward_norm(mid, rs, ("g2", "s2"), c_all, xh2_all, rs2_all)
         ready("f")
         ready("p")
 
@@ -300,23 +300,31 @@
                     for j, off in enumerate(offs):
                         yield c, chip_of(0, who, OFFSETS.index(off), flip), src, PIECE * j
 
-    if fast:
-        for c, chip, src, k in pieces():
-            pull(src.at[k:k + 7], wqo.at[c, chip], "qo")
-        for c, chip, src, k in pieces():
-            pull(src.at[k + 7:k + 13], wf.at[c, chip], "f")
-        for c, chip, src, k in pieces():
-            pull(src.at[k + 13:k + 19], wp.at[pl.ds(12 * chip + 6 * c, 6)], "p")
-    else:
+    def pull_first():
+        if fast:
+            for c, chip, src, k in pieces():
+                pull(src.at[k:k + 7], wqo.at[c, chip], "qo")
+            return
+        sm_ref[...] = sm_in[...]
         for c in range(2):
             for h in range(2):
                 src = w_in[0].at[2 * c + h].reshape(16, 3, high, width)
                 pull(src, wqo.at[c, :, 1 + 3 * h:4 + 3 * h], "qo")
+
+    def pull_rest():
+        if fast:
+            for c, chip, src, k in pieces():
+                pull(src.at[k + 7:k + 13], wf.at[c, chip], "f")
+            for c, chip, src, k in pieces():
+                pull(src.at[k + 13:k + 19], wp.at[pl.ds(12 * chip + 6 * c, 6)], "p")
+            return
+        for c in range(2):
+            for h in range(2):
                 src = w_in[0].at[4 + 2 * c + h].reshape(16, 3, high, width)
                 pull(src, wf.at[c, :, 3 * h:3 * h + 3], "f")
         pull(w_in[1], wp, "p")
-        sm_ref[...] = sm_in[...]
-
+
+    pull_first()
     arrived = set()
 
     def ready(part):
@@ -328,8 +336,10 @@
                     pltpu.make_async_copy(wqo.at[c, :, 1:7], wqo.at[c, :, 1:7], load_sem.at[s]).wait()
             else:
                 pltpu.make_async_copy(ref, ref, load_sem.at[s]).wait()
-            if part == "qo" and fast:
-                unpack_small()
+            if part == "qo":
+                pull_rest()
+                if fast:
+                    unpack_small()
 
     def one_hot(v, size):
         return (lax.broadcasted_iota(jnp.int32, (size, width), 0) == sm_in[v:v + 1, :]).astype(BF16)
@@ -520,26 +530,49 @@
     return tuple(functools.partial(lax.ppermute, axis_name=AXES, perm=p) for p in (cw, ccw, swap, pair))
 
 
-def gather_pieces(piece):
+PLAN = (
+    ("s0", 0, 0),
+    ("s1", 1, 2),
+    ("s2", 2, 4),
+    ("s3", 3, 4),
+    ("s4", 4, 4),
+    ("c0", 1, 1),
+    ("c1", 2, 2),
+    ("c2", 4, 4),
+    ("c3", 4, 4),
+    ("c4", 4, 4),
+    ("cs0", 2, 2),
+    ("cs1", 3, 3),
+    ("cs2", 3, 4),
+    ("cs3", 4, 5),
+    ("cs4", 5, 5),
+)
+
+
+def gather_pieces(piece, table):
     cw, ccw, swap, pair = both_ways()
-    stage = lax.optimization_barrier
     half = piece.shape[0] // 2
-
-    right, left, s0, c0 = stage((cw(piece), ccw(piece), swap(piece), pair(piece)))
-    p1 = jnp.concatenate([right, left])
-    s1, c1, cs0 = swap(p1), pair(p1), pair(s0)
-    right, left, c1, cs0 = stage((cw(right), ccw(left), c1, cs0))
-    p2 = jnp.concatenate([right, left])
-    s2, c2 = swap(p2), pair(p2)
-    right, left, c2, s1 = stage((cw(right), ccw(left), c2, s1))
-    p3 = jnp.concatenate([right, left])
-    s3, c3, cs1 = swap(p3), pair(p3), pair(s1)
-    right, left, c3, cs1, s2 = stage((cw(right[:half]), ccw(left[half:]), c3, cs1, s2))
-    p4 = jnp.concatenate([right, left])
-    s4, c4, cs2 = swap(p4), pair(p4), pair(s2)
-    s3, s4, c4, cs2 = stage((s3, s4, c4, cs2))
-    cs3, cs4 = pair(s3), pair(s4)
-    return [p4, p3, p2, p1, piece, s4, s3, s2, s1, s0, c4, c3, c2, c1, c0, cs4, cs3, cs2, cs1, cs0]
+    have = {"p0": piece}
+    right = left = piece
+    for stage in range(6):
+        arrivals = {}
+        if stage < 4:
+            if stage == 3:
+                right, left = right[:half], left[half:]
+            arrivals = {"right": cw(right), "left": ccw(left)}
+        for what, first, _ in PLAN:
+            if first == stage:
+                have[what] = swap(have["p" + what[1:]]) if what[0] == "s" else pair(have[what[1:] if what[1] == "s" else "p" + what[1:]])
+        if stage == 5:
+            break
+        arrivals |= {what: have[what] for what, _, last in PLAN if last == stage}
+        if stage == 4:
+            arrivals["table"] = table
+        have |= dict(zip(arrivals, lax.optimization_barrier(tuple(arrivals.values()))))
+        if stage < 4:
+            right, left = have["right"], have["left"]
+            have[f"p{stage + 1}"] = jnp.concatenate([right, left])
+    return [have[f"{kind}{k}"] for kind in ("p", "s", "c", "cs") for k in (4, 3, 2, 1, 0)], have["table"]
 
 
 def scatter_sums(outs):
@@ -613,7 +646,7 @@
         row = jnp.concatenate(vectors).astype(BF16)
         row = jnp.pad(row[None, None, :], ((0, 0), (0, 15), (0, width - row.shape[0])))
         piece = jnp.concatenate([row, both.reshape(12, 16, width), proj.reshape(6, 16, width)])
-        pieces = gather_pieces(piece)
+        pieces, table = gather_pieces(piece, table)
         shape = piece.shape
         d_shapes = []
         for offs in BATCHES:

time: 200 us -> 195 us (0.975)
  waiting for transfers between devices: 88.7 us -> 84.3 us
    ppermute x23, waiting for transfers between devices: 47.2 us -> 40 us  [the longest x8 28.9 us: gather_pieces(): arrivals = {'right': cw(right), 'left': ccw(left)}]
    ppermute x23, starting transfers between devices: 19 us -> 23.5 us  [the longest x10 11 us: gather_pieces(): pair(have[what[1:] if what[1] == 's' else 'p' + what[1:]])]
    ppermute x1, waiting for transfers between devices: 2.41 us -> 5.65 us  [scatter_sums(): moved[1] = swap(add(flipped[1], got[1][1]))]
    ppermute x2, starting transfers between devices: 5.77 us -> 3.77 us  [scatter_sums(): right, left = (cw(first[:half]), ccw(first[half:]))]
  transfers between devices with their start and end apart: 43 -> 43, of which waited for: 19 -> 21; matrix products, arithmetic and copies ran while one was open for 4% -> 4% of each run, Pallas kernels for 0% -> 0%
where the time goes in v4:
time: 195 us; the launch traced here: 192 us
  waiting for transfers between devices  84.3 us (43%)
  starting transfers between devices  48.7 us (25%)
  Pallas kernels  42.8 us (22%)
  other arithmetic  8.77 us (4%)
  local copies, waits for them, and re-layouts  6 us (3%)
    pallas_call x1, Pallas kernels, run_kernel(): pl.pallas_call(functools.partial(kernel, fast, n_in, len(out_shape)), out...  42.8 us
    ppermute x8, waiting for transfers between devices, gather_pieces(): arrivals = {'right': cw(right), 'left': ccw(left)}  28.9 us
    ppermute x10, starting transfers between devices, gather_pieces(): pair(have[what[1:] if what[1] == 's' else 'p' + what[1:]])  11 us
    ppermute x1, waiting for transfers between devices, scatter_sums(): left = ccw((third[1] + left.astype(F32)).astype(BF16))  9.73 us
    ppermute x1, waiting for transfers between devices, scatter_sums(): right = cw((fourth[0] + right.astype(F32)).astype(BF16))  8.95 us
    ppermute x8, starting transfers between devices, gather_pieces(): arrivals = {'right': cw(right), 'left': ccw(left)}  8.85 us
    ppermute x1, waiting for transfers between devices, scatter_sums(): left = ccw((second[1] + left.astype(F32)).astype(BF16))  8.31 us
    ppermute x5, waiting for transfers between devices, gather_pieces(): swap(have['p' + what[1:]])  8.09 us
  transfers between devices with their start and end apart: 43, of which 21 were waited for; matrix products, arithmetic and copies ran while one was open for 4% of the time, Pallas kernels for 0%

profile of v4, /device:TPU:17, one launch (start us, length us, event | category | flops | bytes accessed | tf_op | source)
XLA Modules:
  0.0 192.2 jit_solution(5528735586774635348)
XLA Ops:
  9.6 3.8 %collective-permute-done.3.refs_14_ = bf16[19,16,768]{2,1,0:T(8,128)(2,1)S(1)} collective-permute-done((bf16[19,16,768]{2,1,0:T(8,128)(2,1)S(1)}, bf16[19,16,768]{2,1,0:T(8,128)(2,1)S(1)}, u32[]{:S(2)}, u32[]{:S(2)}) %collective-permute-start.3) | collective-permute-done | bytes 466976 | tf_op jit(solution)/shard_map/ppermute | solution.py:565
  13.4 5.1 %collective-permute-done.2 = bf16[19,16,768]{2,1,0:T(8,128)(2,1)S(1)} collective-permute-done((bf16[19,16,768]{2,1,0:T(8,128)(2,1)S(1)}, bf16[19,16,768]{2,1,0:T(8,128)(2,1)S(1)}, u32[]{:S(2)}, u32[]{:S(2)}) %collective-permute-start.2) | collective-permute-done | bytes 466976 | tf_op jit(solution)/shard_map/ppermute | solution.py:562
  18.6 2.0 %collective-permute-start.4 = (bf16[19,16,768]{2,1,0:T(8,128)(2,1)S(1)}, bf16[19,16,768]{2,1,0:T(8,128)(2,1)S(1)}, u32[]{:S(2)}, u32[]{:S(2)}) collective-permute-start(bf16[19,16,768]{2,1,0:T(8,128)(2,1)S(1)} %collective-permute-done.1), channel_id=1, source_target_pairs={{0,2},{2,4},{4,6},{6,22},{22,20},{20,18},{18,16},{16,0},{8,10},{10... | collective-permute-start | bytes 1400840 | tf_op jit(solution)/shard_map/ppermute | solution.py:562
  23.9 5.7 %collective-permute-done.4 = bf16[19,16,768]{2,1,0:T(8,128)(2,1)S(1)} collective-permute-done((bf16[19,16,768]{2,1,0:T(8,128)(2,1)S(1)}, bf16[19,16,768]{2,1,0:T(8,128)(2,1)S(1)}, u32[]{:S(2)}, u32[]{:S(2)}) %collective-permute-start.4) | collective-permute-done | bytes 466976 | tf_op jit(solution)/shard_map/ppermute | solution.py:562
  33.1 2.1 %collective-permute-start.7 = (bf16[38,16,768]{2,1,0:T(8,128)(2,1)S(1)}, bf16[38,16,768]{2,1,0:T(8,128)(2,1)S(1)}, u32[]{:S(2)}, u32[]{:S(2)}) collective-permute-start(bf16[38,16,768]{2,1,0:T(8,128)(2,1)S(1)} %constant_dynamic-update-slice_fusion.refs_7_), channel_id=1, source_target_pairs={{0,8},{2,10},{4,12},{6,14},{22,30},{20,28},{18,26},{16,24},{8,0},{... | collective-permute-start | bytes 2801672 | tf_op jit(solution)/shard_map/ppermute | solution.py:565
  36.9 4.6 %collective-permute-done.8 = bf16[19,16,768]{2,1,0:T(8,128)(2,1)S(1)} collective-permute-done((bf16[19,16,768]{2,1,0:T(8,128)(2,1)S(1)}, bf16[19,16,768]{2,1,0:T(8,128)(2,1)S(1)}, u32[]{:S(2)}, u32[]{:S(2)}) %collective-permute-start.8) | collective-permute-done | bytes 466976 | tf_op jit(solution)/shard_map/ppermute | solution.py:562
  41.5 2.0 %collective-permute-done.9 = bf16[19,16,768]{2,1,0:T(8,128)(2,1)S(1)} collective-permute-done((bf16[19,16,768]{2,1,0:T(8,128)(2,1)S(1)}, bf16[19,16,768]{2,1,0:T(8,128)(2,1)S(1)}, u32[]{:S(2)}, u32[]{:S(2)}) %collective-permute-start.9) | collective-permute-done | bytes 466976 | tf_op jit(solution)/shard_map/ppermute | solution.py:562
  43.5 3.8 %collective-permute-start.14 = (bf16[9,16,768]{2,1,0:T(8,128)(2,1)S(1)}, bf16[9,16,768]{2,1,0:T(8,128)(2,1)S(1)}, u32[]{:S(2)}, u32[]{:S(2)}) collective-permute-start(bf16[9,16,768]{2,1,0:T(8,128)(2,1)S(1)} %slice.171), channel_id=1, source_target_pairs={{0,2},{2,4},{4,6},{6,22},{22,20},{20,18},{18,16},{16,0},{8,10},{10... | collective-permute-start | bytes 663560 | tf_op jit(solution)/shard_map/ppermute | solution.py:562
  48.6 2.7 %collective-permute-done.14 = bf16[9,16,768]{2,1,0:T(8,128)(2,1)S(1)} collective-permute-done((bf16[9,16,768]{2,1,0:T(8,128)(2,1)S(1)}, bf16[9,16,768]{2,1,0:T(8,128)(2,1)S(1)}, u32[]{:S(2)}, u32[]{:S(2)}) %collective-permute-start.14) | collective-permute-done | bytes 221216 | tf_op jit(solution)/shard_map/ppermute | solution.py:562
  51.5 6.8 %collective-permute-done.15 = bf16[10,16,768]{2,1,0:T(8,128)(2,1)S(1)} collective-permute-done((bf16[10,16,768]{2,1,0:T(8,128)(2,1)S(1)}, bf16[10,16,768]{2,1,0:T(8,128)(2,1)S(1)}, u32[]{:S(2)}, u32[]{:S(2)}) %collective-permute-start.15) | collective-permute-done | bytes 245792 | tf_op jit(solution)/shard_map/ppermute | solution.py:562
  58.2 2.3 %collective-permute-start.19 = (bf16[38,16,768]{2,1,0:T(8,128)(2,1)S(1)}, bf16[38,16,768]{2,1,0:T(8,128)(2,1)}, u32[]{:S(2)}, u32[]{:S(2)}) collective-permute-start(bf16[38,16,768]{2,1,0:T(8,128)(2,1)S(1)} %constant_dynamic-update-slice_fusion.4.refs_6_), channel_id=1, source_target_pairs={{0,1},{1,0},{2,3},{3,2},{4,5},{5,4},{6,7},{7,6},{8,9},{9,8},{10,11... | collective-permute-start | bytes 2801672 | tf_op jit(solution)/shard_map/ppermute | solution.py:565
  64.8 4.2 %collective-permute-done.17.refs_10_ = bf16[19,16,768]{2,1,0:T(8,128)(2,1)} collective-permute-done((bf16[19,16,768]{2,1,0:T(8,128)(2,1)S(1)}, bf16[19,16,768]{2,1,0:T(8,128)(2,1)}, u32[]{:S(2)}, u32[]{:S(2)}) %collective-permute-start.17) | collective-permute-done | bytes 466976 | tf_op jit(solution)/shard_map/ppermute | solution.py:565
  71.9 42.8 %blocks.1 = (bf16[256,768]{1,0:T(8,128)(2,1)}, bf16[256,768]{1,0:T(8,128)(2,1)}, f32[1,9216]{1,0:T(1,128)}, bf16[1,19,16,768]{3,2,1,0:T(8,128)(2,1)}, bf16[1,19,...) custom-call(s32[1,65]{1,0:T(1,128)} %constant_dynamic-slice_fusion.r, ...), custom_call_target="tpu_custom_call" | custom-call | flops 22000001024 | bytes 32000000 | tf_op jit(solution)/shard_map/blocks/pallas_call | solution.py:469
  120.9 5.9 %collective-permute-done.28 = bf16[1,19,16,768]{3,2,1,0:T(8,128)(2,1)S(1)} collective-permute-done((bf16[1,19,16,768]{3,2,1,0:T(8,128)(2,1)S(1)}, bf16[1,19,16,768]{3,2,1,0:T(8,128)(2,1)S(1)}, u32[]{:S(2)}, u32[]{:S(2)}) %collective-permute-start.28) | collective-permute-done | bytes 466976 | tf_op jit(solution)/shard_map/ppermute | solution.py:592
  127.1 3.7 %collective-permute-start.34 = (bf16[9,16,768]{2,1,0:T(8,128)(2,1)S(1)}, bf16[9,16,768]{2,1,0:T(8,128)(2,1)S(1)}, u32[]{:S(2)}, u32[]{:S(2)}) collective-permute-start(bf16[9,16,768]{2,1,0:T(8,128)(2,1)S(1)} %slice_bitcast_fusion.11), channel_id=1, source_target_pairs={{0,2},{2,4},{4,6},{6,22},{22,20},{20,18},{18,16},{16,0},{8,10},{10... | collective-permute-start | bytes 663560 | tf_op jit(solution)/shard_map/ppermute | solution.py:601
  131.2 5.7 %collective-permute-done.33 = bf16[2,19,16,768]{3,2,1,0:T(8,128)(2,1)S(1)} collective-permute-done((bf16[2,19,16,768]{3,2,1,0:T(8,128)(2,1)S(1)}, bf16[2,19,16,768]{3,2,1,0:T(8,128)(2,1)S(1)}, u32[]{:S(2)}, u32[]{:S(2)}) %collective-permute-start.33) | collective-permute-done | bytes 933920 | tf_op jit(solution)/shard_map/ppermute | solution.py:595
  137.9 5.9 %collective-permute-start.36 = (bf16[19,16,768]{2,1,0:T(8,128)(2,1)S(1)}, bf16[19,16,768]{2,1,0:T(8,128)(2,1)S(1)}, u32[]{:S(2)}, u32[]{:S(2)}) collective-permute-start(bf16[19,16,768]{2,1,0:T(8,128)(2,1)S(1)} %get-tuple-element.129), channel_id=1, source_target_pairs={{0,2},{2,4},{4,6},{6,22},{22,20},{20,18},{18,16},{16,0},{8,10},{10... | collective-permute-start | bytes 1400840 | tf_op jit(solution)/shard_map/ppermute | solution.py:606
  145.5 8.3 %collective-permute-done.37 = bf16[19,16,768]{2,1,0:T(8,128)(2,1)S(1)} collective-permute-done((bf16[19,16,768]{2,1,0:T(8,128)(2,1)S(1)}, bf16[19,16,768]{2,1,0:T(8,128)(2,1)S(1)}, u32[]{:S(2)}, u32[]{:S(2)}) %collective-permute-start.37) | collective-permute-done | bytes 466976 | tf_op jit(solution)/shard_map/ppermute | solution.py:607
  154.5 4.4 %collective-permute-start.38 = (bf16[19,16,768]{2,1,0:T(8,128)(2,1)S(1)}, bf16[19,16,768]{2,1,0:T(8,128)(2,1)S(1)}, u32[]{:S(2)}, u32[]{:S(2)}) collective-permute-start(bf16[19,16,768]{2,1,0:T(8,128)(2,1)S(1)} %get-tuple-element.127), channel_id=1, source_target_pairs={{0,2},{2,4},{4,6},{6,22},{22,20},{20,18},{18,16},{16,0},{8,10},{10... | collective-permute-start | bytes 1400840 | tf_op jit(solution)/shard_map/ppermute | solution.py:611
  159.1 9.7 %collective-permute-done.39 = bf16[19,16,768]{2,1,0:T(8,128)(2,1)S(1)} collective-permute-done((bf16[19,16,768]{2,1,0:T(8,128)(2,1)S(1)}, bf16[19,16,768]{2,1,0:T(8,128)(2,1)S(1)}, u32[]{:S(2)}, u32[]{:S(2)}) %collective-permute-start.39) | collective-permute-done | bytes 466976 | tf_op jit(solution)/shard_map/ppermute | solution.py:612
  169.4 4.4 %collective-permute-start.40 = (bf16[19,16,768]{2,1,0:T(8,128)(2,1)S(1)}, bf16[19,16,768]{2,1,0:T(8,128)(2,1)S(1)}, u32[]{:S(2)}, u32[]{:S(2)}) collective-permute-start(bf16[19,16,768]{2,1,0:T(8,128)(2,1)S(1)} %get-tuple-element.124), channel_id=1, source_target_pairs={{0,2},{2,4},{4,6},{6,22},{22,20},{20,18},{18,16},{16,0},{8,10},{10... | collective-permute-start | bytes 1400840 | tf_op jit(solution)/shard_map/ppermute | solution.py:616
  173.8 9.0 %collective-permute-done.40 = bf16[19,16,768]{2,1,0:T(8,128)(2,1)S(1)} collective-permute-done((bf16[19,16,768]{2,1,0:T(8,128)(2,1)S(1)}, bf16[19,16,768]{2,1,0:T(8,128)(2,1)S(1)}, u32[]{:S(2)}, u32[]{:S(2)}) %collective-permute-start.40) | collective-permute-done | bytes 466976 | tf_op jit(solution)/shard_map/ppermute | solution.py:616
  182.8 1.9 collective-permute-done.41
  185.6 2.3 %collective-permute-start.42 = (f32[4,24,768]{2,1,0:T(8,128)S(1)}, f32[4,24,768]{2,1,0:T(8,128)S(1)}, u32[]{:S(2)}, u32[]{:S(2)}) collective-permute-start(f32[4,24,768]{2,1,0:T(8,128)S(1)} %get-tuple-element.145), channel_id=1, source_target_pairs={{0,1},{1,0},{2,3},{3,2},{4,5},{5,4},{6,7},{7,6},{8,9},{9,8},{10,11... | collective-permute-start | bytes 884744 | tf_op jit(solution)/shard_map/ppermute | solution.py:660
  (185 shorter events, 41.4 us)
Async XLA Ops:
  7.0 11.6 %collective-permute-start.2 = (bf16[19,16,768]{2,1,0:T(8,128)(2,1)S(1)}, bf16[19,16,768]{2,1,0:T(8,128)(2,1)S(1)}, u32[]{:S(2)}, u32[]{:S(2)}) collective-permute-start(bf16[19,16,768]{2,1,0:T(8,128)(2,1)S(1)} %fusion.28.refs_9_), channel_id=1, source_target_pairs={{0,16},{2,0},{4,2},{6,4},{22,6},{20,22},{18,20},{16,18},{8,24},{10... | collective-permute-start | bytes 1400840 | tf_op jit(solution)/shard_map/ppermute | solution.py:562
  7.1 11.5 %collective-permute-start.1 = (bf16[19,16,768]{2,1,0:T(8,128)(2,1)S(1)}, bf16[19,16,768]{2,1,0:T(8,128)(2,1)S(1)}, u32[]{:S(2)}, u32[]{:S(2)}) collective-permute-start(bf16[19,16,768]{2,1,0:T(8,128)(2,1)S(1)} %fusion.28.refs_9_), channel_id=1, source_target_pairs={{0,2},{2,4},{4,6},{6,22},{22,20},{20,18},{18,16},{16,0},{8,10},{10... | collective-permute-start | bytes 1400840 | tf_op jit(solution)/shard_map/ppermute | solution.py:562
  8.4 14.2 %collective-permute-start.6 = (bf16[19,16,768]{2,1,0:T(8,128)(2,1)S(1)}, bf16[19,16,768]{2,1,0:T(8,128)(2,1)S(1)}, u32[]{:S(2)}, u32[]{:S(2)}) collective-permute-start(bf16[19,16,768]{2,1,0:T(8,128)(2,1)S(1)} %fusion.28.refs_9_), channel_id=1, source_target_pairs={{0,1},{1,0},{2,3},{3,2},{4,5},{5,4},{6,7},{7,6},{8,9},{9,8},{10,11... | collective-permute-start | bytes 1400840 | tf_op jit(solution)/shard_map/ppermute | solution.py:565
  18.6 11.0 %collective-permute-start.4 = (bf16[19,16,768]{2,1,0:T(8,128)(2,1)S(1)}, bf16[19,16,768]{2,1,0:T(8,128)(2,1)S(1)}, u32[]{:S(2)}, u32[]{:S(2)}) collective-permute-start(bf16[19,16,768]{2,1,0:T(8,128)(2,1)S(1)} %collective-permute-done.1), channel_id=1, source_target_pairs={{0,2},{2,4},{4,6},{6,22},{22,20},{20,18},{18,16},{16,0},{8,10},{10... | collective-permute-start | bytes 1400840 | tf_op jit(solution)/shard_map/ppermute | solution.py:562
  20.6 10.9 %collective-permute-start.5 = (bf16[19,16,768]{2,1,0:T(8,128)(2,1)S(1)}, bf16[19,16,768]{2,1,0:T(8,128)(2,1)S(1)}, u32[]{:S(2)}, u32[]{:S(2)}) collective-permute-start(bf16[19,16,768]{2,1,0:T(8,128)(2,1)S(1)} %collective-permute-done.2), channel_id=1, source_target_pairs={{0,16},{2,0},{4,2},{6,4},{22,6},{20,22},{18,20},{16,18},{8,24},{10... | collective-permute-start | bytes 1400840 | tf_op jit(solution)/shard_map/ppermute | solution.py:562
  20.7 14.5 %collective-permute-start.11 = (bf16[38,16,768]{2,1,0:T(8,128)(2,1)S(1)}, bf16[38,16,768]{2,1,0:T(8,128)(2,1)S(1)}, u32[]{:S(2)}, u32[]{:S(2)}) collective-permute-start(bf16[38,16,768]{2,1,0:T(8,128)(2,1)S(1)} %constant_dynamic-update-slice_fusion.2.refs_8_), channel_id=1, source_target_pairs={{0,1},{1,0},{2,3},{3,2},{4,5},{5,4},{6,7},{7,6},{8,9},{9,8},{10,11... | collective-permute-start | bytes 2801672 | tf_op jit(solution)/shard_map/ppermute | solution.py:565
  22.4 14.5 %collective-permute-start.10 = (bf16[38,16,768]{2,1,0:T(8,128)(2,1)S(1)}, bf16[38,16,768]{2,1,0:T(8,128)(2,1)S(1)}, u32[]{:S(2)}, u32[]{:S(2)}) collective-permute-start(bf16[38,16,768]{2,1,0:T(8,128)(2,1)S(1)} %constant_dynamic-update-slice_fusion.2.refs_8_), channel_id=1, source_target_pairs={{0,8},{2,10},{4,12},{6,14},{22,30},{20,28},{18,26},{16,24},{8,0},{... | collective-permute-start | bytes 2801672 | tf_op jit(solution)/shard_map/ppermute | solution.py:565
  31.9 11.6 %collective-permute-start.9 = (bf16[19,16,768]{2,1,0:T(8,128)(2,1)S(1)}, bf16[19,16,768]{2,1,0:T(8,128)(2,1)S(1)}, u32[]{:S(2)}, u32[]{:S(2)}) collective-permute-start(bf16[19,16,768]{2,1,0:T(8,128)(2,1)S(1)} %collective-permute-done.5), channel_id=1, source_target_pairs={{0,16},{2,0},{4,2},{6,4},{22,6},{20,22},{18,20},{16,18},{8,24},{10... | collective-permute-start | bytes 1400840 | tf_op jit(solution)/shard_map/ppermute | solution.py:562
  33.1 27.5 %collective-permute-start.7 = (bf16[38,16,768]{2,1,0:T(8,128)(2,1)S(1)}, bf16[38,16,768]{2,1,0:T(8,128)(2,1)S(1)}, u32[]{:S(2)}, u32[]{:S(2)}) collective-permute-start(bf16[38,16,768]{2,1,0:T(8,128)(2,1)S(1)} %constant_dynamic-update-slice_fusion.refs_7_), channel_id=1, source_target_pairs={{0,8},{2,10},{4,12},{6,14},{22,30},{20,28},{18,26},{16,24},{8,0},{... | collective-permute-start | bytes 2801672 | tf_op jit(solution)/shard_map/ppermute | solution.py:565
  35.2 26.1 %collective-permute-start.18 = (bf16[38,16,768]{2,1,0:T(8,128)(2,1)S(1)}, bf16[38,16,768]{2,1,0:T(8,128)(2,1)S(1)}, u32[]{:S(2)}, u32[]{:S(2)}) collective-permute-start(bf16[38,16,768]{2,1,0:T(8,128)(2,1)S(1)} %constant_dynamic-update-slice_fusion.refs_7_), channel_id=1, source_target_pairs={{0,1},{1,0},{2,3},{3,2},{4,5},{5,4},{6,7},{7,6},{8,9},{9,8},{10,11... | collective-permute-start | bytes 2801672 | tf_op jit(solution)/shard_map/ppermute | solution.py:565
  47.3 13.3 %collective-permute-start.16 = (bf16[38,16,768]{2,1,0:T(8,128)(2,1)S(1)}, bf16[38,16,768]{2,1,0:T(8,128)(2,1)S(1)}, u32[]{:S(2)}, u32[]{:S(2)}) collective-permute-start(bf16[38,16,768]{2,1,0:T(8,128)(2,1)S(1)} %collective-permute-done.10.refs_13_), channel_id=1, source_target_pairs={{0,1},{1,0},{2,3},{3,2},{4,5},{5,4},{6,7},{7,6},{8,9},{9,8},{10,11... | collective-permute-start | bytes 2801672 | tf_op jit(solution)/shard_map/ppermute | solution.py:565
  48.5 12.8 %collective-permute-start.13 = (bf16[38,16,768]{2,1,0:T(8,128)(2,1)S(1)}, bf16[38,16,768]{2,1,0:T(8,128)(2,1)S(1)}, u32[]{:S(2)}, u32[]{:S(2)}) collective-permute-start(bf16[38,16,768]{2,1,0:T(8,128)(2,1)S(1)} %constant_dynamic-update-slice_fusion.4.refs_6_), channel_id=1, source_target_pairs={{0,8},{2,10},{4,12},{6,14},{22,30},{20,28},{18,26},{16,24},{8,0},{... | collective-permute-start | bytes 2801672 | tf_op jit(solution)/shard_map/ppermute | solution.py:565
  115.3 11.5 %collective-permute-start.29 = (bf16[2,2,19,16,768]{4,3,2,1,0:T(8,128)(2,1)}, bf16[2,2,19,16,768]{4,3,2,1,0:T(8,128)(2,1)S(1)}, u32[]{:S(2)}, u32[]{:S(2)}) collective-permute-start(bf16[2,2,19,16,768]{4,3,2,1,0:T(8,128)(2,1)} %get-tuple-element.101), channel_id=1, source_target_pairs={{0,1},{1,0},{2,3},{3,2},{4,5},{5,4},{6,7},{7,6},{8,9},{9,8},{10,11... | collective-permute-start | bytes 5603336 | tf_op jit(solution)/shard_map/ppermute | solution.py:586
  120.4 16.4 %collective-permute-start.33 = (bf16[2,19,16,768]{3,2,1,0:T(8,128)(2,1)S(1)}, bf16[2,19,16,768]{3,2,1,0:T(8,128)(2,1)S(1)}, u32[]{:S(2)}, u32[]{:S(2)}) collective-permute-start(bf16[2,19,16,768]{3,2,1,0:T(8,128)(2,1)S(1)} %fusion), channel_id=1, source_target_pairs={{0,8},{2,10},{4,12},{6,14},{22,30},{20,28},{18,26},{16,24},{8,0},{... | collective-permute-start | bytes 2801672 | tf_op jit(solution)/shard_map/ppermute | solution.py:595
  131.1 22.7 %collective-permute-start.32 = (bf16[2,19,16,768]{3,2,1,0:T(8,128)(2,1)S(1)}, bf16[2,19,16,768]{3,2,1,0:T(8,128)(2,1)S(1)}, u32[]{:S(2)}, u32[]{:S(2)}) collective-permute-start(bf16[2,19,16,768]{3,2,1,0:T(8,128)(2,1)S(1)} %fusion.2), channel_id=1, source_target_pairs={{0,8},{2,10},{4,12},{6,14},{22,30},{20,28},{18,26},{16,24},{8,0},{... | collective-permute-start | bytes 2801672 | tf_op jit(solution)/shard_map/ppermute | solution.py:602
  137.5 16.2 %collective-permute-start.37 = (bf16[19,16,768]{2,1,0:T(8,128)(2,1)S(1)}, bf16[19,16,768]{2,1,0:T(8,128)(2,1)S(1)}, u32[]{:S(2)}, u32[]{:S(2)}) collective-permute-start(bf16[19,16,768]{2,1,0:T(8,128)(2,1)S(1)} %get-tuple-element.128), channel_id=1, source_target_pairs={{0,16},{2,0},{4,2},{6,4},{22,6},{20,22},{18,20},{16,18},{8,24},{10... | collective-permute-start | bytes 1400840 | tf_op jit(solution)/shard_map/ppermute | solution.py:607
  137.9 15.9 %collective-permute-start.36 = (bf16[19,16,768]{2,1,0:T(8,128)(2,1)S(1)}, bf16[19,16,768]{2,1,0:T(8,128)(2,1)S(1)}, u32[]{:S(2)}, u32[]{:S(2)}) collective-permute-start(bf16[19,16,768]{2,1,0:T(8,128)(2,1)S(1)} %get-tuple-element.129), channel_id=1, source_target_pairs={{0,2},{2,4},{4,6},{6,22},{22,20},{20,18},{18,16},{16,0},{8,10},{10... | collective-permute-start | bytes 1400840 | tf_op jit(solution)/shard_map/ppermute | solution.py:606
  143.8 15.1 %collective-permute-start.25 = (bf16[2,1,19,16,768]{4,3,2,1,0:T(8,128)(2,1)S(1)}, bf16[2,1,19,16,768]{4,3,2,1,0:T(8,128)(2,1)S(1)}, u32[]{:S(2)}, u32[]{:S(2)}) collective-permute-start(bf16[2,1,19,16,768]{4,3,2,1,0:T(8,128)(2,1)S(1)} %copy-done.23), channel_id=1, source_target_pairs={{0,1},{1,0},{2,3},{3,2},{4,5},{5,4},{6,7},{7,6},{8,9},{9,8},{10,11... | collective-permute-start | bytes 2801672 | tf_op jit(solution)/shard_map/ppermute | solution.py:597
  145.4 13.7 %collective-permute-start.31 = (bf16[2,19,16,768]{3,2,1,0:T(8,128)(2,1)S(1)}, bf16[2,19,16,768]{3,2,1,0:T(8,128)(2,1)S(1)}, u32[]{:S(2)}, u32[]{:S(2)}) collective-permute-start(bf16[2,19,16,768]{3,2,1,0:T(8,128)(2,1)S(1)} %fusion.4), channel_id=1, source_target_pairs={{0,8},{2,10},{4,12},{6,14},{22,30},{20,28},{18,26},{16,24},{8,0},{... | collective-permute-start | bytes 2801672 | tf_op jit(solution)/shard_map/ppermute | solution.py:608
  154.4 14.4 %collective-permute-start.39 = (bf16[19,16,768]{2,1,0:T(8,128)(2,1)S(1)}, bf16[19,16,768]{2,1,0:T(8,128)(2,1)S(1)}, u32[]{:S(2)}, u32[]{:S(2)}) collective-permute-start(bf16[19,16,768]{2,1,0:T(8,128)(2,1)S(1)} %get-tuple-element.126), channel_id=1, source_target_pairs={{0,16},{2,0},{4,2},{6,4},{22,6},{20,22},{18,20},{16,18},{8,24},{10... | collective-permute-start | bytes 1400840 | tf_op jit(solution)/shard_map/ppermute | solution.py:612
  154.5 14.4 %collective-permute-start.38 = (bf16[19,16,768]{2,1,0:T(8,128)(2,1)S(1)}, bf16[19,16,768]{2,1,0:T(8,128)(2,1)S(1)}, u32[]{:S(2)}, u32[]{:S(2)}) collective-permute-start(bf16[19,16,768]{2,1,0:T(8,128)(2,1)S(1)} %get-tuple-element.127), channel_id=1, source_target_pairs={{0,2},{2,4},{4,6},{6,22},{22,20},{20,18},{18,16},{16,0},{8,10},{10... | collective-permute-start | bytes 1400840 | tf_op jit(solution)/shard_map/ppermute | solution.py:611
  159.0 14.8 %collective-permute-start.26 = (bf16[1,19,16,768]{3,2,1,0:T(8,128)(2,1)S(1)}, bf16[1,19,16,768]{3,2,1,0:T(8,128)(2,1)S(1)}, u32[]{:S(2)}, u32[]{:S(2)}) collective-permute-start(bf16[1,19,16,768]{3,2,1,0:T(8,128)(2,1)S(1)} %fusion.21), channel_id=1, source_target_pairs={{0,8},{2,10},{4,12},{6,14},{22,30},{20,28},{18,26},{16,24},{8,0},{... | collective-permute-start | bytes 1400840 | tf_op jit(solution)/shard_map/ppermute | solution.py:613
  169.4 13.3 %collective-permute-start.40 = (bf16[19,16,768]{2,1,0:T(8,128)(2,1)S(1)}, bf16[19,16,768]{2,1,0:T(8,128)(2,1)S(1)}, u32[]{:S(2)}, u32[]{:S(2)}) collective-permute-start(bf16[19,16,768]{2,1,0:T(8,128)(2,1)S(1)} %get-tuple-element.124), channel_id=1, source_target_pairs={{0,2},{2,4},{4,6},{6,22},{22,20},{20,18},{18,16},{16,0},{8,10},{10... | collective-permute-start | bytes 1400840 | tf_op jit(solution)/shard_map/ppermute | solution.py:616
  173.8 10.9 %collective-permute-start.41 = (bf16[19,16,768]{2,1,0:T(8,128)(2,1)S(1)}, bf16[19,16,768]{2,1,0:T(8,128)(2,1)S(1)}, u32[]{:S(2)}, u32[]{:S(2)}) collective-permute-start(bf16[19,16,768]{2,1,0:T(8,128)(2,1)S(1)} %get-tuple-element.125), channel_id=1, source_target_pairs={{0,16},{2,0},{4,2},{6,4},{22,6},{20,22},{18,20},{16,18},{8,24},{10... | collective-permute-start | bytes 1400840 | tf_op jit(solution)/shard_map/ppermute | solution.py:617
  (52 other events, 457.8 us)

commit v5 on v4

--- a/solution.py
+++ b/solution.py
@@ -533,15 +533,15 @@
 PLAN = (
     ("s0", 0, 0),
     ("s1", 1, 2),
-    ("s2", 2, 4),
+    ("s2", 2, 3),
     ("s3", 3, 4),
     ("s4", 4, 4),
-    ("c0", 1, 1),
+    ("c0", 0, 0),
     ("c1", 2, 2),
     ("c2", 4, 4),
     ("c3", 4, 4),
-    ("c4", 4, 4),
-    ("cs0", 2, 2),
+    ("c4", 4, 5),
+    ("cs0", 1, 2),
     ("cs1", 3, 3),
     ("cs2", 3, 4),
     ("cs3", 4, 5),
@@ -593,7 +593,7 @@
     sent[3], got[0] = stage((sent[3], got[0]))
     got[3] = pair(sent[3])
     moved[1] = swap(add(flipped[1], got[1][1]))
-    sent[4], got[1] = stage((sent[4], got[1]))
+    sent[4], got[2] = stage((sent[4], got[2]))
     got[4] = pair(sent[4])
     moved[0], got[2], got[3] = stage((moved[0], got[2], got[3]))
     first = total(0)[0].astype(BF16)

time: 195 us -> 195 us (level)
  waiting for transfers between devices: 84.3 us -> 77.6 us
  starting transfers between devices: 48.7 us -> 55 us
    ppermute x1, waiting for transfers between devices: 5.65 us -> 0.9 us  [scatter_sums(): moved[1] = swap(add(flipped[1], got[1][1]))]
    ppermute x2, starting transfers between devices: 3.77 us -> 7.97 us  [scatter_sums(): right, left = (cw(first[:half]), ccw(first[half:]))]
    ppermute x2, waiting for transfers between devices: 0.14 us -> 4.13 us  [scatter_sums(): right, left = (cw(first[:half]), ccw(first[half:]))]
    ppermute x1, waiting for transfers between devices: 5.92 us -> 2.19 us  [scatter_sums(): moved[0] = swap(add(flipped[0], got[0][1]))]
    ppermute x8, starting transfers between devices: 8.85 us -> 6.24 us  [gather_pieces(): arrivals = {'right': cw(right), 'left': ccw(left)}]
    ppermute x5, starting transfers between devices: 3.68 us -> 5.97 us  [gather_pieces(): swap(have['p' + what[1:]])]
    ppermute x10, starting transfers between devices: 11 us -> 8.77 us  [gather_pieces(): pair(have[what[1:] if what[1] == 's' else 'p' + what[1:]])]
    ppermute x10, waiting for transfers between devices: 2.97 us -> 0.89 us  [gather_pieces(): pair(have[what[1:] if what[1] == 's' else 'p' + what[1:]])]
where the time goes in v5:
time: 195 us; the launch traced here: 192 us
  waiting for transfers between devices  77.6 us (40%)
  starting transfers between devices  55 us (28%)
  Pallas kernels  42.9 us (22%)
  other arithmetic  8.77 us (4%)
  local copies, waits for them, and re-layouts  6.53 us (3%)
    pallas_call x1, Pallas kernels, run_kernel(): pl.pallas_call(functools.partial(kernel, fast, n_in, len(out_shape)), out...  42.9 us
    ppermute x8, waiting for transfers between devices, gather_pieces(): arrivals = {'right': cw(right), 'left': ccw(left)}  27.3 us
    ppermute x5, waiting for transfers between devices, gather_pieces(): swap(have['p' + what[1:]])  9.69 us
    ppermute x1, waiting for transfers between devices, scatter_sums(): left = ccw((third[1] + left.astype(F32)).astype(BF16))  9.4 us
    ppermute x10, starting transfers between devices, gather_pieces(): pair(have[what[1:] if what[1] == 's' else 'p' + what[1:]])  8.77 us
    ppermute x1, waiting for transfers between devices, scatter_sums(): right = cw((fourth[0] + right.astype(F32)).astype(BF16))  8.62 us
    ppermute x2, starting transfers between devices, scatter_sums(): right, left = (cw(first[:half]), ccw(first[half:]))  7.97 us
    ppermute x1, waiting for transfers between devices, scatter_sums(): left = ccw((second[1] + left.astype(F32)).astype(BF16))  7.59 us
  transfers between devices with their start and end apart: 43, of which 21 were waited for; matrix products, arithmetic and copies ran while one was open for 4% of the time, Pallas kernels for 0%

profile of v5, /device:TPU:17, one launch (start us, length us, event | category | flops | bytes accessed | tf_op | source)
XLA Modules:
  0.0 192.4 jit_solution(11135175706744871612)
XLA Ops:
  8.8 5.0 %collective-permute-done.3.refs_14_ = bf16[19,16,768]{2,1,0:T(8,128)(2,1)S(1)} collective-permute-done((bf16[19,16,768]{2,1,0:T(8,128)(2,1)S(1)}, bf16[19,16,768]{2,1,0:T(8,128)(2,1)S(1)}, u32[]{:S(2)}, u32[]{:S(2)}) %collective-permute-start.3) | collective-permute-done | bytes 466976 | tf_op jit(solution)/shard_map/ppermute | solution.py:565
  13.8 5.4 %collective-permute-done.2 = bf16[19,16,768]{2,1,0:T(8,128)(2,1)S(1)} collective-permute-done((bf16[19,16,768]{2,1,0:T(8,128)(2,1)S(1)}, bf16[19,16,768]{2,1,0:T(8,128)(2,1)S(1)}, u32[]{:S(2)}, u32[]{:S(2)}) %collective-permute-start.2) | collective-permute-done | bytes 466976 | tf_op jit(solution)/shard_map/ppermute | solution.py:562
  20.9 2.0 %collective-permute-start.10 = (bf16[38,16,768]{2,1,0:T(8,128)(2,1)S(1)}, bf16[38,16,768]{2,1,0:T(8,128)(2,1)S(1)}, u32[]{:S(2)}, u32[]{:S(2)}) collective-permute-start(bf16[38,16,768]{2,1,0:T(8,128)(2,1)S(1)} %constant_dynamic-update-slice_fusion.refs_8_), channel_id=1, source_target_pairs={{0,1},{1,0},{2,3},{3,2},{4,5},{5,4},{6,7},{7,6},{8,9},{9,8},{10,11... | collective-permute-start | bytes 2801672 | tf_op jit(solution)/shard_map/ppermute | solution.py:565
  24.2 5.8 %collective-permute-done.5 = bf16[19,16,768]{2,1,0:T(8,128)(2,1)S(1)} collective-permute-done((bf16[19,16,768]{2,1,0:T(8,128)(2,1)S(1)}, bf16[19,16,768]{2,1,0:T(8,128)(2,1)S(1)}, u32[]{:S(2)}, u32[]{:S(2)}) %collective-permute-start.5) | collective-permute-done | bytes 466976 | tf_op jit(solution)/shard_map/ppermute | solution.py:562
  33.4 2.3 %collective-permute-start.15 = (bf16[38,16,768]{2,1,0:T(8,128)(2,1)S(1)}, bf16[38,16,768]{2,1,0:T(8,128)(2,1)S(1)}, u32[]{:S(2)}, u32[]{:S(2)}) collective-permute-start(bf16[38,16,768]{2,1,0:T(8,128)(2,1)S(1)} %constant_dynamic-update-slice_fusion.4.refs_7_), channel_id=1, source_target_pairs={{0,8},{2,10},{4,12},{6,14},{22,30},{20,28},{18,26},{16,24},{8,0},{... | collective-permute-start | bytes 2801672 | tf_op jit(solution)/shard_map/ppermute | solution.py:565
  35.7 6.0 %collective-permute-done.7 = bf16[19,16,768]{2,1,0:T(8,128)(2,1)S(1)} collective-permute-done((bf16[19,16,768]{2,1,0:T(8,128)(2,1)S(1)}, bf16[19,16,768]{2,1,0:T(8,128)(2,1)S(1)}, u32[]{:S(2)}, u32[]{:S(2)}) %collective-permute-start.7) | collective-permute-done | bytes 466976 | tf_op jit(solution)/shard_map/ppermute | solution.py:562
  41.7 2.0 %collective-permute-done.8 = bf16[19,16,768]{2,1,0:T(8,128)(2,1)S(1)} collective-permute-done((bf16[19,16,768]{2,1,0:T(8,128)(2,1)S(1)}, bf16[19,16,768]{2,1,0:T(8,128)(2,1)S(1)}, u32[]{:S(2)}, u32[]{:S(2)}) %collective-permute-start.8) | collective-permute-done | bytes 466976 | tf_op jit(solution)/shard_map/ppermute | solution.py:562
  43.7 2.8 %collective-permute-start.16 = (bf16[38,16,768]{2,1,0:T(8,128)(2,1)S(1)}, bf16[38,16,768]{2,1,0:T(8,128)(2,1)S(1)}, u32[]{:S(2)}, u32[]{:S(2)}) collective-permute-start(bf16[38,16,768]{2,1,0:T(8,128)(2,1)S(1)} %collective-permute-done.9.refs_13_), channel_id=1, source_target_pairs={{0,1},{1,0},{2,3},{3,2},{4,5},{5,4},{6,7},{7,6},{8,9},{9,8},{10,11... | collective-permute-start | bytes 2801672 | tf_op jit(solution)/shard_map/ppermute | solution.py:565
  49.1 6.4 %collective-permute-done.13 = bf16[9,16,768]{2,1,0:T(8,128)(2,1)S(1)} collective-permute-done((bf16[9,16,768]{2,1,0:T(8,128)(2,1)S(1)}, bf16[9,16,768]{2,1,0:T(8,128)(2,1)S(1)}, u32[]{:S(2)}, u32[]{:S(2)}) %collective-permute-start.13) | collective-permute-done | bytes 221216 | tf_op jit(solution)/shard_map/ppermute | solution.py:562
  61.5 2.9 %collective-permute-done.17.refs_10_ = bf16[19,16,768]{2,1,0:T(8,128)(2,1)} collective-permute-done((bf16[19,16,768]{2,1,0:T(8,128)(2,1)S(1)}, bf16[19,16,768]{2,1,0:T(8,128)(2,1)}, u32[]{:S(2)}, u32[]{:S(2)}) %collective-permute-start.17) | collective-permute-done | bytes 466976 | tf_op jit(solution)/shard_map/ppermute | solution.py:565
  67.8 42.9 %blocks.1 = (bf16[256,768]{1,0:T(8,128)(2,1)}, bf16[256,768]{1,0:T(8,128)(2,1)}, f32[1,9216]{1,0:T(1,128)}, bf16[1,19,16,768]{3,2,1,0:T(8,128)(2,1)}, bf16[1,19,...) custom-call(s32[1,65]{1,0:T(1,128)} %constant_dynamic-slice_fusion.r, ...), custom_call_target="tpu_custom_call" | custom-call | flops 22000001024 | bytes 32000000 | tf_op jit(solution)/shard_map/blocks/pallas_call | solution.py:469
  111.6 1.9 collective-permute-done.27
  116.6 2.2 %collective-permute-done.32 = bf16[2,2,19,16,768]{4,3,2,1,0:T(8,128)(2,1)S(1)} collective-permute-done((bf16[2,2,19,16,768]{4,3,2,1,0:T(8,128)(2,1)}, bf16[2,2,19,16,768]{4,3,2,1,0:T(8,128)(2,1)S(1)}, u32[]{:S(2)}, u32[]{:S(2)}) %collective-permute-start.32) | collective-permute-done | bytes 1867808 | tf_op jit(solution)/shard_map/ppermute | solution.py:586
  120.7 2.2 %collective-permute-done.28 = bf16[1,19,16,768]{3,2,1,0:T(8,128)(2,1)S(1)} collective-permute-done((bf16[1,19,16,768]{3,2,1,0:T(8,128)(2,1)S(1)}, bf16[1,19,16,768]{3,2,1,0:T(8,128)(2,1)S(1)}, u32[]{:S(2)}, u32[]{:S(2)}) %collective-permute-start.28) | collective-permute-done | bytes 466976 | tf_op jit(solution)/shard_map/ppermute | solution.py:592
  123.1 7.9 %collective-permute-start.34 = (bf16[9,16,768]{2,1,0:T(8,128)(2,1)S(1)}, bf16[9,16,768]{2,1,0:T(8,128)(2,1)S(1)}, u32[]{:S(2)}, u32[]{:S(2)}) collective-permute-start(bf16[9,16,768]{2,1,0:T(8,128)(2,1)S(1)} %slice_bitcast_fusion.12), channel_id=1, source_target_pairs={{0,2},{2,4},{4,6},{6,22},{22,20},{20,18},{18,16},{16,0},{8,10},{10... | collective-permute-start | bytes 663560 | tf_op jit(solution)/shard_map/ppermute | solution.py:601
  134.5 2.5 %collective-permute-done.35 = bf16[10,16,768]{2,1,0:T(8,128)(2,1)S(1)} collective-permute-done((bf16[10,16,768]{2,1,0:T(8,128)(2,1)S(1)}, bf16[10,16,768]{2,1,0:T(8,128)(2,1)S(1)}, u32[]{:S(2)}, u32[]{:S(2)}) %collective-permute-start.35) | collective-permute-done | bytes 245792 | tf_op jit(solution)/shard_map/ppermute | solution.py:601
  137.9 6.1 %collective-permute-start.36 = (bf16[19,16,768]{2,1,0:T(8,128)(2,1)S(1)}, bf16[19,16,768]{2,1,0:T(8,128)(2,1)S(1)}, u32[]{:S(2)}, u32[]{:S(2)}) collective-permute-start(bf16[19,16,768]{2,1,0:T(8,128)(2,1)S(1)} %get-tuple-element.127), channel_id=1, source_target_pairs={{0,2},{2,4},{4,6},{6,22},{22,20},{20,18},{18,16},{16,0},{8,10},{10... | collective-permute-start | bytes 1400840 | tf_op jit(solution)/shard_map/ppermute | solution.py:606
  146.2 7.6 %collective-permute-done.37 = bf16[19,16,768]{2,1,0:T(8,128)(2,1)S(1)} collective-permute-done((bf16[19,16,768]{2,1,0:T(8,128)(2,1)S(1)}, bf16[19,16,768]{2,1,0:T(8,128)(2,1)S(1)}, u32[]{:S(2)}, u32[]{:S(2)}) %collective-permute-start.37) | collective-permute-done | bytes 466976 | tf_op jit(solution)/shard_map/ppermute | solution.py:607
  154.5 4.5 %collective-permute-start.38 = (bf16[19,16,768]{2,1,0:T(8,128)(2,1)S(1)}, bf16[19,16,768]{2,1,0:T(8,128)(2,1)S(1)}, u32[]{:S(2)}, u32[]{:S(2)}) collective-permute-start(bf16[19,16,768]{2,1,0:T(8,128)(2,1)S(1)} %get-tuple-element.125), channel_id=1, source_target_pairs={{0,2},{2,4},{4,6},{6,22},{22,20},{20,18},{18,16},{16,0},{8,10},{10... | collective-permute-start | bytes 1400840 | tf_op jit(solution)/shard_map/ppermute | solution.py:611
  159.2 9.4 %collective-permute-done.39 = bf16[19,16,768]{2,1,0:T(8,128)(2,1)S(1)} collective-permute-done((bf16[19,16,768]{2,1,0:T(8,128)(2,1)S(1)}, bf16[19,16,768]{2,1,0:T(8,128)(2,1)S(1)}, u32[]{:S(2)}, u32[]{:S(2)}) %collective-permute-start.39) | collective-permute-done | bytes 466976 | tf_op jit(solution)/shard_map/ppermute | solution.py:612
  169.3 4.7 %collective-permute-start.40 = (bf16[19,16,768]{2,1,0:T(8,128)(2,1)S(1)}, bf16[19,16,768]{2,1,0:T(8,128)(2,1)S(1)}, u32[]{:S(2)}, u32[]{:S(2)}) collective-permute-start(bf16[19,16,768]{2,1,0:T(8,128)(2,1)S(1)} %get-tuple-element.122), channel_id=1, source_target_pairs={{0,2},{2,4},{4,6},{6,22},{22,20},{20,18},{18,16},{16,0},{8,10},{10... | collective-permute-start | bytes 1400840 | tf_op jit(solution)/shard_map/ppermute | solution.py:616
  173.9 8.6 %collective-permute-done.40 = bf16[19,16,768]{2,1,0:T(8,128)(2,1)S(1)} collective-permute-done((bf16[19,16,768]{2,1,0:T(8,128)(2,1)S(1)}, bf16[19,16,768]{2,1,0:T(8,128)(2,1)S(1)}, u32[]{:S(2)}, u32[]{:S(2)}) %collective-permute-start.40) | collective-permute-done | bytes 466976 | tf_op jit(solution)/shard_map/ppermute | solution.py:616
  182.5 2.0 %collective-permute-done.41 = bf16[19,16,768]{2,1,0:T(8,128)(2,1)S(1)} collective-permute-done((bf16[19,16,768]{2,1,0:T(8,128)(2,1)S(1)}, bf16[19,16,768]{2,1,0:T(8,128)(2,1)S(1)}, u32[]{:S(2)}, u32[]{:S(2)}) %collective-permute-start.41) | collective-permute-done | bytes 466976 | tf_op jit(solution)/shard_map/ppermute | solution.py:617
  185.5 2.6 %collective-permute-start.42 = (f32[4,24,768]{2,1,0:T(8,128)S(1)}, f32[4,24,768]{2,1,0:T(8,128)S(1)}, u32[]{:S(2)}, u32[]{:S(2)}) collective-permute-start(f32[4,24,768]{2,1,0:T(8,128)S(1)} %get-tuple-element.143), channel_id=1, source_target_pairs={{0,1},{1,0},{2,3},{3,2},{4,5},{5,4},{6,7},{7,6},{8,9},{9,8},{10,11... | collective-permute-start | bytes 884744 | tf_op jit(solution)/shard_map/ppermute | solution.py:660
  (185 shorter events, 45.2 us)
Async XLA Ops:
  7.3 11.9 %collective-permute-start.2 = (bf16[19,16,768]{2,1,0:T(8,128)(2,1)S(1)}, bf16[19,16,768]{2,1,0:T(8,128)(2,1)S(1)}, u32[]{:S(2)}, u32[]{:S(2)}) collective-permute-start(bf16[19,16,768]{2,1,0:T(8,128)(2,1)S(1)} %fusion.28.refs_9_), channel_id=1, source_target_pairs={{0,16},{2,0},{4,2},{6,4},{22,6},{20,22},{18,20},{16,18},{8,24},{10... | collective-permute-start | bytes 1400840 | tf_op jit(solution)/shard_map/ppermute | solution.py:562
  7.5 11.7 %collective-permute-start.1 = (bf16[19,16,768]{2,1,0:T(8,128)(2,1)S(1)}, bf16[19,16,768]{2,1,0:T(8,128)(2,1)S(1)}, u32[]{:S(2)}, u32[]{:S(2)}) collective-permute-start(bf16[19,16,768]{2,1,0:T(8,128)(2,1)S(1)} %fusion.28.refs_9_), channel_id=1, source_target_pairs={{0,2},{2,4},{4,6},{6,22},{22,20},{20,18},{18,16},{16,0},{8,10},{10... | collective-permute-start | bytes 1400840 | tf_op jit(solution)/shard_map/ppermute | solution.py:562
  19.2 10.8 %collective-permute-start.5 = (bf16[19,16,768]{2,1,0:T(8,128)(2,1)S(1)}, bf16[19,16,768]{2,1,0:T(8,128)(2,1)S(1)}, u32[]{:S(2)}, u32[]{:S(2)}) collective-permute-start(bf16[19,16,768]{2,1,0:T(8,128)(2,1)S(1)} %collective-permute-done.1), channel_id=1, source_target_pairs={{0,2},{2,4},{4,6},{6,22},{22,20},{20,18},{18,16},{16,0},{8,10},{10... | collective-permute-start | bytes 1400840 | tf_op jit(solution)/shard_map/ppermute | solution.py:562
  20.8 11.0 %collective-permute-start.6 = (bf16[19,16,768]{2,1,0:T(8,128)(2,1)S(1)}, bf16[19,16,768]{2,1,0:T(8,128)(2,1)S(1)}, u32[]{:S(2)}, u32[]{:S(2)}) collective-permute-start(bf16[19,16,768]{2,1,0:T(8,128)(2,1)S(1)} %collective-permute-done.2), channel_id=1, source_target_pairs={{0,16},{2,0},{4,2},{6,4},{22,6},{20,22},{18,20},{16,18},{8,24},{10... | collective-permute-start | bytes 1400840 | tf_op jit(solution)/shard_map/ppermute | solution.py:562
  20.9 14.8 %collective-permute-start.10 = (bf16[38,16,768]{2,1,0:T(8,128)(2,1)S(1)}, bf16[38,16,768]{2,1,0:T(8,128)(2,1)S(1)}, u32[]{:S(2)}, u32[]{:S(2)}) collective-permute-start(bf16[38,16,768]{2,1,0:T(8,128)(2,1)S(1)} %constant_dynamic-update-slice_fusion.refs_8_), channel_id=1, source_target_pairs={{0,1},{1,0},{2,3},{3,2},{4,5},{5,4},{6,7},{7,6},{8,9},{9,8},{10,11... | collective-permute-start | bytes 2801672 | tf_op jit(solution)/shard_map/ppermute | solution.py:565
  22.8 12.8 %collective-permute-start.9 = (bf16[38,16,768]{2,1,0:T(8,128)(2,1)S(1)}, bf16[38,16,768]{2,1,0:T(8,128)(2,1)S(1)}, u32[]{:S(2)}, u32[]{:S(2)}) collective-permute-start(bf16[38,16,768]{2,1,0:T(8,128)(2,1)S(1)} %constant_dynamic-update-slice_fusion.refs_8_), channel_id=1, source_target_pairs={{0,8},{2,10},{4,12},{6,14},{22,30},{20,28},{18,26},{16,24},{8,0},{... | collective-permute-start | bytes 2801672 | tf_op jit(solution)/shard_map/ppermute | solution.py:565
  23.1 10.3 %collective-permute-start.11 = (bf16[19,16,768]{2,1,0:T(8,128)(2,1)S(1)}, bf16[19,16,768]{2,1,0:T(8,128)(2,1)S(1)}, u32[]{:S(2)}, u32[]{:S(2)}) collective-permute-start(bf16[19,16,768]{2,1,0:T(8,128)(2,1)S(1)} %collective-permute-done.3.refs_14_), channel_id=1, source_target_pairs={{0,1},{1,0},{2,3},{3,2},{4,5},{5,4},{6,7},{7,6},{8,9},{9,8},{10,11... | collective-permute-start | bytes 1400840 | tf_op jit(solution)/shard_map/ppermute | solution.py:565
  31.8 9.9 %collective-permute-start.7 = (bf16[19,16,768]{2,1,0:T(8,128)(2,1)S(1)}, bf16[19,16,768]{2,1,0:T(8,128)(2,1)S(1)}, u32[]{:S(2)}, u32[]{:S(2)}) collective-permute-start(bf16[19,16,768]{2,1,0:T(8,128)(2,1)S(1)} %collective-permute-done.5), channel_id=1, source_target_pairs={{0,2},{2,4},{4,6},{6,22},{22,20},{20,18},{18,16},{16,0},{8,10},{10... | collective-permute-start | bytes 1400840 | tf_op jit(solution)/shard_map/ppermute | solution.py:562
  32.8 10.9 %collective-permute-start.8 = (bf16[19,16,768]{2,1,0:T(8,128)(2,1)S(1)}, bf16[19,16,768]{2,1,0:T(8,128)(2,1)S(1)}, u32[]{:S(2)}, u32[]{:S(2)}) collective-permute-start(bf16[19,16,768]{2,1,0:T(8,128)(2,1)S(1)} %collective-permute-done.6), channel_id=1, source_target_pairs={{0,16},{2,0},{4,2},{6,4},{22,6},{20,22},{18,20},{16,18},{8,24},{10... | collective-permute-start | bytes 1400840 | tf_op jit(solution)/shard_map/ppermute | solution.py:562
  33.4 22.7 %collective-permute-start.15 = (bf16[38,16,768]{2,1,0:T(8,128)(2,1)S(1)}, bf16[38,16,768]{2,1,0:T(8,128)(2,1)S(1)}, u32[]{:S(2)}, u32[]{:S(2)}) collective-permute-start(bf16[38,16,768]{2,1,0:T(8,128)(2,1)S(1)} %constant_dynamic-update-slice_fusion.4.refs_7_), channel_id=1, source_target_pairs={{0,8},{2,10},{4,12},{6,14},{22,30},{20,28},{18,26},{16,24},{8,0},{... | collective-permute-start | bytes 2801672 | tf_op jit(solution)/shard_map/ppermute | solution.py:565
  43.7 12.5 %collective-permute-start.16 = (bf16[38,16,768]{2,1,0:T(8,128)(2,1)S(1)}, bf16[38,16,768]{2,1,0:T(8,128)(2,1)S(1)}, u32[]{:S(2)}, u32[]{:S(2)}) collective-permute-start(bf16[38,16,768]{2,1,0:T(8,128)(2,1)S(1)} %collective-permute-done.9.refs_13_), channel_id=1, source_target_pairs={{0,1},{1,0},{2,3},{3,2},{4,5},{5,4},{6,7},{7,6},{8,9},{9,8},{10,11... | collective-permute-start | bytes 2801672 | tf_op jit(solution)/shard_map/ppermute | solution.py:565
  46.5 12.9 %collective-permute-start.12 = (bf16[38,16,768]{2,1,0:T(8,128)(2,1)S(1)}, bf16[38,16,768]{2,1,0:T(8,128)(2,1)}, u32[]{:S(2)}, u32[]{:S(2)}) collective-permute-start(bf16[38,16,768]{2,1,0:T(8,128)(2,1)S(1)} %constant_dynamic-update-slice_fusion.2.refs_6_), channel_id=1, source_target_pairs={{0,8},{2,10},{4,12},{6,14},{22,30},{20,28},{18,26},{16,24},{8,0},{... | collective-permute-start | bytes 2801672 | tf_op jit(solution)/shard_map/ppermute | solution.py:565
  119.1 13.8 %collective-permute-start.33 = (bf16[2,19,16,768]{3,2,1,0:T(8,128)(2,1)S(1)}, bf16[2,19,16,768]{3,2,1,0:T(8,128)(2,1)S(1)}, u32[]{:S(2)}, u32[]{:S(2)}) collective-permute-start(bf16[2,19,16,768]{3,2,1,0:T(8,128)(2,1)S(1)} %fusion), channel_id=1, source_target_pairs={{0,8},{2,10},{4,12},{6,14},{22,30},{20,28},{18,26},{16,24},{8,0},{... | collective-permute-start | bytes 2801672 | tf_op jit(solution)/shard_map/ppermute | solution.py:595
  123.1 11.4 %collective-permute-start.34 = (bf16[9,16,768]{2,1,0:T(8,128)(2,1)S(1)}, bf16[9,16,768]{2,1,0:T(8,128)(2,1)S(1)}, u32[]{:S(2)}, u32[]{:S(2)}) collective-permute-start(bf16[9,16,768]{2,1,0:T(8,128)(2,1)S(1)} %slice_bitcast_fusion.12), channel_id=1, source_target_pairs={{0,2},{2,4},{4,6},{6,22},{22,20},{20,18},{18,16},{16,0},{8,10},{10... | collective-permute-start | bytes 663560 | tf_op jit(solution)/shard_map/ppermute | solution.py:601
  131.3 22.5 %collective-permute-start.31 = (bf16[2,19,16,768]{3,2,1,0:T(8,128)(2,1)S(1)}, bf16[2,19,16,768]{3,2,1,0:T(8,128)(2,1)S(1)}, u32[]{:S(2)}, u32[]{:S(2)}) collective-permute-start(bf16[2,19,16,768]{3,2,1,0:T(8,128)(2,1)S(1)} %fusion.2), channel_id=1, source_target_pairs={{0,8},{2,10},{4,12},{6,14},{22,30},{20,28},{18,26},{16,24},{8,0},{... | collective-permute-start | bytes 2801672 | tf_op jit(solution)/shard_map/ppermute | solution.py:602
  137.6 16.2 %collective-permute-start.37 = (bf16[19,16,768]{2,1,0:T(8,128)(2,1)S(1)}, bf16[19,16,768]{2,1,0:T(8,128)(2,1)S(1)}, u32[]{:S(2)}, u32[]{:S(2)}) collective-permute-start(bf16[19,16,768]{2,1,0:T(8,128)(2,1)S(1)} %get-tuple-element.126), channel_id=1, source_target_pairs={{0,16},{2,0},{4,2},{6,4},{22,6},{20,22},{18,20},{16,18},{8,24},{10... | collective-permute-start | bytes 1400840 | tf_op jit(solution)/shard_map/ppermute | solution.py:607
  137.9 15.9 %collective-permute-start.36 = (bf16[19,16,768]{2,1,0:T(8,128)(2,1)S(1)}, bf16[19,16,768]{2,1,0:T(8,128)(2,1)S(1)}, u32[]{:S(2)}, u32[]{:S(2)}) collective-permute-start(bf16[19,16,768]{2,1,0:T(8,128)(2,1)S(1)} %get-tuple-element.127), channel_id=1, source_target_pairs={{0,2},{2,4},{4,6},{6,22},{22,20},{20,18},{18,16},{16,0},{8,10},{10... | collective-permute-start | bytes 1400840 | tf_op jit(solution)/shard_map/ppermute | solution.py:606
  144.1 15.0 %collective-permute-start.25 = (bf16[2,1,19,16,768]{4,3,2,1,0:T(8,128)(2,1)S(1)}, bf16[2,1,19,16,768]{4,3,2,1,0:T(8,128)(2,1)S(1)}, u32[]{:S(2)}, u32[]{:S(2)}) collective-permute-start(bf16[2,1,19,16,768]{4,3,2,1,0:T(8,128)(2,1)S(1)} %copy-done.23), channel_id=1, source_target_pairs={{0,1},{1,0},{2,3},{3,2},{4,5},{5,4},{6,7},{7,6},{8,9},{9,8},{10,11... | collective-permute-start | bytes 2801672 | tf_op jit(solution)/shard_map/ppermute | solution.py:597
  145.8 13.4 %collective-permute-start.30 = (bf16[2,19,16,768]{3,2,1,0:T(8,128)(2,1)S(1)}, bf16[2,19,16,768]{3,2,1,0:T(8,128)(2,1)S(1)}, u32[]{:S(2)}, u32[]{:S(2)}) collective-permute-start(bf16[2,19,16,768]{3,2,1,0:T(8,128)(2,1)S(1)} %fusion.4), channel_id=1, source_target_pairs={{0,8},{2,10},{4,12},{6,14},{22,30},{20,28},{18,26},{16,24},{8,0},{... | collective-permute-start | bytes 2801672 | tf_op jit(solution)/shard_map/ppermute | solution.py:608
  154.4 14.2 %collective-permute-start.39 = (bf16[19,16,768]{2,1,0:T(8,128)(2,1)S(1)}, bf16[19,16,768]{2,1,0:T(8,128)(2,1)S(1)}, u32[]{:S(2)}, u32[]{:S(2)}) collective-permute-start(bf16[19,16,768]{2,1,0:T(8,128)(2,1)S(1)} %get-tuple-element.124), channel_id=1, source_target_pairs={{0,16},{2,0},{4,2},{6,4},{22,6},{20,22},{18,20},{16,18},{8,24},{10... | collective-permute-start | bytes 1400840 | tf_op jit(solution)/shard_map/ppermute | solution.py:612
  154.5 14.2 %collective-permute-start.38 = (bf16[19,16,768]{2,1,0:T(8,128)(2,1)S(1)}, bf16[19,16,768]{2,1,0:T(8,128)(2,1)S(1)}, u32[]{:S(2)}, u32[]{:S(2)}) collective-permute-start(bf16[19,16,768]{2,1,0:T(8,128)(2,1)S(1)} %get-tuple-element.125), channel_id=1, source_target_pairs={{0,2},{2,4},{4,6},{6,22},{22,20},{20,18},{18,16},{16,0},{8,10},{10... | collective-permute-start | bytes 1400840 | tf_op jit(solution)/shard_map/ppermute | solution.py:611
  159.2 14.8 %collective-permute-start.26 = (bf16[1,19,16,768]{3,2,1,0:T(8,128)(2,1)S(1)}, bf16[1,19,16,768]{3,2,1,0:T(8,128)(2,1)S(1)}, u32[]{:S(2)}, u32[]{:S(2)}) collective-permute-start(bf16[1,19,16,768]{3,2,1,0:T(8,128)(2,1)S(1)} %fusion.21), channel_id=1, source_target_pairs={{0,8},{2,10},{4,12},{6,14},{22,30},{20,28},{18,26},{16,24},{8,0},{... | collective-permute-start | bytes 1400840 | tf_op jit(solution)/shard_map/ppermute | solution.py:613
  169.3 13.3 %collective-permute-start.40 = (bf16[19,16,768]{2,1,0:T(8,128)(2,1)S(1)}, bf16[19,16,768]{2,1,0:T(8,128)(2,1)S(1)}, u32[]{:S(2)}, u32[]{:S(2)}) collective-permute-start(bf16[19,16,768]{2,1,0:T(8,128)(2,1)S(1)} %get-tuple-element.122), channel_id=1, source_target_pairs={{0,2},{2,4},{4,6},{6,22},{22,20},{20,18},{18,16},{16,0},{8,10},{10... | collective-permute-start | bytes 1400840 | tf_op jit(solution)/shard_map/ppermute | solution.py:616
  173.9 10.7 %collective-permute-start.41 = (bf16[19,16,768]{2,1,0:T(8,128)(2,1)S(1)}, bf16[19,16,768]{2,1,0:T(8,128)(2,1)S(1)}, u32[]{:S(2)}, u32[]{:S(2)}) collective-permute-start(bf16[19,16,768]{2,1,0:T(8,128)(2,1)S(1)} %get-tuple-element.123), channel_id=1, source_target_pairs={{0,16},{2,0},{4,2},{6,4},{22,6},{20,22},{18,20},{16,18},{8,24},{10... | collective-permute-start | bytes 1400840 | tf_op jit(solution)/shard_map/ppermute | solution.py:617
  (52 other events, 467.0 us)
